TPU v7x, 128 devices: a whole 4x4x4 slice. The times are simulated.
128 devices in a mesh: dp: 8 (over x, core), strand: 2 (over z_hi), ctx: 8 (over z_lo, y).
Axes of the slice: x: 4, y: 4, z: 4 (z_hi: 2, z_lo: 2; z = z_hi * 2 + z_lo), core: 2. Of those that a mesh axis runs over, the one named last changes fastest.
Arguments:
- qkv: bfloat16 [8, 2, 1024, 3, 2048], P('dp', 'strand', 'ctx'), may hold values from -8 to 8
- out_weight: bfloat16 [2048, 4096], P('ctx'), may hold values from -4 to 4
- cotangent: bfloat16 [8, 2, 1024, 4096], P('dp', 'strand', 'ctx'), may hold values from -1.796875 to 1.796875
Outputs:
- mixed: bfloat16 [8, 2, 1024, 4096], P('dp', 'strand', 'ctx')
- qkv_grad: bfloat16 [8, 2, 1024, 3, 2048], P('dp', 'strand', 'ctx')
- weight_grad: float32 [2048, 4096], P('ctx', ('dp', 'strand'))
All inputs are finite; a program needn't handle non-finite values.
Results may differ from a plain program's by a relative error of at most 0.019.
Values may be sent and summed in bfloat16 or wider, within the bound.
No kernel may reach another device: no remote copies, remote signals or barrier semaphores. Data moves between devices by JAX's collectives and lax.ppermute only.
A program may use at most 192 MiB of HBM per device.

v0:
```python
import math

import jax
import jax.numpy as jnp
from jax import lax
from jax.sharding import PartitionSpec as P

DH = 128


def from_partner(block, axis, bit):
    count = lax.axis_size(axis)
    route = []
    for low in range(count):
        high = low | 1 << bit
        if high != low and high < count:
            route += [(low, high), (high, low)]
    return lax.ppermute(block, axis, route)


def body(qkv, out_weight, cotangent):
    tok_rows = qkv.shape[2]
    local_heads = out_weight.shape[0] // DH
    mirror_bits = (lax.axis_size("strand") * lax.axis_size("ctx")).bit_length() - 1
    scale = 1.0 / math.sqrt(DH)
    spread = lax.all_to_all(qkv, "ctx", split_axis=4, concat_axis=2, tiled=True)
    seq_len = spread.shape[2]
    queries = spread[0, 0, :, 0].reshape(seq_len, local_heads, DH)
    keys_all = spread[0, 0, :, 1].reshape(seq_len, local_heads, DH)
    values_all = spread[0, 0, :, 2].reshape(seq_len, local_heads, DH)
    scores = (
        jnp.einsum("qhd,khd->hqk", queries, keys_all, preferred_element_type=jnp.float32) * scale
    )
    peak = jnp.max(scores, axis=-1, keepdims=True)
    expo = jnp.exp(scores - peak)
    probs32 = expo / jnp.sum(expo, axis=-1, keepdims=True)
    probs = probs32.astype(jnp.bfloat16)
    attended = jnp.einsum("hqk,khd->qhd", probs, values_all, preferred_element_type=jnp.float32)
    attended = attended.astype(jnp.bfloat16).reshape(seq_len, local_heads * DH)
    summed = lax.psum_scatter(
        jnp.dot(attended, out_weight, preferred_element_type=jnp.float32).astype(jnp.bfloat16),
        "ctx",
        scatter_dimension=0,
        tiled=True,
    ).astype(jnp.float32)
    partner = summed
    for bit_number in range(mirror_bits):
        partner = from_partner(partner.astype(jnp.bfloat16), ("strand", "ctx"), bit_number).astype(
            partner.dtype
        )
    mixed_rows = summed + jnp.flip(partner, 0)
    mixed = mixed_rows.astype(jnp.bfloat16).reshape(1, 1, tok_rows, -1)
    own_grad = cotangent[0, 0]
    partner_grad = own_grad
    for bit_number in range(mirror_bits):
        partner_grad = from_partner(partner_grad, ("strand", "ctx"), bit_number)
    upstream_rows = (
        own_grad.astype(jnp.float32) + jnp.flip(partner_grad, 0).astype(jnp.float32)
    ).astype(jnp.bfloat16)
    piece = lax.all_gather(upstream_rows, "ctx", axis=0, tiled=True)
    grad_piece = lax.dot_general(
        piece, out_weight, (((1,), (1,)), ((), ())), preferred_element_type=jnp.float32
    )
    weight_total = lax.dot_general(
        attended, piece, (((0,), (0,)), ((), ())), preferred_element_type=jnp.float32
    )
    weight_grad = lax.psum_scatter(
        weight_total.astype(jnp.bfloat16), ("dp", "strand"), scatter_dimension=1, tiled=True
    ).astype(jnp.float32)
    grad_att = grad_piece.astype(jnp.bfloat16).reshape(seq_len, local_heads, DH)
    grad_probs = jnp.einsum(
        "qhd,khd->hqk", grad_att, values_all, preferred_element_type=jnp.float32
    )
    grad_values = jnp.einsum(
        "hqk,qhd->khd", probs, grad_att, preferred_element_type=jnp.float32
    ).astype(jnp.bfloat16)
    centre = jnp.sum(grad_probs * probs32, axis=-1, keepdims=True)
    grad_scores = (probs32 * (grad_probs - centre) * scale).astype(jnp.bfloat16)
    grad_queries = jnp.einsum(
        "hqk,khd->qhd", grad_scores, keys_all, preferred_element_type=jnp.float32
    ).astype(jnp.bfloat16)
    grad_keys = jnp.einsum(
        "hqk,qhd->khd", grad_scores, queries, preferred_element_type=jnp.float32
    ).astype(jnp.bfloat16)
    stacked_grads = jnp.stack([grad_queries, grad_keys, grad_values], axis=1).reshape(
        1, 1, seq_len, 3, local_heads * DH
    )
    qkv_grad = lax.all_to_all(stacked_grads, "ctx", split_axis=2, concat_axis=4, tiled=True)
    return (mixed, qkv_grad, weight_grad)


def solution(mesh):
    placed = (P("dp", "strand", "ctx", None, None), P("ctx", None), P("dp", "strand", "ctx", None))
    return jax.shard_map(
        body,
        mesh=mesh,
        in_specs=placed,
        out_specs=(
            P("dp", "strand", "ctx", None),
            P("dp", "strand", "ctx", None, None),
            P("ctx", ("dp", "strand")),
        ),
        check_vma=False,
    )
```

profile of v0, /device:TPU:8, one launch (start us, length us, event | category | flops | bytes accessed | tf_op | source)
XLA Modules:
  0.0 500.9 jit_solution(15770570235759808041)
XLA Ops:
  7.2 4.3 copy.26
  11.5 32.3 %all_to_all.36 = bf16[1,1,128,3,2048]{2,3,1,0,4:T(4,128)(2,1)S(1)} all-to-all(bf16[1,1,128,3,2048]{2,3,1,0,4:T(4,128)(2,1)} %copy.26), channel_id=1, replica_groups=mesh['dp'=8,'strand'=2,'ctx'=8] {'ctx'}, dimensions={4} | all-to-all | bytes 3145728 | tf_op jit(solution)/shard_map/all_to_all | solution.py:26
  43.8 2.4 copy.49
  46.3 3.7 all_to_all.29
  52.2 7.4 %fusion.40 = (f32[2,1024]{1,0:T(2,128)S(1)}, f32[2,1024,1024]{1,2,0:T(8,128)}) fusion(bf16[1024,2,128]{0,2,1:T(8,128)(2,1)S(1)} %bitcast.61, bf16[1024,2,128]{0,2,1:T(8,128)(2,1)} %bitcast.63), kind=kOutput, calls=%fused_computation.35 | convolution fusion | flops 543163392 | bytes 9445376 | tf_op jit(solution)/shard_map/sub | solution.py:35
  59.7 4.1 fusion.19
  64.6 5.6 %convolution_convert_fusion = bf16[1024,4096]{1,0:T(8,128)(2,1)} fusion(bf16[1024,256]{0,1:T(8,128)(2,1)S(1)} %bitcast.65, bf16[256,4096]{1,0:T(8,128)(2,1)S(1)} %copy-done), kind=kOutput, calls=%fused_computation.6 | convolution fusion | flops 2151677952 | bytes 11010048 | tf_op jit(solution)/shard_map/dot_general | solution.py:41
  71.3 40.8 %collective-permute-done.4 = bf16[128,4096]{1,0:T(8,128)(2,1)S(1)} collective-permute-done((bf16[128,4096]{1,0:T(8,128)(2,1)S(1)}, bf16[128,4096]{1,0:T(8,128)(2,1)S(1)}, u32[]{:S(2)}, u32[]{:S(2)}) %collective-permute-start.4) | collective-permute-done | bytes 1048608 | tf_op jit(solution)/shard_map/ppermute | solution.py:18
  112.2 46.9 %collective-permute-done.5 = bf16[128,4096]{1,0:T(8,128)(2,1)S(1)} collective-permute-done((bf16[128,4096]{1,0:T(8,128)(2,1)S(1)}, bf16[128,4096]{1,0:T(8,128)(2,1)S(1)}, u32[]{:S(2)}, u32[]{:S(2)}) %collective-permute-start.5) | collective-permute-done | bytes 1048608 | tf_op jit(solution)/shard_map/ppermute | solution.py:18
  159.1 21.4 %collective-permute-done.6 = bf16[128,4096]{1,0:T(8,128)(2,1)S(1)} collective-permute-done((bf16[128,4096]{1,0:T(8,128)(2,1)S(1)}, bf16[128,4096]{1,0:T(8,128)(2,1)S(1)}, u32[]{:S(2)}, u32[]{:S(2)}) %collective-permute-start.6) | collective-permute-done | bytes 1048608 | tf_op jit(solution)/shard_map/ppermute | solution.py:18
  180.5 6.7 %collective-permute-start.7 = (bf16[128,4096]{1,0:T(8,128)(2,1)S(1)}, bf16[128,4096]{1,0:T(8,128)(2,1)}, u32[]{:S(2)}, u32[]{:S(2)}) collective-permute-start(bf16[128,4096]{1,0:T(8,128)(2,1)S(1)} %collective-permute-done.6), channel_id=1, source_target_pairs={{0,8},{8,0},{1,9},{9,1},{2,10},{10,2},{3,11},{11,3},{4,12},{12,4},... | collective-permute-start | bytes 3145736 | tf_op jit(solution)/shard_map/ppermute | solution.py:18
  187.2 12.9 %collective-permute-done.7 = bf16[128,4096]{1,0:T(8,128)(2,1)} collective-permute-done((bf16[128,4096]{1,0:T(8,128)(2,1)S(1)}, bf16[128,4096]{1,0:T(8,128)(2,1)}, u32[]{:S(2)}, u32[]{:S(2)}) %collective-permute-start.7) | collective-permute-done | bytes 1048608 | tf_op jit(solution)/shard_map/ppermute | solution.py:18
  200.1 12.6 %rev.9 = bf16[128,4096]{1,0:T(8,128)(2,1)S(1)} reverse(bf16[128,4096]{1,0:T(8,128)(2,1)} %collective-permute-done.7), dimensions={0} | reverse | bytes 2097152 | tf_op jit(solution)/shard_map/jit(_flip)/rev | solution.py:58
  212.7 2.4 add_convert_fusion
  215.3 35.7 %collective-permute-start = (bf16[128,4096]{1,0:T(8,128)(2,1)}, bf16[128,4096]{1,0:T(8,128)(2,1)}, u32[]{:S(2)}, u32[]{:S(2)}) collective-permute-start(bf16[128,4096]{1,0:T(8,128)(2,1)} %reduce-scatter.3.cloned.1.call-done), channel_id=1, source_target_pairs={{0,1},{1,0},{2,3},{3,2},{4,5},{5,4},{6,7},{7,6},{8,9},{9,8},{10,11... | collective-permute-start | bytes 3145736 | tf_op jit(solution)/shard_map/ppermute | solution.py:18
  250.9 98.9 %all-gather.2.cloned.1.call-done = bf16[1024,4096]{1,0:T(8,128)(2,1)} async-done(((bf16[128,4096]{1,0:T(8,128)(2,1)}), bf16[1024,4096]{1,0:T(8,128)(2,1)}) %all-gather.2.cloned.1.call-update) | async-done | bytes 8388624 | tf_op jit(solution)/shard_map/all_gather | solution.py:60
  349.8 7.2 %convolution_convert_fusion.1 = bf16[256,4096]{1,0:T(8,128)(2,1)} fusion(bf16[1024,256]{0,1:T(8,128)(2,1)} %bitcast.66, bf16[1024,4096]{1,0:T(8,128)(2,1)} %all-gather.2.cloned.1.call-done), kind=kOutput, calls=%fused_computation.9 | convolution fusion | flops 2148532224 | bytes 11010048 | tf_op jit(solution)/shard_map/dot_general | solution.py:64
  357.0 5.7 %convolution_convert_fusion.2 = bf16[1024,256]{0,1:T(8,128)(2,1)S(1)} fusion(bf16[1024,4096]{1,0:T(8,128)(2,1)} %all-gather.2.cloned.1.call-done, bf16[256,4096]{1,0:T(8,128)(2,1)S(1)} %copy-done), kind=kOutput, calls=%fused_computation.24 | convolution fusion | flops 2147745792 | bytes 11010048 | tf_op jit(solution)/shard_map/dot_general | solution.py:61
  362.8 4.1 collective-permute-start.1
  366.9 5.1 %fusion.22 = bf16[2,128,1024]{2,1,0:T(8,128)(2,1)S(1)} fusion(bf16[1024,2,128]{0,2,1:T(8,128)(2,1)S(1)} %bitcast.56, f32[2,1024,1024]{1,2,0:T(8,128)} %get-tuple-element.7, f32[2,1024]{1,0:T(2,128)S(1)} %get-tuple-element.6), kind=kOutput, calls=%fused_computation.23 | convolution fusion | flops 541327360 | bytes 9445376 | tf_op jit(solution)/shard_map/hqk,qhd->khd/dot_general | solution.py:74
  372.9 5.6 %fusion.41 = f32[2,1024,1024]{1,2,0:T(8,128)} fusion(bf16[1024,2,128]{0,2,1:T(8,128)(2,1)} %bitcast.57, bf16[1024,2,128]{0,2,1:T(8,128)(2,1)S(1)} %bitcast.54), kind=kOutput, calls=%fused_computation.36 | convolution fusion | flops 536870912 | bytes 9437184 | tf_op jit(solution)/shard_map/qhd,khd->hqk/dot_general | solution.py:71
  378.5 12.1 %collective-permute-done.1 = bf16[128,4096]{1,0:T(8,128)(2,1)} collective-permute-done((bf16[128,4096]{1,0:T(8,128)(2,1)}, bf16[128,4096]{1,0:T(8,128)(2,1)}, u32[]{:S(2)}, u32[]{:S(2)}) %collective-permute-start.1) | collective-permute-done | bytes 1048608 | tf_op jit(solution)/shard_map/ppermute | solution.py:18
  392.5 13.5 %fusion.25 = bf16[2,1024,128]{1,2,0:T(8,128)(2,1)S(1)} fusion(bf16[1024,2,128]{0,2,1:T(8,128)(2,1)S(1)} %bitcast.64, f32[2,1024,1024]{1,2,0:T(8,128)} %fusion.41, f32[2,1024,1024]{1,2,0:T(8,128)} %get-tuple-element.7, f32[2,1024]{1,0:T(2,128)S(1)} %get-tuple-element.6), kind=kOutput, calls=%fused_computation.25 | convolution fusion | flops 551816192 | bytes 17833984 | tf_op jit(solution)/shard_map/hqk,khd->qhd/dot_general | solution.py:79
  408.0 12.6 %fusion.28 = bf16[2,1024,128]{1,2,0:T(8,128)(2,1)S(1)} fusion(bf16[1024,2,128]{0,2,1:T(8,128)(2,1)S(1)} %bitcast.62, f32[2,1024,1024]{1,2,0:T(8,128)} %fusion.41, f32[2,1024,1024]{1,2,0:T(8,128)} %get-tuple-element.7, f32[2,1024]{1,0:T(2,128)S(1)} %get-tuple-element.6), kind=kOutput, calls=%fused_computation.26 | convolution fusion | flops 551816192 | bytes 17833984 | tf_op jit(solution)/shard_map/hqk,qhd->khd/dot_general | solution.py:82
  422.5 6.0 %pad_maximum_fusion = bf16[1,1,1024,3,256]{4,3,1,0,2:T(4,128)(2,1)} fusion(bf16[1,1,1024,1,256]{4,3,1,0,2:T(2,128)(2,1)S(1)} %copy.38, bf16[1,1,1024,1,256]{4,3,1,0,2:T(2,128)(2,1)} %copy.37, bf16[1,1,1024,1,256]{4,3,1,0,2:T(2,128)(2,1)} %copy.36), kind=kLoop, calls=%fused_computation.14 | loop fusion | flops 4718592 | bytes 3145728 | tf_op jit(solution)/shard_map/stack | solution.py:85
  428.5 5.9 %all-to-all-start.1 = ((bf16[1,1,1024,3,256]{4,3,1,0,2:T(4,128)(2,1)}), bf16[1,1,1024,3,256]{4,3,1,0,2:T(4,128)(2,1)}, u32[]{:S(2)}, u32[]{:S(2)}) async-start(bf16[1,1,1024,3,256]{4,3,1,0,2:T(4,128)(2,1)} %pad_maximum_fusion), calls=%async_computation.2 | async-start | bytes 4194304 | tf_op jit(solution)/shard_map/all_to_all | solution.py:88
  436.0 24.2 %all-to-all-done.1 = bf16[1,1,1024,3,256]{4,3,1,0,2:T(4,128)(2,1)} async-done(((bf16[1,1,1024,3,256]{4,3,1,0,2:T(4,128)(2,1)}), bf16[1,1,1024,3,256]{4,3,1,0,2:T(4,128)(2,1)}, u32[]{:S(2)}, u32[]{:S(2)}) %all-to-all-start.1) | async-done | bytes 1572896 | tf_op jit(solution)/shard_map/all_to_all | solution.py:88
  460.3 3.9 copy.39
  464.2 3.7 all_to_all.33
  469.5 11.1 %collective-permute-done.3 = bf16[128,4096]{1,0:T(8,128)(2,1)S(1)} collective-permute-done((bf16[128,4096]{1,0:T(8,128)(2,1)}, bf16[128,4096]{1,0:T(8,128)(2,1)S(1)}, u32[]{:S(2)}, u32[]{:S(2)}) %collective-permute-start.3) | collective-permute-done | bytes 1048608 | tf_op jit(solution)/shard_map/ppermute | solution.py:18
  480.7 10.6 %rev.8 = f32[128,4096]{1,0:T(8,128)} reverse(bf16[128,4096]{1,0:T(8,128)(2,1)S(1)} %collective-permute-done.3), dimensions={0} | reverse | bytes 3145728 | tf_op jit(solution)/shard_map/jit(_flip)/rev | solution.py:51
  491.3 3.0 fusion.31
  (40 shorter events, 14.3 us)
Async XLA Ops:
  7.2 57.5 %copy-start = (bf16[256,4096]{1,0:T(8,128)(2,1)S(1)}, bf16[256,4096]{1,0:T(8,128)(2,1)}, u32[]{:S(2)}) copy-start(bf16[256,4096]{1,0:T(8,128)(2,1)} %param.4) | copy-start | bytes 6291460
  7.2 208.1 %reduce-scatter.3.cloned.1.call-start = ((), (), s32[]{:S(2)}) async-start(), calls=%async_computation.4 | async-start | bytes 9437184 | tf_op jit(solution)/shard_map/reduce_scatter | solution.py:40
  52.2 11.6 %copy-start.2 = (bf16[1,1,1024,1,256]{2,4,3,1,0:T(8,128)(2,1)}, bf16[1,1,1024,1,256]{2,4,3,1,0:T(8,128)(2,1)S(1)}, u32[]{:S(2)}) copy-start(bf16[1,1,1024,1,256]{2,4,3,1,0:T(8,128)(2,1)S(1)} %get-tuple-element.4) | copy-start | bytes 1572868
  52.2 11.6 %copy-start.6 = (bf16[1,1,1024,1,256]{2,4,3,1,0:T(8,128)(2,1)}, bf16[1,1,1024,1,256]{2,4,3,1,0:T(8,128)(2,1)S(1)}, u32[]{:S(2)}) copy-start(bf16[1,1,1024,1,256]{2,4,3,1,0:T(8,128)(2,1)S(1)} %get-tuple-element.5) | copy-start | bytes 1572868
  63.8 0.8 copy-start.9
  64.6 5.7 %copy-start.4 = (bf16[1,1,128,4096]{3,2,1,0:T(8,128)(2,1)S(1)}, bf16[1,1,128,4096]{3,2,1,0:T(8,128)(2,1)}, u32[]{:S(2)}) copy-start(bf16[1,1,128,4096]{3,2,1,0:T(8,128)(2,1)} %param.5) | copy-start | bytes 3145732
  70.3 279.5 %all-gather.2.cloned.1.call-start = ((), (), s32[]{:S(2)}) async-start(), calls=%async_computation.5 | async-start | bytes 9437184 | tf_op jit(solution)/shard_map/all_gather | solution.py:60
  70.4 41.8 %collective-permute-start.4 = (bf16[128,4096]{1,0:T(8,128)(2,1)S(1)}, bf16[128,4096]{1,0:T(8,128)(2,1)S(1)}, u32[]{:S(2)}, u32[]{:S(2)}) collective-permute-start(bf16[128,4096]{1,0:T(8,128)(2,1)S(1)} %bitcast.55), channel_id=1, source_target_pairs={{0,1},{1,0},{2,3},{3,2},{4,5},{5,4},{6,7},{7,6},{8,9},{9,8},{10,11... | collective-permute-start | bytes 3145736 | tf_op jit(solution)/shard_map/ppermute | solution.py:18
  112.2 46.9 %collective-permute-start.5 = (bf16[128,4096]{1,0:T(8,128)(2,1)S(1)}, bf16[128,4096]{1,0:T(8,128)(2,1)S(1)}, u32[]{:S(2)}, u32[]{:S(2)}) collective-permute-start(bf16[128,4096]{1,0:T(8,128)(2,1)S(1)} %collective-permute-done.4), channel_id=1, source_target_pairs={{0,2},{2,0},{1,3},{3,1},{4,6},{6,4},{5,7},{7,5},{8,10},{10,8},{9,1... | collective-permute-start | bytes 3145736 | tf_op jit(solution)/shard_map/ppermute | solution.py:18
  159.1 21.4 %collective-permute-start.6 = (bf16[128,4096]{1,0:T(8,128)(2,1)S(1)}, bf16[128,4096]{1,0:T(8,128)(2,1)S(1)}, u32[]{:S(2)}, u32[]{:S(2)}) collective-permute-start(bf16[128,4096]{1,0:T(8,128)(2,1)S(1)} %collective-permute-done.5), channel_id=1, source_target_pairs={{0,4},{4,0},{1,5},{5,1},{2,6},{6,2},{3,7},{7,3},{8,12},{12,8},{9,1... | collective-permute-start | bytes 3145736 | tf_op jit(solution)/shard_map/ppermute | solution.py:18
  180.5 19.6 %collective-permute-start.7 = (bf16[128,4096]{1,0:T(8,128)(2,1)S(1)}, bf16[128,4096]{1,0:T(8,128)(2,1)}, u32[]{:S(2)}, u32[]{:S(2)}) collective-permute-start(bf16[128,4096]{1,0:T(8,128)(2,1)S(1)} %collective-permute-done.6), channel_id=1, source_target_pairs={{0,8},{8,0},{1,9},{9,1},{2,10},{10,2},{3,11},{11,3},{4,12},{12,4},... | collective-permute-start | bytes 3145736 | tf_op jit(solution)/shard_map/ppermute | solution.py:18
  215.2 252.7 %reduce-scatter.5.cloned.1.call-start = ((), (), s32[]{:S(2)}) async-start(), calls=%async_computation.6 | async-start | bytes 2228224 | tf_op jit(solution)/shard_map/reduce_scatter | solution.py:67
  215.3 147.5 %collective-permute-start = (bf16[128,4096]{1,0:T(8,128)(2,1)}, bf16[128,4096]{1,0:T(8,128)(2,1)}, u32[]{:S(2)}, u32[]{:S(2)}) collective-permute-start(bf16[128,4096]{1,0:T(8,128)(2,1)} %reduce-scatter.3.cloned.1.call-done), channel_id=1, source_target_pairs={{0,1},{1,0},{2,3},{3,2},{4,5},{5,4},{6,7},{7,6},{8,9},{9,8},{10,11... | collective-permute-start | bytes 3145736 | tf_op jit(solution)/shard_map/ppermute | solution.py:18
  362.8 9.3 %copy-start.5 = (bf16[1024,256]{0,1:T(8,128)(2,1)}, bf16[1024,256]{0,1:T(8,128)(2,1)S(1)}, u32[]{:S(2)}) copy-start(bf16[1024,256]{0,1:T(8,128)(2,1)S(1)} %convolution_convert_fusion.2) | copy-start | bytes 1572868
  362.8 27.8 %collective-permute-start.1 = (bf16[128,4096]{1,0:T(8,128)(2,1)}, bf16[128,4096]{1,0:T(8,128)(2,1)}, u32[]{:S(2)}, u32[]{:S(2)}) collective-permute-start(bf16[128,4096]{1,0:T(8,128)(2,1)} %collective-permute-done), channel_id=1, source_target_pairs={{0,2},{2,0},{1,3},{3,1},{4,6},{6,4},{5,7},{7,5},{8,10},{10,8},{9,1... | collective-permute-start | bytes 3145736 | tf_op jit(solution)/shard_map/ppermute | solution.py:18
  366.9 6.0 %copy-start.3 = (bf16[1,1,1024,1,256]{2,4,3,1,0:T(8,128)(2,1)S(1)}, bf16[1,1,1024,1,256]{2,4,3,1,0:T(8,128)(2,1)}, u32[]{:S(2)}) copy-start(bf16[1,1,1024,1,256]{2,4,3,1,0:T(8,128)(2,1)} %copy-done.2) | copy-start | bytes 1572868
  372.0 20.4 %copy-start.8 = (bf16[1,1,1024,1,256]{2,4,3,1,0:T(8,128)(2,1)S(1)}, bf16[1,1,1024,1,256]{2,4,3,1,0:T(8,128)(2,1)}, u32[]{:S(2)}) copy-start(bf16[1,1,1024,1,256]{2,4,3,1,0:T(8,128)(2,1)} %get-tuple-element.3) | copy-start | bytes 1572868
  378.5 29.5 %copy-start.7 = (bf16[1,1,1024,1,256]{2,4,3,1,0:T(8,128)(2,1)S(1)}, bf16[1,1,1024,1,256]{2,4,3,1,0:T(8,128)(2,1)}, u32[]{:S(2)}) copy-start(bf16[1,1,1024,1,256]{2,4,3,1,0:T(8,128)(2,1)} %copy-done.6) | copy-start | bytes 1572868
  390.6 43.8 %collective-permute-start.2 = (bf16[128,4096]{1,0:T(8,128)(2,1)}, bf16[128,4096]{1,0:T(8,128)(2,1)}, u32[]{:S(2)}, u32[]{:S(2)}) collective-permute-start(bf16[128,4096]{1,0:T(8,128)(2,1)} %collective-permute-done.1), channel_id=1, source_target_pairs={{0,4},{4,0},{1,5},{5,1},{2,6},{6,2},{3,7},{7,3},{8,12},{12,8},{9,1... | collective-permute-start | bytes 3145736 | tf_op jit(solution)/shard_map/ppermute | solution.py:18
  422.5 71.8 %copy-start.1 = (bf16[256,4096]{1,0:T(8,128)(2,1)S(1)}, bf16[256,4096]{1,0:T(8,128)(2,1)}, u32[]{:S(2)}) copy-start(bf16[256,4096]{1,0:T(8,128)(2,1)} %param.4) | copy-start | bytes 6291460
  428.5 31.7 %all-to-all-start.1 = ((bf16[1,1,1024,3,256]{4,3,1,0,2:T(4,128)(2,1)}), bf16[1,1,1024,3,256]{4,3,1,0,2:T(4,128)(2,1)}, u32[]{:S(2)}, u32[]{:S(2)}) async-start(bf16[1,1,1024,3,256]{4,3,1,0,2:T(4,128)(2,1)} %pad_maximum_fusion), calls=%async_computation.2 | async-start | bytes 4194304 | tf_op jit(solution)/shard_map/all_to_all | solution.py:88
  434.4 46.3 %collective-permute-start.3 = (bf16[128,4096]{1,0:T(8,128)(2,1)}, bf16[128,4096]{1,0:T(8,128)(2,1)S(1)}, u32[]{:S(2)}, u32[]{:S(2)}) collective-permute-start(bf16[128,4096]{1,0:T(8,128)(2,1)} %collective-permute-done.2), channel_id=1, source_target_pairs={{0,8},{8,0},{1,9},{9,1},{2,10},{10,2},{3,11},{11,3},{4,12},{12,4},... | collective-permute-start | bytes 3145736 | tf_op jit(solution)/shard_map/ppermute | solution.py:18
Sparse Core Ops, SparseCore 0:
  70.4 126.1 reduce-scatter.2
  215.3 134.4 all-gather.1
  357.1 78.0 reduce-scatter.4
where the time goes:
time: 503 us; the launch traced here: 501 us
  waiting for transfers between devices  268 us (53%)
  matrix products  67 us (13%)
  starting transfers between devices  57 us (11%)
  local copies, waits for them, and re-layouts  49.3 us (10%)
  blocking collectives  32.3 us (6%)
  between operations  13.9 us (3%)
  other arithmetic  13.1 us (3%)
    ppermute x8, waiting for transfers between devices, from_partner(): return lax.ppermute(block, axis, route)  145 us
    all_gather x1, waiting for transfers between devices, body(): piece = lax.all_gather(upstream_rows, 'ctx', axis=0, tiled=True)  98.9 us
    ppermute x8, starting transfers between devices, from_partner(): return lax.ppermute(block, axis, route)  51 us
    all_to_all x1, blocking collectives, body(): spread = lax.all_to_all(qkv, 'ctx', split_axis=4, concat_axis=2, tiled=True)  32.3 us
    all_to_all x1, waiting for transfers between devices, body(): lax.all_to_all(stacked_grads, 'ctx', split_axis=2, concat_axis=4, tiled=T...  24.2 us
    dot_general x1, matrix products, body(): jnp.einsum('hqk,khd->qhd', grad_scores, keys_all, preferred_element_type=...  13.5 us
    rev x1, local copies, waits for them, and re-layouts, body(): jnp.flip(partner_grad, 0).astype(jnp.float32)  12.6 us
    dot_general x1, matrix products, body(): jnp.einsum('hqk,qhd->khd', grad_scores, queries, preferred_element_type=j...  12.6 us
  transfers between devices with their start and end apart: 12, of which 8 were waited for; matrix products, arithmetic and copies ran while one was open for 16% of the time, Pallas kernels for 0%

commit v1 on v0

v1 whole, which is shorter than its diff:
```python
import functools
import math

import jax
import jax.numpy as jnp
from jax import lax
from jax.experimental import pallas as pl
from jax.experimental.pallas import tpu as pltpu
from jax.sharding import PartitionSpec as P

DH = 128
N = 8
SEQ = 1024
ROWS = SEQ // N
HALF = ROWS // 2
GW = 256
D = 4096
F32 = jnp.float32
BF16 = jnp.bfloat16
VMEM_LIMIT = 56 * 1024 * 1024


def flip_matrix(n):
    a = lax.broadcasted_iota(jnp.int32, (n, n), 0)
    b = lax.broadcasted_iota(jnp.int32, (n, n), 1)
    return (a + b == n - 1).astype(BF16)


def dot(a, b, ca, cb):
    return lax.dot_general(a, b, (((ca,), (cb,)), ((), ())), preferred_element_type=F32)


def params(**kw):
    return pltpu.CompilerParams(vmem_limit_bytes=VMEM_LIMIT, **kw)


def cost(flops, nbytes, trans=0):
    return pl.CostEstimate(flops=int(flops), bytes_accessed=int(nbytes), transcendentals=int(trans))


def struct(*shape, dtype=BF16):
    return jax.ShapeDtypeStruct(shape, dtype)


def split_kernel(c_ref, x_ref, *outs):
    for k in range(N):
        g = jnp.bitwise_xor(c_ref[0], k)
        outs[k][...] = x_ref[:, :, pl.ds(pl.multiple_of(g * GW, GW), GW)]


def split(c, x):
    return pl.pallas_call(
        split_kernel,
        in_specs=[pl.BlockSpec(memory_space=pltpu.SMEM), pl.BlockSpec(memory_space=pltpu.VMEM)],
        out_specs=[pl.BlockSpec(memory_space=pltpu.VMEM)] * N,
        out_shape=[struct(3, ROWS, GW)] * N,
        compiler_params=params(),
        cost_estimate=cost(0, 2 * 3 * ROWS * 2048 * 2),
        name="split",
    )(c, x)


def assemble_kernel(c_ref, *refs):
    out = refs[N]
    for k in range(N):
        g = jnp.bitwise_xor(c_ref[0], k)
        out[:, :, pl.ds(pl.multiple_of(g * GW, GW), GW)] = refs[k][...]


def assemble(c, blocks):
    return pl.pallas_call(
        assemble_kernel,
        in_specs=[pl.BlockSpec(memory_space=pltpu.SMEM)] + [pl.BlockSpec(memory_space=pltpu.VMEM)] * N,
        out_specs=pl.BlockSpec(memory_space=pltpu.VMEM),
        out_shape=struct(3, ROWS, 2048),
        compiler_params=params(),
        cost_estimate=cost(0, 2 * 3 * ROWS * 2048 * 2),
        name="assemble",
    )(c, *blocks)


def fwd_kernel(*refs):
    blocks = refs[:N]
    cat, att_own, att_send, probs_t = refs[N:]
    q = pl.program_id(1)

    @pl.when(q == 0)
    def _():
        flip = flip_matrix(HALF)
        for j in range(N):
            cat[1, ROWS * j : ROWS * (j + 1), :] = blocks[j][1]
            cat[2, ROWS * j : ROWS * (j + 1), :] = blocks[j][2]
            cat[0, HALF * j : HALF * (j + 1), :] = blocks[j][0, :HALF, :]
            mirrored = dot(flip, blocks[N - 1 - j][0, HALF:, :], 1, 0).astype(BF16)
            cat[0, 512 + HALF * j : 512 + HALF * (j + 1), :] = mirrored

    queries = cat[0, pl.ds(pl.multiple_of(q * 256, 256), 256), :]
    scores = dot(cat[1], queries, 1, 1) * (1.0 / math.sqrt(DH))
    peak = jnp.max(scores, axis=0, keepdims=True)
    expo = jnp.exp(scores - peak)
    probs = (expo * (1.0 / jnp.sum(expo, axis=0, keepdims=True))).astype(BF16)
    probs_t[0] = probs
    att = jnp.transpose(dot(cat[2], probs, 0, 0)).astype(BF16)

    @pl.when(q < 2)
    def _():
        att_own[...] = att

    @pl.when(q >= 2)
    def _():
        att_send[...] = att


def low_half(h, q):
    return (jnp.minimum(q, 1), h)


def high_half(h, q):
    return (jnp.maximum(q - 2, 0), h)


def attention_fwd(blocks):
    return pl.pallas_call(
        fwd_kernel,
        grid=(2, 4),
        in_specs=[pl.BlockSpec((3, ROWS, DH), lambda h, q: (0, 0, h))] * N,
        out_specs=[
            pl.BlockSpec((3, SEQ, DH), lambda h, q: (0, 0, h)),
            pl.BlockSpec((256, DH), low_half),
            pl.BlockSpec((256, DH), high_half),
            pl.BlockSpec((1, SEQ, 256), lambda h, q: (h, 0, q)),
        ],
        out_shape=[struct(3, SEQ, GW), struct(512, GW), struct(512, GW), struct(2, SEQ, SEQ)],
        compiler_params=params(dimension_semantics=("arbitrary", "arbitrary")),
        cost_estimate=cost(4 * 4 * SEQ * SEQ * DH, 10 << 20, 2 * SEQ * SEQ),
        name="attention_fwd",
    )(*blocks)


def bwd_kernel(cat, probs_t, g_own, g_recv, *refs):
    outs = refs[:N]
    dq, dk, dv = refs[N:]
    q = pl.program_id(1)
    queries = cat[0, pl.ds(pl.multiple_of(q * 256, 256), 256), :]
    grad = jnp.where(q < 2, g_own[...], g_recv[...])
    probs_low = probs_t[0]
    grad_probs = dot(cat[2], grad, 1, 1)
    probs = probs_low.astype(F32)
    product = probs * grad_probs
    centre = jnp.sum(product, axis=0, keepdims=True)
    grad_scores = ((product - probs * centre) * (1.0 / math.sqrt(DH))).astype(BF16)
    part_v = dot(probs_low, grad, 1, 0)
    part_k = dot(grad_scores, queries, 1, 0)

    @pl.when(q == 0)
    def _():
        dv[...] = part_v
        dk[...] = part_k

    @pl.when(q > 0)
    def _():
        dv[...] += part_v
        dk[...] += part_k

    part_q = jnp.transpose(dot(cat[1], grad_scores, 0, 0)).astype(BF16)
    dq[pl.ds(pl.multiple_of(q * 256, 256), 256), :] = part_q

    @pl.when(q == 3)
    def _():
        flip = flip_matrix(HALF)
        for j in range(N):
            outs[j][0, :HALF, :] = dq[HALF * j : HALF * (j + 1), :]
            low = 512 + HALF * (N - 1 - j)
            outs[j][0, HALF:, :] = dot(flip, dq[low : low + HALF, :], 1, 0).astype(BF16)
            outs[j][1] = dk[ROWS * j : ROWS * (j + 1), :].astype(BF16)
            outs[j][2] = dv[ROWS * j : ROWS * (j + 1), :].astype(BF16)


def attention_bwd(cat, probs_t, g_own, g_recv):
    return pl.pallas_call(
        bwd_kernel,
        grid=(2, 4),
        in_specs=[
            pl.BlockSpec((3, SEQ, DH), lambda h, q: (0, 0, h)),
            pl.BlockSpec((1, SEQ, 256), lambda h, q: (h, 0, q)),
            pl.BlockSpec((256, DH), low_half),
            pl.BlockSpec((256, DH), high_half),
        ],
        out_specs=[pl.BlockSpec((3, ROWS, DH), lambda h, q: (0, 0, h))] * N,
        out_shape=[struct(3, ROWS, GW)] * N,
        scratch_shapes=[pltpu.VMEM((SEQ, DH), BF16), pltpu.VMEM((SEQ, DH), F32), pltpu.VMEM((SEQ, DH), F32)],
        compiler_params=params(dimension_semantics=("arbitrary", "arbitrary")),
        cost_estimate=cost(8 * 2 * SEQ * SEQ * DH, 8 << 20),
        name="attention_bwd",
    )(cat, probs_t, g_own, g_recv)


def grad_kernel(*refs):
    pieces = refs[:9]
    w, out, acc = refs[9:]
    k = pl.program_id(0)
    rows = jnp.concatenate([p[...] for p in pieces], axis=0)
    part = dot(rows, w[...], 1, 1)

    @pl.when(k == 0)
    def _():
        acc[...] = part

    @pl.when(k > 0)
    def _():
        acc[...] += part

    @pl.when(k == 3)
    def _():
        out[...] = acc[...].astype(BF16)


def grad_attended(pieces, w):
    return pl.pallas_call(
        grad_kernel,
        grid=(4,),
        in_specs=[pl.BlockSpec((p.shape[0], 1024), lambda k: (0, k)) for p in pieces]
        + [pl.BlockSpec((GW, 1024), lambda k: (0, k))],
        out_specs=pl.BlockSpec((512, GW), lambda k: (0, 0)),
        out_shape=struct(512, GW),
        scratch_shapes=[pltpu.VMEM((512, GW), F32)],
        compiler_params=params(),
        cost_estimate=cost(2 * 512 * GW * D, 7 << 20),
        name="grad_attended",
    )(*pieces, w)


def project_kernel(own, recv, w, *outs):
    both = (own[...].astype(F32) + recv[...].astype(F32)).astype(BF16)
    part = dot(both, w[...], 1, 0).astype(BF16)
    low = 0
    for out in outs:
        out[...] = part[low : low + out.shape[0], :]
        low += out.shape[0]


def project(own, recv, w):
    rows = (64, 64, 32, 32, 64, 64, 64, 64, 64)
    return pl.pallas_call(
        project_kernel,
        grid=(4,),
        in_specs=[
            pl.BlockSpec((512, GW), lambda k: (0, 0)),
            pl.BlockSpec((512, GW), lambda k: (0, 0)),
            pl.BlockSpec((GW, 1024), lambda k: (0, k)),
        ],
        out_specs=[pl.BlockSpec((r, 1024), lambda k: (0, k)) for r in rows],
        out_shape=[struct(r, D) for r in rows],
        compiler_params=params(),
        cost_estimate=cost(2 * 512 * GW * D, 7 << 20),
        name="project",
    )(own, recv, w)


def weight_kernel(d_ref, own, recv, *refs):
    pieces = refs[:9]
    out_own, out_other = refs[9:]
    both = (own[...].astype(F32) + recv[...].astype(F32)).astype(BF16)
    rows = jnp.concatenate([p[...] for p in pieces], axis=0)
    part = dot(both, rows, 0, 0).astype(BF16)
    first, second = part[:, :512], part[:, 512:]
    core = jnp.bitwise_and(d_ref[0], 1)
    out_own[0] = jnp.where(core == 0, first, second)
    out_other[0] = jnp.where(core == 0, second, first)


def weight_part(d, own, recv, pieces):
    def columns(x, d_ref):
        return (0, jnp.bitwise_xor(lax.shift_right_logical(d_ref[0], 1), x))

    return pl.pallas_call(
        weight_kernel,
        grid_spec=pltpu.PrefetchScalarGridSpec(
            num_scalar_prefetch=1,
            grid=(4,),
            in_specs=[pl.BlockSpec((512, GW), lambda x, d_ref: (0, 0))] * 2
            + [pl.BlockSpec((p.shape[0], 1024), columns) for p in pieces],
            out_specs=[pl.BlockSpec((1, GW, 512), lambda x, d_ref: (x, 0, 0))] * 2,
        ),
        out_shape=[struct(4, GW, 512)] * 2,
        compiler_params=params(),
        cost_estimate=cost(2 * 512 * GW * D, 7 << 20),
        name="weight_part",
    )(d, own, recv, *pieces)


def by_xor(x, axis, k):
    return lax.ppermute(x, axis, [(i, i ^ k) for i in range(N)])


def mirror(x):
    return lax.ppermute(x, ("strand", "ctx"), [(i, 2 * N - 1 - i) for i in range(2 * N)])


def other_strand(x):
    return lax.ppermute(x, "strand", [(0, 1), (1, 0)])


def flip_rows(x):
    return dot(flip_matrix(x.shape[0]), x, 1, 0)


def add(*terms):
    total = terms[0].astype(F32)
    for t in terms[1:]:
        total = total + t.astype(F32)
    return total


def gather_rows(u):
    y1, y3, z = (by_xor(u, "ctx", k) for k in (1, 3, 4))
    y2a = by_xor(y3[:32], "ctx", 1)
    y2b = by_xor(y1[32:], "ctx", 3)
    zy1 = by_xor(z, "ctx", 1)
    zy3 = by_xor(z, "ctx", 3)
    zy2 = by_xor(jnp.concatenate([y2a, y2b], axis=0), "ctx", 4)
    return [u, y1, y2a, y2b, y3, z, zy1, zy2, zy3]


def scatter_rows(parts):
    p0, p1, p2a, p2b, p3, p4, p5, p6, p7 = parts
    r5 = by_xor(p5, "ctx", 1)
    r7 = by_xor(p7, "ctx", 3)
    r6 = by_xor(p6, "ctx", 4)
    p2a = add(p2a, r6[:32]).astype(BF16)
    p2b = add(p2b, r6[32:]).astype(BF16)
    p4 = add(p4, r5, r7).astype(BF16)
    r2a = by_xor(p2a, "ctx", 1)
    r2b = by_xor(p2b, "ctx", 3)
    r4 = by_xor(p4, "ctx", 4)
    p3 = add(p3, jnp.pad(r2a, ((0, 32), (0, 0)))).astype(BF16)
    p1 = add(p1, jnp.pad(r2b, ((32, 0), (0, 0)))).astype(BF16)
    r3 = by_xor(p3, "ctx", 3)
    r1 = by_xor(p1, "ctx", 1)
    return add(p0, r1, r3, r4)


def body(qkv, out_weight, cotangent):
    c = lax.axis_index("ctx").astype(jnp.int32).reshape(1)
    d = lax.axis_index("dp").astype(jnp.int32).reshape(1)
    s = lax.axis_index("strand")
    mine = jnp.transpose(qkv[0, 0], (1, 0, 2))
    cot = cotangent[0, 0]

    cot_recv = mirror(cot[HALF:])
    sent = split(c, mine)
    blocks = [sent[0]] + [by_xor(sent[k], "ctx", k) for k in range(1, N)]

    upstream = (cot[:HALF].astype(F32) + flip_rows(cot_recv)).astype(BF16)
    pieces = gather_rows(upstream)

    cat, att_own, att_send, probs_t = attention_fwd(blocks)
    att_recv = other_strand(att_send)
    partial = project(att_own, att_recv, out_weight)

    g_own = grad_attended(pieces, out_weight)
    g_recv = other_strand(g_own)

    mixed_own = scatter_rows(partial).astype(BF16)
    mixed_recv = mirror(mixed_own)
    mixed = jnp.concatenate([mixed_own, flip_rows(mixed_recv).astype(BF16)], axis=0)

    grads = attention_bwd(cat, probs_t, g_own, g_recv)
    back = [grads[0]] + [by_xor(grads[k], "ctx", k) for k in range(1, N)]
    qkv_grad = jnp.transpose(assemble(c, back), (1, 0, 2))

    w_own, w_other = weight_part(d, att_own, att_recv, pieces)
    w_sum = add(w_own, by_xor(w_other, "dp", 1)).astype(BF16)
    w_chip = add(w_sum[0], *[by_xor(w_sum[x], "dp", 2 * x) for x in range(1, 4)])
    first, second = w_chip[:, :GW], w_chip[:, GW:]
    w_keep = jnp.where(s == 0, first, second)
    w_send = jnp.where(s == 0, second, first).astype(BF16)
    weight_grad = w_keep + other_strand(w_send).astype(F32)
    return (mixed[None, None], qkv_grad[None, None], weight_grad)


def solution(mesh):
    placed = (P("dp", "strand", "ctx", None, None), P("ctx", None), P("dp", "strand", "ctx", None))
    return jax.shard_map(
        body,
        mesh=mesh,
        in_specs=placed,
        out_specs=(
            P("dp", "strand", "ctx", None),
            P("dp", "strand", "ctx", None, None),
            P("ctx", ("dp", "strand")),
        ),
        check_vma=False,
    )
```

time: 503 us -> 191 us (0.38)
  waiting for transfers between devices: 268 us -> 59.7 us
  matrix products: 67 us -> 0.58 us
  Pallas kernels: 0 us -> 47 us
  local copies, waits for them, and re-layouts: 49.3 us -> 3.53 us
  blocking collectives: 32.3 us -> 0 us
  between operations: 13.9 us -> 0.99 us
  starting transfers between devices: 57 us -> 68.4 us
    all_gather x1 -> x0, waiting for transfers between devices: 98.9 us -> none  [body(): piece = lax.all_gather(upstream_rows, 'ctx', axis=0, tiled=True)]
    ppermute x8 -> x39, waiting for transfers between devices: 145 us -> 59.7 us  [the longest x34 41.5 us: by_xor(): return lax.ppermute(x, axis, [(i, i ^ k) for i in range(N)])]
    dot_general x8 -> x2, matrix products: 59.5 us -> 0.58 us  [dot(): lax.dot_general(a, b, (((ca,), (cb,)), ((), ())), preferred_element_type=...]
    pallas_call x0 -> x7, Pallas kernels: none -> 47 us  [the longest x1 13.8 us: attention_bwd(): pl.pallas_call(bwd_kernel, grid=(2, 4), in_specs=[pl.BlockSpec((3, SEQ, D...]
    all_to_all x1 -> x0, blocking collectives: 32.3 us -> none  [body(): spread = lax.all_to_all(qkv, 'ctx', split_axis=4, concat_axis=2, tiled=True)]
    all_to_all x1 -> x0, waiting for transfers between devices: 24.2 us -> none  [body(): lax.all_to_all(stacked_grads, 'ctx', split_axis=2, concat_axis=4, tiled=T...]
    rev x2 -> x0, local copies, waits for them, and re-layouts: 23.2 us -> none  [the longest x1 12.6 us: body(): jnp.flip(partner_grad, 0).astype(jnp.float32)]
    ppermute x8 -> x39, starting transfers between devices: 51 us -> 68.4 us  [the longest x34 53.9 us: by_xor(): return lax.ppermute(x, axis, [(i, i ^ k) for i in range(N)])]
  transfers between devices with their start and end apart: 12 -> 39, of which waited for: 8 -> 17; matrix products, arithmetic and copies ran while one was open for 16% -> 4% of each run, Pallas kernels for 0% -> 17%
where the time goes in v1:
time: 191 us; the launch traced here: 189 us
  starting transfers between devices  68.4 us (36%)
  waiting for transfers between devices  59.7 us (31%)
  Pallas kernels  47 us (25%)
  other arithmetic  8.53 us (4%)
  local copies, waits for them, and re-layouts  3.53 us (2%)
    ppermute x34, starting transfers between devices, by_xor(): return lax.ppermute(x, axis, [(i, i ^ k) for i in range(N)])  53.9 us
    ppermute x34, waiting for transfers between devices, by_xor(): return lax.ppermute(x, axis, [(i, i ^ k) for i in range(N)])  41.5 us
    ppermute x3, waiting for transfers between devices, other_strand(): return lax.ppermute(x, 'strand', [(0, 1), (1, 0)])  18.2 us
    pallas_call x1, Pallas kernels, attention_bwd(): pl.pallas_call(bwd_kernel, grid=(2, 4), in_specs=[pl.BlockSpec((3, SEQ, D...  13.8 us
    pallas_call x1, Pallas kernels, attention_fwd(): pl.pallas_call(fwd_kernel, grid=(2, 4), in_specs=[pl.BlockSpec((3, ROWS,...  11.9 us
    ppermute x3, starting transfers between devices, other_strand(): return lax.ppermute(x, 'strand', [(0, 1), (1, 0)])  8.21 us
    ppermute x2, starting transfers between devices, mirror(): lax.ppermute(x, ('strand', 'ctx'), [(i, 2 * N - 1 - i) for i in range(2 *...  6.25 us
    pallas_call x1, Pallas kernels, weight_part(): pl.pallas_call(weight_kernel, grid_spec=pltpu.PrefetchScalarGridSpec(num_...  5.57 us
  transfers between devices with their start and end apart: 39, of which 17 were waited for; matrix products, arithmetic and copies ran while one was open for 4% of the time, Pallas kernels for 17%

profile of v1, /device:TPU:8, one launch (start us, length us, event | category | flops | bytes accessed | tf_op | source)
XLA Modules:
  0.0 188.7 jit_solution(8218252291342371577)
XLA Ops:
  0.6 2.8 %split.1 = (bf16[3,128,256]{2,1,0:T(8,128)(2,1)}, bf16[3,128,256]{2,1,0:T(8,128)(2,1)}, bf16[3,128,256]{2,1,0:T(8,128)(2,1)}, bf16[3,128,256]{2,1,0:T(8,128)(2,1...) custom-call(s32[1]{0:T(128)} %bitcast.c_ref, ...), custom_call_target="tpu_custom_call" | custom-call | bytes 3145728 | tf_op jit(solution)/shard_map/split/pallas_call | solution.py:52
  3.8 2.7 %collective-permute-start.1 = (bf16[3,128,256]{2,1,0:T(8,128)(2,1)}, bf16[3,128,256]{2,1,0:T(8,128)(2,1)S(1)}, u32[]{:S(2)}, u32[]{:S(2)}) collective-permute-start(bf16[3,128,256]{2,1,0:T(8,128)(2,1)} %get-tuple-element.36), channel_id=1, source_target_pairs={{0,2},{1,3},{2,0},{3,1},{4,6},{5,7},{6,4},{7,5},{8,10},{9,11},{10,... | collective-permute-start | bytes 589832 | tf_op jit(solution)/shard_map/ppermute | solution.py:293
  11.4 3.6 %collective-permute-start.5 = (bf16[3,128,256]{2,1,0:T(8,128)(2,1)}, bf16[3,128,256]{2,1,0:T(8,128)(2,1)S(1)}, u32[]{:S(2)}, u32[]{:S(2)}) collective-permute-start(bf16[3,128,256]{2,1,0:T(8,128)(2,1)} %get-tuple-element.40), channel_id=1, source_target_pairs={{0,6},{1,7},{2,4},{3,5},{4,2},{5,3},{6,0},{7,1},{8,14},{9,15},{10,... | collective-permute-start | bytes 589832 | tf_op jit(solution)/shard_map/ppermute | solution.py:293
  18.5 3.9 %collective-permute-done.4.refs_5_ = bf16[3,128,256]{2,1,0:T(8,128)(2,1)S(1)} collective-permute-done((bf16[3,128,256]{2,1,0:T(8,128)(2,1)}, bf16[3,128,256]{2,1,0:T(8,128)(2,1)S(1)}, u32[]{:S(2)}, u32[]{:S(2)}) %collective-permute-start.4) | collective-permute-done | bytes 196640 | tf_op jit(solution)/shard_map/ppermute | solution.py:293
  22.4 6.1 %collective-permute-done.5.refs_6_ = bf16[3,128,256]{2,1,0:T(8,128)(2,1)S(1)} collective-permute-done((bf16[3,128,256]{2,1,0:T(8,128)(2,1)}, bf16[3,128,256]{2,1,0:T(8,128)(2,1)S(1)}, u32[]{:S(2)}, u32[]{:S(2)}) %collective-permute-start.5) | collective-permute-done | bytes 196640 | tf_op jit(solution)/shard_map/ppermute | solution.py:293
  29.2 11.9 %attention_fwd.1 = (bf16[3,1024,256]{2,1,0:T(8,128)(2,1)}, bf16[512,256]{1,0:T(8,128)(2,1)}, bf16[512,256]{1,0:T(8,128)(2,1)}, bf16[2,1024,1024]{2,1,0:T(8,128)(2,1)}) custom-call(bf16[3,128,256]{2,1,0:T(8,128)(2,1)} %get-tuple-element.34.refs_0_, bf16[3,128,256]{2,1,0:T(8,128)(2,1)} %copy-done.25, bf16[3,128,256]{2,1,0:T(8,128)(2,1)} %copy-done.26, ...), custom_call_target="tpu_custom_call" | custom-call | flops 2147483648 | bytes 10485760 | tf_op jit(solution)/shard_map/attention_fwd/pallas_call | solution.py:123
  41.1 3.7 %collective-permute-start.7 = (bf16[512,256]{1,0:T(8,128)(2,1)}, bf16[512,256]{1,0:T(8,128)(2,1)S(1)}, u32[]{:S(2)}, u32[]{:S(2)}) collective-permute-start(bf16[512,256]{1,0:T(8,128)(2,1)} %get-tuple-element.43), channel_id=1, source_target_pairs={{0,8},{8,0},{1,9},{9,1},{2,10},{10,2},{3,11},{11,3},{4,12},{12,4},... | collective-permute-start | bytes 786440 | tf_op jit(solution)/shard_map/ppermute | solution.py:301
  45.1 8.9 %collective-permute-done.7.recv = bf16[512,256]{1,0:T(8,128)(2,1)S(1)} collective-permute-done((bf16[512,256]{1,0:T(8,128)(2,1)}, bf16[512,256]{1,0:T(8,128)(2,1)S(1)}, u32[]{:S(2)}, u32[]{:S(2)}) %collective-permute-start.7) | collective-permute-done | bytes 262176 | tf_op jit(solution)/shard_map/ppermute | solution.py:301
  54.7 4.9 %project.1 = (bf16[64,4096]{1,0:T(8,128)(2,1)}, bf16[64,4096]{1,0:T(8,128)(2,1)}, bf16[32,4096]{1,0:T(8,128)(2,1)}, bf16[32,4096]{1,0:T(8,128)(2,1)}, bf16[64,40...) custom-call(bf16[512,256]{1,0:T(8,128)(2,1)} %get-tuple-element.42.o, ...), custom_call_target="tpu_custom_call" | custom-call | flops 1073741824 | bytes 7340032 | tf_op jit(solution)/shard_map/project/pallas_call | solution.py:244
  66.8 7.9 %collective-permute-done.8 = bf16[64,4096]{1,0:T(8,128)(2,1)S(1)} collective-permute-done((bf16[64,4096]{1,0:T(8,128)(2,1)}, bf16[64,4096]{1,0:T(8,128)(2,1)S(1)}, u32[]{:S(2)}, u32[]{:S(2)}) %collective-permute-start.8) | collective-permute-done | bytes 524320 | tf_op jit(solution)/shard_map/ppermute | solution.py:293
  74.7 2.1 %collective-permute-start.18 = (bf16[64,4096]{1,0:T(8,128)(2,1)S(1)}, bf16[64,4096]{1,0:T(8,128)(2,1)S(1)}, u32[]{:S(2)}, u32[]{:S(2)}) collective-permute-start(bf16[64,4096]{1,0:T(8,128)(2,1)S(1)} %fusion.refs_0_), channel_id=1, source_target_pairs={{0,1},{1,0},{2,3},{3,2},{4,5},{5,4},{6,7},{7,6},{8,9},{9,8},{10,11... | collective-permute-start | bytes 1572872 | tf_op jit(solution)/shard_map/ppermute | solution.py:293
  78.1 2.0 %collective-permute-start.9 = (bf16[32,4096]{1,0:T(8,128)(2,1)S(1)}, bf16[32,4096]{1,0:T(8,128)(2,1)S(1)}, u32[]{:S(2)}, u32[]{:S(2)}) collective-permute-start(bf16[32,4096]{1,0:T(8,128)(2,1)S(1)} %get-tuple-element.68), channel_id=1, source_target_pairs={{0,3},{1,2},{2,1},{3,0},{4,7},{5,6},{6,5},{7,4},{8,11},{9,10},{10,... | collective-permute-start | bytes 786440 | tf_op jit(solution)/shard_map/ppermute | solution.py:293
  81.7 4.0 %collective-permute-done.19.refs_4_ = bf16[64,4096]{1,0:T(8,128)(2,1)S(1)} collective-permute-done((bf16[64,4096]{1,0:T(8,128)(2,1)S(1)}, bf16[64,4096]{1,0:T(8,128)(2,1)S(1)}, u32[]{:S(2)}, u32[]{:S(2)}) %collective-permute-start.19) | collective-permute-done | bytes 524320 | tf_op jit(solution)/shard_map/ppermute | solution.py:293
  85.7 2.7 %collective-permute-start.15 = (bf16[64,4096]{1,0:T(8,128)(2,1)}, bf16[64,4096]{1,0:T(8,128)(2,1)}, u32[]{:S(2)}, u32[]{:S(2)}) collective-permute-start(bf16[64,4096]{1,0:T(8,128)(2,1)} %add_convert_fusion.2), channel_id=1, source_target_pairs={{0,4},{1,5},{2,6},{3,7},{4,0},{5,1},{6,2},{7,3},{8,12},{9,13},{10,... | collective-permute-start | bytes 1572872 | tf_op jit(solution)/shard_map/ppermute | solution.py:293
  88.5 2.8 %collective-permute-start.20 = (bf16[32,4096]{1,0:T(8,128)(2,1)S(1)}, bf16[32,4096]{1,0:T(8,128)(2,1)S(1)}, u32[]{:S(2)}, u32[]{:S(2)}) collective-permute-start(bf16[32,4096]{1,0:T(8,128)(2,1)S(1)} %slice.55), channel_id=1, source_target_pairs={{0,1},{1,0},{2,3},{3,2},{4,5},{5,4},{6,7},{7,6},{8,9},{9,8},{10,11... | collective-permute-start | bytes 786440 | tf_op jit(solution)/shard_map/ppermute | solution.py:293
  91.4 2.4 %collective-permute-start.21 = (bf16[32,4096]{1,0:T(8,128)(2,1)S(1)}, bf16[32,4096]{1,0:T(8,128)(2,1)S(1)}, u32[]{:S(2)}, u32[]{:S(2)}) collective-permute-start(bf16[32,4096]{1,0:T(8,128)(2,1)S(1)} %slice.56), channel_id=1, source_target_pairs={{0,3},{1,2},{2,1},{3,0},{4,7},{5,6},{6,5},{7,4},{8,11},{9,10},{10,... | collective-permute-start | bytes 786440 | tf_op jit(solution)/shard_map/ppermute | solution.py:293
  94.7 3.8 %collective-permute-done.20.refs_2_ = bf16[32,4096]{1,0:T(8,128)(2,1)S(1)} collective-permute-done((bf16[32,4096]{1,0:T(8,128)(2,1)S(1)}, bf16[32,4096]{1,0:T(8,128)(2,1)S(1)}, u32[]{:S(2)}, u32[]{:S(2)}) %collective-permute-start.20) | collective-permute-done | bytes 262176 | tf_op jit(solution)/shard_map/ppermute | solution.py:293
  98.5 2.1 %collective-permute-start.23 = (bf16[64,4096]{1,0:T(8,128)(2,1)S(1)}, bf16[64,4096]{1,0:T(8,128)(2,1)S(1)}, u32[]{:S(2)}, u32[]{:S(2)}) collective-permute-start(bf16[64,4096]{1,0:T(8,128)(2,1)S(1)} %collective-permute-done.22.refs_5_), channel_id=1, source_target_pairs={{0,1},{1,0},{2,3},{3,2},{4,5},{5,4},{6,7},{7,6},{8,9},{9,8},{10,11... | collective-permute-start | bytes 1572872 | tf_op jit(solution)/shard_map/ppermute | solution.py:293
  101.0 2.0 %collective-permute-start.12 = (bf16[64,4096]{1,0:T(8,128)(2,1)}, bf16[64,4096]{1,0:T(8,128)(2,1)}, u32[]{:S(2)}, u32[]{:S(2)}) collective-permute-start(bf16[64,4096]{1,0:T(8,128)(2,1)} %add_convert_fusion.3), channel_id=1, source_target_pairs={{0,3},{1,2},{2,1},{3,0},{4,7},{5,6},{6,5},{7,4},{8,11},{9,10},{10,... | collective-permute-start | bytes 1572872 | tf_op jit(solution)/shard_map/ppermute | solution.py:293
  104.9 5.6 %collective-permute-done.25.refs_8_ = bf16[64,4096]{1,0:T(8,128)(2,1)S(1)} collective-permute-done((bf16[64,4096]{1,0:T(8,128)(2,1)S(1)}, bf16[64,4096]{1,0:T(8,128)(2,1)S(1)}, u32[]{:S(2)}, u32[]{:S(2)}) %collective-permute-start.25) | collective-permute-done | bytes 524320 | tf_op jit(solution)/shard_map/ppermute | solution.py:293
  110.6 2.6 %collective-permute-start.10 = (bf16[64,4096]{1,0:T(8,128)(2,1)}, bf16[64,4096]{1,0:T(8,128)(2,1)S(1)}, u32[]{:S(2)}, u32[]{:S(2)}) collective-permute-start(bf16[64,4096]{1,0:T(8,128)(2,1)} %add_convert_fusion.4), channel_id=1, source_target_pairs={{0,1},{1,0},{2,3},{3,2},{4,5},{5,4},{6,7},{7,6},{8,9},{9,8},{10,11... | collective-permute-start | bytes 1572872 | tf_op jit(solution)/shard_map/ppermute | solution.py:293
  113.9 5.6 %weight_part.1 = (bf16[4,256,512]{2,1,0:T(8,128)(2,1)}, bf16[4,256,512]{2,1,0:T(8,128)(2,1)}) custom-call(s32[1]{0:T(128)} %bitcast.8.d_ref, bf16[512,256]{1,0:T(8,128)(2,1)} %get-tuple-element.42.own, bf16[512,256]{1,0:T(8,128)(2,1)} %copy-done.14, bf16[64,4096]{1,0:T(8,128)(2,1)} %copy-done, bf16[64,4096]{1,0:T(8,128)(2,1)} %copy-done.2, ...), custom_call_target="tpu_custom_call" | custom-call | flops 1073741824 | bytes 7340032 | tf_op jit(solution)/shard_map/weight_part/pallas_call | solution.py:276
  122.0 6.0 %collective-permute-start.16 = (bf16[64,4096]{1,0:T(8,128)(2,1)S(1)}, bf16[64,4096]{1,0:T(8,128)(2,1)S(1)}, u32[]{:S(2)}, u32[]{:S(2)}) collective-permute-start(bf16[64,4096]{1,0:T(8,128)(2,1)S(1)} %add_convert_fusion.1), channel_id=1, source_target_pairs={{0,15},{1,14},{2,13},{3,12},{4,11},{5,10},{6,9},{7,8},{8,7},{9,6},... | collective-permute-start | bytes 1572872 | tf_op jit(solution)/shard_map/ppermute | solution.py:297
  128.0 5.3 %grad_attended.1.g_own = bf16[512,256]{1,0:T(8,128)(2,1)} custom-call(bf16[64,4096]{1,0:T(8,128)(2,1)} %copy-done, bf16[64,4096]{1,0:T(8,128)(2,1)} %copy-done.2, bf16[32,4096]{1,0:T(8,128)(2,1)} %copy-done.3, bf16[32,4096]{1,0:T(8,128)(2,1)} %copy-done.4, bf16[64,4096]{1,0:T(8,128)(2,1)} %copy-done.1, bf16[64,4096]{1,0:T(8,128)(2,1)} %copy-done.5, ...), custom_call_target="tpu_custom_call" | custom-call | flops 1073741824 | bytes 7340032 | tf_op jit(solution)/shard_map/grad_attended/pallas_call | solution.py:219
  135.3 2.1 %collective-permute-start.37 = (bf16[256,512]{1,0:T(8,128)(2,1)S(1)}, bf16[256,512]{1,0:T(8,128)(2,1)S(1)}, u32[]{:S(2)}, u32[]{:S(2)}) collective-permute-start(bf16[256,512]{1,0:T(8,128)(2,1)S(1)} %get-tuple-element.66), channel_id=1, source_target_pairs={{0,96},{16,112},{32,64},{48,80},{64,32},{80,48},{96,0},{112,16},{1... | collective-permute-start | bytes 786440 | tf_op jit(solution)/shard_map/ppermute | solution.py:293
  138.0 7.3 %collective-permute-done.26.g_recv = bf16[512,256]{1,0:T(8,128)(2,1)S(1)} collective-permute-done((bf16[512,256]{1,0:T(8,128)(2,1)}, bf16[512,256]{1,0:T(8,128)(2,1)S(1)}, u32[]{:S(2)}, u32[]{:S(2)}) %collective-permute-start.26) | collective-permute-done | bytes 262176 | tf_op jit(solution)/shard_map/ppermute | solution.py:301
  146.0 13.8 %attention_bwd.1 = (bf16[3,128,256]{2,1,0:T(8,128)(2,1)}, bf16[3,128,256]{2,1,0:T(8,128)(2,1)}, bf16[3,128,256]{2,1,0:T(8,128)(2,1)}, bf16[3,128,256]{2,1,0:T(8,...) custom-call(bf16[3,1024,256]{2,1,0:T(8,128)(2,1)} %get-tuple-element, ...), custom_call_target="tpu_custom_call" | custom-call | flops 2147483648 | bytes 8388608 | tf_op jit(solution)/shard_map/attention_bwd/pallas_call | solution.py:180
  164.1 4.2 %collective-permute-start.31 = (bf16[3,128,256]{2,1,0:T(8,128)(2,1)}, bf16[3,128,256]{2,1,0:T(8,128)(2,1)S(1)}, u32[]{:S(2)}, u32[]{:S(2)}) collective-permute-start(bf16[3,128,256]{2,1,0:T(8,128)(2,1)} %get-tuple-element.60), channel_id=1, source_target_pairs={{0,5},{1,4},{2,7},{3,6},{4,1},{5,0},{6,3},{7,2},{8,13},{9,12},{10,... | collective-permute-start | bytes 589832 | tf_op jit(solution)/shard_map/ppermute | solution.py:293
  168.5 2.1 %collective-permute-start.32 = (bf16[3,128,256]{2,1,0:T(8,128)(2,1)S(1)}, bf16[3,128,256]{2,1,0:T(8,128)(2,1)S(1)}, u32[]{:S(2)}, u32[]{:S(2)}) collective-permute-start(bf16[3,128,256]{2,1,0:T(8,128)(2,1)S(1)} %copy-done.24), channel_id=1, source_target_pairs={{0,6},{1,7},{2,4},{3,5},{4,2},{5,3},{6,0},{7,1},{8,14},{9,15},{10,... | collective-permute-start | bytes 589832 | tf_op jit(solution)/shard_map/ppermute | solution.py:293
  173.0 4.5 %collective-permute-start.38 = (bf16[256,256]{1,0:T(8,128)(2,1)S(1)}, bf16[256,256]{1,0:T(8,128)(2,1)S(1)}, u32[]{:S(2)}, u32[]{:S(2)}) collective-permute-start(bf16[256,256]{1,0:T(8,128)(2,1)S(1)} %select_convert_fusion), channel_id=1, source_target_pairs={{0,8},{8,0},{1,9},{9,1},{2,10},{10,2},{3,11},{11,3},{4,12},{12,4},... | collective-permute-start | bytes 393224 | tf_op jit(solution)/shard_map/ppermute | solution.py:301
  178.7 3.5 %collective-permute-done.32.refs_6_ = bf16[3,128,256]{2,1,0:T(8,128)(2,1)S(1)} collective-permute-done((bf16[3,128,256]{2,1,0:T(8,128)(2,1)S(1)}, bf16[3,128,256]{2,1,0:T(8,128)(2,1)S(1)}, u32[]{:S(2)}, u32[]{:S(2)}) %collective-permute-start.32) | collective-permute-done | bytes 196640 | tf_op jit(solution)/shard_map/ppermute | solution.py:293
  183.1 2.8 %assemble.1 = bf16[3,128,2048]{2,1,0:T(8,128)(2,1)} custom-call(s32[1]{0:T(128)} %bitcast.c_ref, bf16[3,128,256]{2,1,0:T(8,128)(2,1)} %get-tuple-element.55.refs_0_, bf16[3,128,256]{2,1,0:T(8,128)(2,1)} %copy-done.15, bf16[3,128,256]{2,1,0:T(8,128)(2,1)} %copy-done.16, bf16[3,128,256]{2,1,0:T(8,128)(2,1)} %copy-done.17, bf16[3,128,256]{2,1,0:T(8,128)(2,1)} %copy-done.18, ...), custom_call_target="tpu_custom_call" | custom-call | bytes 3145728 | tf_op jit(solution)/shard_map/assemble/pallas_call | solution.py:71
  (134 shorter events, 41.9 us)
Async XLA Ops:
  3.8 12.9 %collective-permute-start.1 = (bf16[3,128,256]{2,1,0:T(8,128)(2,1)}, bf16[3,128,256]{2,1,0:T(8,128)(2,1)S(1)}, u32[]{:S(2)}, u32[]{:S(2)}) collective-permute-start(bf16[3,128,256]{2,1,0:T(8,128)(2,1)} %get-tuple-element.36), channel_id=1, source_target_pairs={{0,2},{1,3},{2,0},{3,1},{4,6},{5,7},{6,4},{7,5},{8,10},{9,11},{10,... | collective-permute-start | bytes 589832 | tf_op jit(solution)/shard_map/ppermute | solution.py:293
  6.4 12.0 %collective-permute-start.2 = (bf16[3,128,256]{2,1,0:T(8,128)(2,1)}, bf16[3,128,256]{2,1,0:T(8,128)(2,1)S(1)}, u32[]{:S(2)}, u32[]{:S(2)}) collective-permute-start(bf16[3,128,256]{2,1,0:T(8,128)(2,1)} %get-tuple-element.37), channel_id=1, source_target_pairs={{0,3},{1,2},{2,1},{3,0},{4,7},{5,6},{6,5},{7,4},{8,11},{9,10},{10,... | collective-permute-start | bytes 589832 | tf_op jit(solution)/shard_map/ppermute | solution.py:293
  6.9 11.6 %collective-permute-start.3 = (bf16[3,128,256]{2,1,0:T(8,128)(2,1)}, bf16[3,128,256]{2,1,0:T(8,128)(2,1)S(1)}, u32[]{:S(2)}, u32[]{:S(2)}) collective-permute-start(bf16[3,128,256]{2,1,0:T(8,128)(2,1)} %get-tuple-element.38), channel_id=1, source_target_pairs={{0,4},{1,5},{2,6},{3,7},{4,0},{5,1},{6,2},{7,3},{8,12},{9,13},{10,... | collective-permute-start | bytes 589832 | tf_op jit(solution)/shard_map/ppermute | solution.py:293
  8.8 13.6 %collective-permute-start.4 = (bf16[3,128,256]{2,1,0:T(8,128)(2,1)}, bf16[3,128,256]{2,1,0:T(8,128)(2,1)S(1)}, u32[]{:S(2)}, u32[]{:S(2)}) collective-permute-start(bf16[3,128,256]{2,1,0:T(8,128)(2,1)} %get-tuple-element.39), channel_id=1, source_target_pairs={{0,5},{1,4},{2,7},{3,6},{4,1},{5,0},{6,3},{7,2},{8,13},{9,12},{10,... | collective-permute-start | bytes 589832 | tf_op jit(solution)/shard_map/ppermute | solution.py:293
  11.4 17.1 %collective-permute-start.5 = (bf16[3,128,256]{2,1,0:T(8,128)(2,1)}, bf16[3,128,256]{2,1,0:T(8,128)(2,1)S(1)}, u32[]{:S(2)}, u32[]{:S(2)}) collective-permute-start(bf16[3,128,256]{2,1,0:T(8,128)(2,1)} %get-tuple-element.40), channel_id=1, source_target_pairs={{0,6},{1,7},{2,4},{3,5},{4,2},{5,3},{6,0},{7,1},{8,14},{9,15},{10,... | collective-permute-start | bytes 589832 | tf_op jit(solution)/shard_map/ppermute | solution.py:293
  16.7 11.8 %collective-permute-start.6 = (bf16[3,128,256]{2,1,0:T(8,128)(2,1)}, bf16[3,128,256]{2,1,0:T(8,128)(2,1)S(1)}, u32[]{:S(2)}, u32[]{:S(2)}) collective-permute-start(bf16[3,128,256]{2,1,0:T(8,128)(2,1)} %get-tuple-element.41), channel_id=1, source_target_pairs={{0,7},{1,6},{2,5},{3,4},{4,3},{5,2},{6,1},{7,0},{8,15},{9,14},{10,... | collective-permute-start | bytes 589832 | tf_op jit(solution)/shard_map/ppermute | solution.py:293
  41.1 12.8 %collective-permute-start.7 = (bf16[512,256]{1,0:T(8,128)(2,1)}, bf16[512,256]{1,0:T(8,128)(2,1)S(1)}, u32[]{:S(2)}, u32[]{:S(2)}) collective-permute-start(bf16[512,256]{1,0:T(8,128)(2,1)} %get-tuple-element.43), channel_id=1, source_target_pairs={{0,8},{8,0},{1,9},{9,1},{2,10},{10,2},{3,11},{11,3},{4,12},{12,4},... | collective-permute-start | bytes 786440 | tf_op jit(solution)/shard_map/ppermute | solution.py:301
  44.8 19.2 %collective-permute-start.17 = (bf16[64,4096]{1,0:T(8,128)(2,1)S(1)}, bf16[64,4096]{1,0:T(8,128)(2,1)S(1)}, u32[]{:S(2)}, u32[]{:S(2)}) collective-permute-start(bf16[64,4096]{1,0:T(8,128)(2,1)S(1)} %slice_bitcast_fusion), channel_id=1, source_target_pairs={{0,15},{1,14},{2,13},{3,12},{4,11},{5,10},{6,9},{7,8},{8,7},{9,6},... | collective-permute-start | bytes 1572872 | tf_op jit(solution)/shard_map/ppermute | solution.py:297
  59.6 15.2 %collective-permute-start.8 = (bf16[64,4096]{1,0:T(8,128)(2,1)}, bf16[64,4096]{1,0:T(8,128)(2,1)S(1)}, u32[]{:S(2)}, u32[]{:S(2)}) collective-permute-start(bf16[64,4096]{1,0:T(8,128)(2,1)} %get-tuple-element.47), channel_id=1, source_target_pairs={{0,4},{1,5},{2,6},{3,7},{4,0},{5,1},{6,2},{7,3},{8,12},{9,13},{10,... | collective-permute-start | bytes 1572872 | tf_op jit(solution)/shard_map/ppermute | solution.py:293
  60.4 17.6 %collective-permute-start.13 = (bf16[64,4096]{1,0:T(8,128)(2,1)}, bf16[64,4096]{1,0:T(8,128)(2,1)S(1)}, u32[]{:S(2)}, u32[]{:S(2)}) collective-permute-start(bf16[64,4096]{1,0:T(8,128)(2,1)} %get-tuple-element.51), channel_id=1, source_target_pairs={{0,1},{1,0},{2,3},{3,2},{4,5},{5,4},{6,7},{7,6},{8,9},{9,8},{10,11... | collective-permute-start | bytes 1572872 | tf_op jit(solution)/shard_map/ppermute | solution.py:293
  62.4 17.6 %collective-permute-start.14 = (bf16[64,4096]{1,0:T(8,128)(2,1)}, bf16[64,4096]{1,0:T(8,128)(2,1)S(1)}, u32[]{:S(2)}, u32[]{:S(2)}) collective-permute-start(bf16[64,4096]{1,0:T(8,128)(2,1)} %get-tuple-element.52), channel_id=1, source_target_pairs={{0,3},{1,2},{2,1},{3,0},{4,7},{5,6},{6,5},{7,4},{8,11},{9,10},{10,... | collective-permute-start | bytes 1572872 | tf_op jit(solution)/shard_map/ppermute | solution.py:293
  64.3 27.0 %collective-permute-start.22 = (bf16[64,4096]{1,0:T(8,128)(2,1)S(1)}, bf16[64,4096]{1,0:T(8,128)(2,1)S(1)}, u32[]{:S(2)}, u32[]{:S(2)}) collective-permute-start(bf16[64,4096]{1,0:T(8,128)(2,1)S(1)} %fusion.refs_0_), channel_id=1, source_target_pairs={{0,4},{1,5},{2,6},{3,7},{4,0},{5,1},{6,2},{7,3},{8,12},{9,13},{10,... | collective-permute-start | bytes 1572872 | tf_op jit(solution)/shard_map/ppermute | solution.py:293
  66.3 19.4 %collective-permute-start.19 = (bf16[64,4096]{1,0:T(8,128)(2,1)S(1)}, bf16[64,4096]{1,0:T(8,128)(2,1)S(1)}, u32[]{:S(2)}, u32[]{:S(2)}) collective-permute-start(bf16[64,4096]{1,0:T(8,128)(2,1)S(1)} %fusion.refs_0_), channel_id=1, source_target_pairs={{0,3},{1,2},{2,1},{3,0},{4,7},{5,6},{6,5},{7,4},{8,11},{9,10},{10,... | collective-permute-start | bytes 1572872 | tf_op jit(solution)/shard_map/ppermute | solution.py:293
  74.7 13.8 %collective-permute-start.18 = (bf16[64,4096]{1,0:T(8,128)(2,1)S(1)}, bf16[64,4096]{1,0:T(8,128)(2,1)S(1)}, u32[]{:S(2)}, u32[]{:S(2)}) collective-permute-start(bf16[64,4096]{1,0:T(8,128)(2,1)S(1)} %fusion.refs_0_), channel_id=1, source_target_pairs={{0,1},{1,0},{2,3},{3,2},{4,5},{5,4},{6,7},{7,6},{8,9},{9,8},{10,11... | collective-permute-start | bytes 1572872 | tf_op jit(solution)/shard_map/ppermute | solution.py:293
  78.1 25.8 %collective-permute-start.9 = (bf16[32,4096]{1,0:T(8,128)(2,1)S(1)}, bf16[32,4096]{1,0:T(8,128)(2,1)S(1)}, u32[]{:S(2)}, u32[]{:S(2)}) collective-permute-start(bf16[32,4096]{1,0:T(8,128)(2,1)S(1)} %get-tuple-element.68), channel_id=1, source_target_pairs={{0,3},{1,2},{2,1},{3,0},{4,7},{5,6},{6,5},{7,4},{8,11},{9,10},{10,... | collective-permute-start | bytes 786440 | tf_op jit(solution)/shard_map/ppermute | solution.py:293
  80.1 13.7 %collective-permute-start.11 = (bf16[32,4096]{1,0:T(8,128)(2,1)S(1)}, bf16[32,4096]{1,0:T(8,128)(2,1)S(1)}, u32[]{:S(2)}, u32[]{:S(2)}) collective-permute-start(bf16[32,4096]{1,0:T(8,128)(2,1)S(1)} %get-tuple-element.69), channel_id=1, source_target_pairs={{0,1},{1,0},{2,3},{3,2},{4,5},{5,4},{6,7},{7,6},{8,9},{9,8},{10,11... | collective-permute-start | bytes 786440 | tf_op jit(solution)/shard_map/ppermute | solution.py:293
  85.7 33.9 %collective-permute-start.15 = (bf16[64,4096]{1,0:T(8,128)(2,1)}, bf16[64,4096]{1,0:T(8,128)(2,1)}, u32[]{:S(2)}, u32[]{:S(2)}) collective-permute-start(bf16[64,4096]{1,0:T(8,128)(2,1)} %add_convert_fusion.2), channel_id=1, source_target_pairs={{0,4},{1,5},{2,6},{3,7},{4,0},{5,1},{6,2},{7,3},{8,12},{9,13},{10,... | collective-permute-start | bytes 1572872 | tf_op jit(solution)/shard_map/ppermute | solution.py:293
  93.7 16.8 %collective-permute-start.25 = (bf16[64,4096]{1,0:T(8,128)(2,1)S(1)}, bf16[64,4096]{1,0:T(8,128)(2,1)S(1)}, u32[]{:S(2)}, u32[]{:S(2)}) collective-permute-start(bf16[64,4096]{1,0:T(8,128)(2,1)S(1)} %collective-permute-done.22.refs_5_), channel_id=1, source_target_pairs={{0,3},{1,2},{2,1},{3,0},{4,7},{5,6},{6,5},{7,4},{8,11},{9,10},{10,... | collective-permute-start | bytes 1572872 | tf_op jit(solution)/shard_map/ppermute | solution.py:293
  98.5 14.6 %collective-permute-start.23 = (bf16[64,4096]{1,0:T(8,128)(2,1)S(1)}, bf16[64,4096]{1,0:T(8,128)(2,1)S(1)}, u32[]{:S(2)}, u32[]{:S(2)}) collective-permute-start(bf16[64,4096]{1,0:T(8,128)(2,1)S(1)} %collective-permute-done.22.refs_5_), channel_id=1, source_target_pairs={{0,1},{1,0},{2,3},{3,2},{4,5},{5,4},{6,7},{7,6},{8,9},{9,8},{10,11... | collective-permute-start | bytes 1572872 | tf_op jit(solution)/shard_map/ppermute | solution.py:293
  101.0 18.7 %collective-permute-start.12 = (bf16[64,4096]{1,0:T(8,128)(2,1)}, bf16[64,4096]{1,0:T(8,128)(2,1)}, u32[]{:S(2)}, u32[]{:S(2)}) collective-permute-start(bf16[64,4096]{1,0:T(8,128)(2,1)} %add_convert_fusion.3), channel_id=1, source_target_pairs={{0,3},{1,2},{2,1},{3,0},{4,7},{5,6},{6,5},{7,4},{8,11},{9,10},{10,... | collective-permute-start | bytes 1572872 | tf_op jit(solution)/shard_map/ppermute | solution.py:293
  119.5 13.8 %collective-permute-start.34 = (bf16[4,256,512]{2,1,0:T(8,128)(2,1)}, bf16[4,256,512]{2,1,0:T(8,128)(2,1)S(1)}, u32[]{:S(2)}, u32[]{:S(2)}) collective-permute-start(bf16[4,256,512]{2,1,0:T(8,128)(2,1)} %get-tuple-element.64), channel_id=1, source_target_pairs={{0,16},{16,0},{32,48},{48,32},{64,80},{80,64},{96,112},{112,96},{1... | collective-permute-start | bytes 3145736 | tf_op jit(solution)/shard_map/ppermute | solution.py:293
  122.0 39.8 %collective-permute-start.16 = (bf16[64,4096]{1,0:T(8,128)(2,1)S(1)}, bf16[64,4096]{1,0:T(8,128)(2,1)S(1)}, u32[]{:S(2)}, u32[]{:S(2)}) collective-permute-start(bf16[64,4096]{1,0:T(8,128)(2,1)S(1)} %add_convert_fusion.1), channel_id=1, source_target_pairs={{0,15},{1,14},{2,13},{3,12},{4,11},{5,10},{6,9},{7,8},{8,7},{9,6},... | collective-permute-start | bytes 1572872 | tf_op jit(solution)/shard_map/ppermute | solution.py:297
  133.3 12.0 %collective-permute-start.26 = (bf16[512,256]{1,0:T(8,128)(2,1)}, bf16[512,256]{1,0:T(8,128)(2,1)S(1)}, u32[]{:S(2)}, u32[]{:S(2)}) collective-permute-start(bf16[512,256]{1,0:T(8,128)(2,1)} %grad_attended.1.g_own), channel_id=1, source_target_pairs={{0,8},{8,0},{1,9},{9,1},{2,10},{10,2},{3,11},{11,3},{4,12},{12,4},... | collective-permute-start | bytes 786440 | tf_op jit(solution)/shard_map/ppermute | solution.py:301
  133.7 29.0 %collective-permute-start.35 = (bf16[256,512]{1,0:T(8,128)(2,1)S(1)}, bf16[256,512]{1,0:T(8,128)(2,1)S(1)}, u32[]{:S(2)}, u32[]{:S(2)}) collective-permute-start(bf16[256,512]{1,0:T(8,128)(2,1)S(1)} %get-tuple-element.65), channel_id=1, source_target_pairs={{0,32},{16,48},{32,0},{48,16},{64,96},{80,112},{96,64},{112,80},{1... | collective-permute-start | bytes 786440 | tf_op jit(solution)/shard_map/ppermute | solution.py:293
  135.3 28.5 %collective-permute-start.37 = (bf16[256,512]{1,0:T(8,128)(2,1)S(1)}, bf16[256,512]{1,0:T(8,128)(2,1)S(1)}, u32[]{:S(2)}, u32[]{:S(2)}) collective-permute-start(bf16[256,512]{1,0:T(8,128)(2,1)S(1)} %get-tuple-element.66), channel_id=1, source_target_pairs={{0,96},{16,112},{32,64},{48,80},{64,32},{80,48},{96,0},{112,16},{1... | collective-permute-start | bytes 786440 | tf_op jit(solution)/shard_map/ppermute | solution.py:293
  137.4 26.7 %collective-permute-start.36 = (bf16[256,512]{1,0:T(8,128)(2,1)S(1)}, bf16[256,512]{1,0:T(8,128)(2,1)S(1)}, u32[]{:S(2)}, u32[]{:S(2)}) collective-permute-start(bf16[256,512]{1,0:T(8,128)(2,1)S(1)} %get-tuple-element.67), channel_id=1, source_target_pairs={{0,64},{16,80},{32,96},{48,112},{64,0},{80,16},{96,32},{112,48},{1... | collective-permute-start | bytes 786440 | tf_op jit(solution)/shard_map/ppermute | solution.py:293
  161.8 10.5 %collective-permute-start.28 = (bf16[3,128,256]{2,1,0:T(8,128)(2,1)}, bf16[3,128,256]{2,1,0:T(8,128)(2,1)S(1)}, u32[]{:S(2)}, u32[]{:S(2)}) collective-permute-start(bf16[3,128,256]{2,1,0:T(8,128)(2,1)} %get-tuple-element.57), channel_id=1, source_target_pairs={{0,2},{1,3},{2,0},{3,1},{4,6},{5,7},{6,4},{7,5},{8,10},{9,11},{10,... | collective-permute-start | bytes 589832 | tf_op jit(solution)/shard_map/ppermute | solution.py:293
  162.8 10.3 %collective-permute-start.29 = (bf16[3,128,256]{2,1,0:T(8,128)(2,1)}, bf16[3,128,256]{2,1,0:T(8,128)(2,1)S(1)}, u32[]{:S(2)}, u32[]{:S(2)}) collective-permute-start(bf16[3,128,256]{2,1,0:T(8,128)(2,1)} %get-tuple-element.58), channel_id=1, source_target_pairs={{0,3},{1,2},{2,1},{3,0},{4,7},{5,6},{6,5},{7,4},{8,11},{9,10},{10,... | collective-permute-start | bytes 589832 | tf_op jit(solution)/shard_map/ppermute | solution.py:293
  163.8 14.9 %collective-permute-start.30 = (bf16[3,128,256]{2,1,0:T(8,128)(2,1)}, bf16[3,128,256]{2,1,0:T(8,128)(2,1)S(1)}, u32[]{:S(2)}, u32[]{:S(2)}) collective-permute-start(bf16[3,128,256]{2,1,0:T(8,128)(2,1)} %get-tuple-element.59), channel_id=1, source_target_pairs={{0,4},{1,5},{2,6},{3,7},{4,0},{5,1},{6,2},{7,3},{8,12},{9,13},{10,... | collective-permute-start | bytes 589832 | tf_op jit(solution)/shard_map/ppermute | solution.py:293
  164.1 14.6 %collective-permute-start.31 = (bf16[3,128,256]{2,1,0:T(8,128)(2,1)}, bf16[3,128,256]{2,1,0:T(8,128)(2,1)S(1)}, u32[]{:S(2)}, u32[]{:S(2)}) collective-permute-start(bf16[3,128,256]{2,1,0:T(8,128)(2,1)} %get-tuple-element.60), channel_id=1, source_target_pairs={{0,5},{1,4},{2,7},{3,6},{4,1},{5,0},{6,3},{7,2},{8,13},{9,12},{10,... | collective-permute-start | bytes 589832 | tf_op jit(solution)/shard_map/ppermute | solution.py:293
  168.5 13.6 %collective-permute-start.32 = (bf16[3,128,256]{2,1,0:T(8,128)(2,1)S(1)}, bf16[3,128,256]{2,1,0:T(8,128)(2,1)S(1)}, u32[]{:S(2)}, u32[]{:S(2)}) collective-permute-start(bf16[3,128,256]{2,1,0:T(8,128)(2,1)S(1)} %copy-done.24), channel_id=1, source_target_pairs={{0,6},{1,7},{2,4},{3,5},{4,2},{5,3},{6,0},{7,1},{8,14},{9,15},{10,... | collective-permute-start | bytes 589832 | tf_op jit(solution)/shard_map/ppermute | solution.py:293
  173.0 14.9 %collective-permute-start.38 = (bf16[256,256]{1,0:T(8,128)(2,1)S(1)}, bf16[256,256]{1,0:T(8,128)(2,1)S(1)}, u32[]{:S(2)}, u32[]{:S(2)}) collective-permute-start(bf16[256,256]{1,0:T(8,128)(2,1)S(1)} %select_convert_fusion), channel_id=1, source_target_pairs={{0,8},{8,0},{1,9},{9,1},{2,10},{10,2},{3,11},{11,3},{4,12},{12,4},... | collective-permute-start | bytes 393224 | tf_op jit(solution)/shard_map/ppermute | solution.py:301
  (39 other events, 394.6 us)

commit v2 on v1

v2 whole, which is shorter than its diff:
```python
import functools
import math

import jax
import jax.numpy as jnp
from jax import lax
from jax.experimental import pallas as pl
from jax.experimental.pallas import tpu as pltpu
from jax.sharding import PartitionSpec as P

DH = 128
N = 8
SEQ = 1024
ROWS = SEQ // N
HALF = ROWS // 2
GW = 256
D = 4096
F32 = jnp.float32
BF16 = jnp.bfloat16
VMEM_LIMIT = 56 * 1024 * 1024


def flip_matrix(n):
    a = lax.broadcasted_iota(jnp.int32, (n, n), 0)
    b = lax.broadcasted_iota(jnp.int32, (n, n), 1)
    return (a + b == n - 1).astype(BF16)


def dot(a, b, ca, cb):
    return lax.dot_general(a, b, (((ca,), (cb,)), ((), ())), preferred_element_type=F32)


def params(**kw):
    return pltpu.CompilerParams(vmem_limit_bytes=VMEM_LIMIT, **kw)


def cost(flops, nbytes, trans=0):
    return pl.CostEstimate(flops=int(flops), bytes_accessed=int(nbytes), transcendentals=int(trans))


def struct(*shape, dtype=BF16):
    return jax.ShapeDtypeStruct(shape, dtype)


ANY = pl.BlockSpec(memory_space=pl.ANY)


def split_kernel(x_ref, out):
    for g in range(N):
        out[g] = x_ref[:, :, GW * g : GW * (g + 1)]


def split(x):
    return pl.pallas_call(
        split_kernel,
        in_specs=[pl.BlockSpec(memory_space=pltpu.VMEM)],
        out_specs=pl.BlockSpec(memory_space=pltpu.VMEM),
        out_shape=struct(N, 3, ROWS, GW),
        compiler_params=params(),
        cost_estimate=cost(0, 2 * 3 * ROWS * 2048 * 2),
        name="split",
    )(x)


def assemble_kernel(blocks, out):
    for g in range(N):
        out[:, :, GW * g : GW * (g + 1)] = blocks[g]


def assemble(blocks):
    return pl.pallas_call(
        assemble_kernel,
        in_specs=[pl.BlockSpec(memory_space=pltpu.VMEM)],
        out_specs=pl.BlockSpec(memory_space=pltpu.VMEM),
        out_shape=struct(3, ROWS, 2048),
        compiler_params=params(),
        cost_estimate=cost(0, 2 * 3 * ROWS * 2048 * 2),
        name="assemble",
    )(blocks)


def upstream_kernel(cot, recv, after, out):
    flipped = dot(flip_matrix(HALF), recv[...], 1, 0)
    out[...] = (cot[...].astype(F32) + flipped).astype(BF16)


def upstream_rows(cot, recv, after):
    return pl.pallas_call(
        upstream_kernel,
        grid=(2,),
        in_specs=[pl.BlockSpec((HALF, 2048), lambda k: (0, k))] * 2 + [ANY],
        out_specs=pl.BlockSpec((HALF, 2048), lambda k: (0, k)),
        out_shape=struct(HALF, D),
        compiler_params=params(),
        cost_estimate=cost(2 * 64 * 64 * D, 3 << 19),
        name="upstream_rows",
    )(cot, recv, after)


def fwd_kernel(c_ref, *refs):
    blocks = refs[:N]
    after, cat, att_own, att_send, probs_t = refs[N:]
    q = pl.program_id(0)

    @pl.when(q == 0)
    def _():
        flip = flip_matrix(HALF)
        for j in range(N):
            cat[1, ROWS * j : ROWS * (j + 1), :] = blocks[j][0, 1]
            cat[2, ROWS * j : ROWS * (j + 1), :] = blocks[j][0, 2]
            cat[0, HALF * j : HALF * (j + 1), :] = blocks[j][0, 0, :HALF, :]
            mirrored = dot(flip, blocks[N - 1 - j][0, 0, HALF:, :], 1, 0).astype(BF16)
            cat[0, 512 + HALF * j : 512 + HALF * (j + 1), :] = mirrored

    for h in range(2):
        cols = slice(DH * h, DH * (h + 1))
        queries = cat[0, pl.ds(pl.multiple_of(q * 256, 256), 256), cols]
        scores = dot(cat[1, :, cols], queries, 1, 1) * (1.0 / math.sqrt(DH))
        peak = jnp.max(scores, axis=0, keepdims=True)
        expo = jnp.exp(scores - peak)
        probs = (expo * (1.0 / jnp.sum(expo, axis=0, keepdims=True))).astype(BF16)
        probs_t[h] = probs
        att = jnp.transpose(dot(cat[2, :, cols], probs, 0, 0)).astype(BF16)

        @pl.when(q < 2)
        def _():
            att_own[:, cols] = att

        @pl.when(q >= 2)
        def _():
            att_send[:, cols] = att


def low_half(q, *_):
    return (jnp.minimum(q, 1), 0)


def high_half(q, *_):
    return (jnp.maximum(q - 2, 0), 0)


def attention_fwd(c, blocks, after):
    def block(j):
        return pl.BlockSpec((1, 3, ROWS, GW), lambda q, c_ref: (jnp.bitwise_xor(c_ref[0], j), 0, 0, 0))

    return pl.pallas_call(
        fwd_kernel,
        grid_spec=pltpu.PrefetchScalarGridSpec(
            num_scalar_prefetch=1,
            grid=(4,),
            in_specs=[block(j) for j in range(N)] + [ANY],
            out_specs=[
                pl.BlockSpec((3, SEQ, GW), lambda q, c_ref: (0, 0, 0)),
                pl.BlockSpec((256, GW), low_half),
                pl.BlockSpec((256, GW), high_half),
                pl.BlockSpec((2, SEQ, 256), lambda q, c_ref: (0, 0, q)),
            ],
        ),
        out_shape=[struct(3, SEQ, GW), struct(512, GW), struct(512, GW), struct(2, SEQ, SEQ)],
        compiler_params=params(),
        cost_estimate=cost(4 * 4 * SEQ * SEQ * DH, 10 << 20, 2 * SEQ * SEQ),
        name="attention_fwd",
    )(c, *([blocks] * N), after)


def bwd_kernel(c_ref, cat, probs_t, g_own, g_recv, after, after2, out, dq, dk, dv):
    q = pl.program_id(0)
    rows = pl.ds(pl.multiple_of(q * 256, 256), 256)
    for h in range(2):
        cols = slice(DH * h, DH * (h + 1))
        queries = cat[0, rows, cols]
        grad = jnp.where(q < 2, g_own[:, cols], g_recv[:, cols])
        probs_low = probs_t[h]
        grad_probs = dot(cat[2, :, cols], grad, 1, 1)
        probs = probs_low.astype(F32)
        product = probs * grad_probs
        centre = jnp.sum(product, axis=0, keepdims=True)
        grad_scores = ((product - probs * centre) * (1.0 / math.sqrt(DH))).astype(BF16)
        part_v = dot(probs_low, grad, 1, 0)
        part_k = dot(grad_scores, queries, 1, 0)

        @pl.when(q == 0)
        def _():
            dv[:, cols] = part_v
            dk[:, cols] = part_k

        @pl.when(q > 0)
        def _():
            dv[:, cols] += part_v
            dk[:, cols] += part_k

        dq[rows, cols] = jnp.transpose(dot(cat[1, :, cols], grad_scores, 0, 0)).astype(BF16)

    @pl.when(q == 3)
    def _():
        flip = flip_matrix(HALF)
        for j in range(N):
            to = jnp.bitwise_xor(c_ref[0], j)
            low = 512 + HALF * (N - 1 - j)
            out[to, 0, :HALF, :] = dq[HALF * j : HALF * (j + 1), :]
            out[to, 0, HALF:, :] = dot(flip, dq[low : low + HALF, :], 1, 0).astype(BF16)
            out[to, 1] = dk[ROWS * j : ROWS * (j + 1), :].astype(BF16)
            out[to, 2] = dv[ROWS * j : ROWS * (j + 1), :].astype(BF16)


def attention_bwd(c, cat, probs_t, g_own, g_recv, after, after2):
    return pl.pallas_call(
        bwd_kernel,
        grid_spec=pltpu.PrefetchScalarGridSpec(
            num_scalar_prefetch=1,
            grid=(4,),
            in_specs=[
                pl.BlockSpec((3, SEQ, GW), lambda q, c_ref: (0, 0, 0)),
                pl.BlockSpec((2, SEQ, 256), lambda q, c_ref: (0, 0, q)),
                pl.BlockSpec((256, GW), low_half),
                pl.BlockSpec((256, GW), high_half),
                ANY,
                ANY,
            ],
            out_specs=pl.BlockSpec((N, 3, ROWS, GW), lambda q, c_ref: (0, 0, 0, 0)),
            scratch_shapes=[pltpu.VMEM((SEQ, GW), BF16), pltpu.VMEM((SEQ, GW), F32), pltpu.VMEM((SEQ, GW), F32)],
        ),
        out_shape=struct(N, 3, ROWS, GW),
        compiler_params=params(),
        cost_estimate=cost(8 * 2 * SEQ * SEQ * DH, 8 << 20),
        name="attention_bwd",
    )(c, cat, probs_t, g_own, g_recv, after, after2)


def grad_kernel(*refs):
    pieces = refs[:9]
    w, after, out, acc = refs[9:]
    k = pl.program_id(0)
    rows = jnp.concatenate([p[...] for p in pieces], axis=0)
    part = dot(rows, w[...], 1, 1)

    @pl.when(k == 0)
    def _():
        acc[...] = part

    @pl.when(k > 0)
    def _():
        acc[...] += part

    @pl.when(k == 3)
    def _():
        out[...] = acc[...].astype(BF16)


def grad_attended(pieces, w, after):
    return pl.pallas_call(
        grad_kernel,
        grid=(4,),
        in_specs=[pl.BlockSpec((p.shape[0], 1024), lambda k: (0, k)) for p in pieces]
        + [pl.BlockSpec((GW, 1024), lambda k: (0, k)), ANY],
        out_specs=pl.BlockSpec((512, GW), lambda k: (0, 0)),
        out_shape=struct(512, GW),
        scratch_shapes=[pltpu.VMEM((512, GW), F32)],
        compiler_params=params(),
        cost_estimate=cost(2 * 512 * GW * D, 7 << 20),
        name="grad_attended",
    )(*pieces, w, after)


def project_kernel(own, recv, w, *outs):
    both = (own[...].astype(F32) + recv[...].astype(F32)).astype(BF16)
    part = dot(both, w[...], 1, 0).astype(BF16)
    low = 0
    for out in outs:
        out[...] = part[low : low + out.shape[0], :]
        low += out.shape[0]


def project(own, recv, w):
    rows = (64, 64, 32, 32, 64, 64, 64, 64, 64)
    return pl.pallas_call(
        project_kernel,
        grid=(4,),
        in_specs=[
            pl.BlockSpec((512, GW), lambda k: (0, 0)),
            pl.BlockSpec((512, GW), lambda k: (0, 0)),
            pl.BlockSpec((GW, 1024), lambda k: (0, k)),
        ],
        out_specs=[pl.BlockSpec((r, 1024), lambda k: (0, k)) for r in rows],
        out_shape=[struct(r, D) for r in rows],
        compiler_params=params(),
        cost_estimate=cost(2 * 512 * GW * D, 7 << 20),
        name="project",
    )(own, recv, w)


def weight_kernel(d_ref, own, recv, *refs):
    pieces = refs[:9]
    out_own, out_other = refs[10:]
    both = (own[...].astype(F32) + recv[...].astype(F32)).astype(BF16)
    rows = jnp.concatenate([p[...] for p in pieces], axis=0)
    part = dot(both, rows, 0, 0).astype(BF16)
    first, second = part[:, :512], part[:, 512:]
    core = jnp.bitwise_and(d_ref[0], 1)
    out_own[0] = jnp.where(core == 0, first, second)
    out_other[0] = jnp.where(core == 0, second, first)


def weight_part(d, own, recv, pieces, after):
    def columns(x, d_ref):
        return (0, jnp.bitwise_xor(lax.shift_right_logical(d_ref[0], 1), x))

    return pl.pallas_call(
        weight_kernel,
        grid_spec=pltpu.PrefetchScalarGridSpec(
            num_scalar_prefetch=1,
            grid=(4,),
            in_specs=[pl.BlockSpec((512, GW), lambda x, d_ref: (0, 0))] * 2
            + [pl.BlockSpec((p.shape[0], 1024), columns) for p in pieces]
            + [ANY],
            out_specs=[pl.BlockSpec((1, GW, 512), lambda x, d_ref: (x, 0, 0))] * 2,
        ),
        out_shape=[struct(4, GW, 512)] * 2,
        compiler_params=params(),
        cost_estimate=cost(2 * 512 * GW * D, 7 << 20),
        name="weight_part",
    )(d, own, recv, *pieces, after)


def by_xor(x, axis, k):
    return lax.ppermute(x, axis, [(i, i ^ k) for i in range(N)])


def mirror(x):
    return lax.ppermute(x, ("strand", "ctx"), [(i, 2 * N - 1 - i) for i in range(2 * N)])


def other_strand(x):
    return lax.ppermute(x, "strand", [(0, 1), (1, 0)])


def flip_rows(x):
    return dot(flip_matrix(x.shape[0]), x, 1, 0)


def add(*terms):
    total = terms[0].astype(F32)
    for t in terms[1:]:
        total = total + t.astype(F32)
    return total


def relay_kernel(y1, y3, after, low, high):
    low[...] = y3[:32, :]
    high[...] = y1[32:, :]


def relay(y1, y3, after):
    return pl.pallas_call(
        relay_kernel,
        in_specs=[pl.BlockSpec(memory_space=pltpu.VMEM)] * 2 + [ANY],
        out_specs=[pl.BlockSpec(memory_space=pltpu.VMEM)] * 2,
        out_shape=[struct(32, D)] * 2,
        compiler_params=params(),
        cost_estimate=cost(0, 3 << 19),
        name="relay",
    )(y1, y3, after)


def gather_rows(u, after):
    y1, y3, z = (by_xor(u, "ctx", k) for k in (1, 3, 4))
    low, high = relay(y1, y3, after)
    y2a = by_xor(low, "ctx", 1)
    y2b = by_xor(high, "ctx", 3)
    zy1 = by_xor(z, "ctx", 1)
    zy3 = by_xor(z, "ctx", 3)
    zy2 = by_xor(jnp.concatenate([y2a, y2b], axis=0), "ctx", 4)
    return [u, y1, y2a, y2b, y3, z, zy1, zy2, zy3]


def scatter_rows(parts):
    p0, p1, p2a, p2b, p3, p4, p5, p6, p7 = parts
    r5 = by_xor(p5, "ctx", 1)
    r7 = by_xor(p7, "ctx", 3)
    r6 = by_xor(p6, "ctx", 4)
    p2a = add(p2a, r6[:32]).astype(BF16)
    p2b = add(p2b, r6[32:]).astype(BF16)
    p4 = add(p4, r5, r7).astype(BF16)
    r2a = by_xor(p2a, "ctx", 1)
    r2b = by_xor(p2b, "ctx", 3)
    r4 = by_xor(p4, "ctx", 4)
    p3 = add(p3, jnp.pad(r2a, ((0, 32), (0, 0)))).astype(BF16)
    p1 = add(p1, jnp.pad(r2b, ((32, 0), (0, 0)))).astype(BF16)
    r3 = by_xor(p3, "ctx", 3)
    r1 = by_xor(p1, "ctx", 1)
    return add(p0, r1, r3, r4), p4


def body(qkv, out_weight, cotangent):
    c = lax.axis_index("ctx").astype(jnp.int32).reshape(1)
    d = lax.axis_index("dp").astype(jnp.int32).reshape(1)
    s = lax.axis_index("strand")
    mine = jnp.transpose(qkv[0, 0], (1, 0, 2))
    cot = cotangent[0, 0]

    cot_recv = mirror(cot[HALF:])
    blocks = lax.all_to_all(split(mine), "ctx", split_axis=0, concat_axis=0, tiled=True)

    upstream = upstream_rows(cot, cot_recv, blocks)
    cat, att_own, att_send, probs_t = attention_fwd(c, blocks, upstream)
    att_recv = other_strand(att_send)
    pieces = gather_rows(upstream, att_own)

    partial = project(att_own, att_recv, out_weight)
    mixed_rows, relayed = scatter_rows(partial)
    mixed_own = mixed_rows.astype(BF16)
    mixed_recv = mirror(mixed_own)
    mixed = jnp.concatenate([mixed_own, flip_rows(mixed_recv).astype(BF16)], axis=0)

    g_own = grad_attended(pieces, out_weight, partial[0])
    g_recv = other_strand(g_own)
    w_own, w_other = weight_part(d, att_own, att_recv, pieces, g_own)

    grads = attention_bwd(c, cat, probs_t, g_own, g_recv, w_own, relayed)
    back = lax.all_to_all(grads, "ctx", split_axis=0, concat_axis=0, tiled=True)
    qkv_grad = jnp.transpose(assemble(back), (1, 0, 2))

    w_sum = add(w_own, by_xor(w_other, "dp", 1)).astype(BF16)
    w_chip = add(w_sum[0], *[by_xor(w_sum[x], "dp", 2 * x) for x in range(1, 4)])
    first, second = w_chip[:, :GW], w_chip[:, GW:]
    w_keep = jnp.where(s == 0, first, second)
    w_send = jnp.where(s == 0, second, first).astype(BF16)
    weight_grad = w_keep + other_strand(w_send).astype(F32)
    return (mixed[None, None], qkv_grad[None, None], weight_grad)


def solution(mesh):
    placed = (P("dp", "strand", "ctx", None, None), P("ctx", None), P("dp", "strand", "ctx", None))
    return jax.shard_map(
        body,
        mesh=mesh,
        in_specs=placed,
        out_specs=(
            P("dp", "strand", "ctx", None),
            P("dp", "strand", "ctx", None, None),
            P("ctx", ("dp", "strand")),
        ),
        check_vma=False,
    )
```

time: 191 us -> 191 us (level)
  starting transfers between devices: 68.4 us -> 40.7 us
  waiting for transfers between devices: 59.7 us -> 78.4 us
  Pallas kernels: 47 us -> 51.1 us
  local copies, waits for them, and re-layouts: 3.53 us -> 7.32 us
    ppermute x34 -> x20, starting transfers between devices: 53.9 us -> 20.7 us  [by_xor(): return lax.ppermute(x, axis, [(i, i ^ k) for i in range(N)])]
    ppermute x2, waiting for transfers between devices: 0.01 us -> 28.3 us  [mirror(): lax.ppermute(x, ('strand', 'ctx'), [(i, 2 * N - 1 - i) for i in range(2 *...]
    ppermute x34 -> x20, waiting for transfers between devices: 41.5 us -> 24.4 us  [by_xor(): return lax.ppermute(x, axis, [(i, i ^ k) for i in range(N)])]
    all_to_all x0 -> x2, starting transfers between devices: none -> 11.6 us  [the longest x1 6.4 us: body(): lax.all_to_all(split(mine), 'ctx', split_axis=0, concat_axis=0, tiled=True)]
    ppermute x3, waiting for transfers between devices: 18.2 us -> 25.7 us  [other_strand(): return lax.ppermute(x, 'strand', [(0, 1), (1, 0)])]
    ppermute x3, starting transfers between devices: 8.21 us -> 2.27 us  [other_strand(): return lax.ppermute(x, 'strand', [(0, 1), (1, 0)])]
    pallas_call x3 -> x5, Pallas kernels: 28.4 us -> 32.6 us  [the longest x1 13.3 us: attention_bwd(): pl.pallas_call(bwd_kernel, grid_spec=pltpu.PrefetchScalarGridSpec(num_sca...]
    unnamed x64 -> x44, local copies, waits for them, and re-layouts: 3.41 us -> 6.35 us
  transfers between devices with their start and end apart: 39 -> 27, of which waited for: 17 -> 8; matrix products, arithmetic and copies ran while one was open for 4% -> 7% of each run, Pallas kernels for 17% -> 16%
where the time goes in v2:
time: 191 us; the launch traced here: 190 us
  waiting for transfers between devices  78.4 us (41%)
  Pallas kernels  51.1 us (27%)
  starting transfers between devices  40.7 us (21%)
  other arithmetic  10.1 us (5%)
  local copies, waits for them, and re-layouts  7.32 us (4%)
    ppermute x2, waiting for transfers between devices, mirror(): lax.ppermute(x, ('strand', 'ctx'), [(i, 2 * N - 1 - i) for i in range(2 *...  28.3 us
    ppermute x3, waiting for transfers between devices, other_strand(): return lax.ppermute(x, 'strand', [(0, 1), (1, 0)])  25.7 us
    ppermute x20, waiting for transfers between devices, by_xor(): return lax.ppermute(x, axis, [(i, i ^ k) for i in range(N)])  24.4 us
    ppermute x20, starting transfers between devices, by_xor(): return lax.ppermute(x, axis, [(i, i ^ k) for i in range(N)])  20.7 us
    pallas_call x1, Pallas kernels, attention_bwd(): pl.pallas_call(bwd_kernel, grid_spec=pltpu.PrefetchScalarGridSpec(num_sca...  13.3 us
    pallas_call x1, Pallas kernels, attention_fwd(): pl.pallas_call(fwd_kernel, grid_spec=pltpu.PrefetchScalarGridSpec(num_sca...  12.3 us
    all_to_all x1, starting transfers between devices, body(): lax.all_to_all(split(mine), 'ctx', split_axis=0, concat_axis=0, tiled=True)  6.4 us
    unnamed x44, local copies, waits for them, and re-layouts  6.35 us
  transfers between devices with their start and end apart: 27, of which 8 were waited for; matrix products, arithmetic and copies ran while one was open for 7% of the time, Pallas kernels for 16%

profile of v2, /device:TPU:8, one launch (start us, length us, event | category | flops | bytes accessed | tf_op | source)
XLA Modules:
  0.0 189.8 jit_solution(13694435630349747404)
XLA Ops:
  0.6 2.7 %split.1 = bf16[8,3,128,256]{3,2,1,0:T(8,128)(2,1)} custom-call(bf16[3,128,2048]{2,1,0:T(8,128)(2,1)} %bitcast.26), custom_call_target="tpu_custom_call" | custom-call | bytes 3145728 | tf_op jit(solution)/shard_map/split/pallas_call | solution.py:54
  3.3 6.4 %all-to-all-start = ((bf16[8,3,128,256]{3,2,1,0:T(8,128)(2,1)}), bf16[8,3,128,256]{3,2,1,0:T(8,128)(2,1)S(1)}, u32[]{:S(2)}, u32[]{:S(2)}) async-start(bf16[8,3,128,256]{3,2,1,0:T(8,128)(2,1)} %split.1), calls=%async_computation | async-start | bytes 3145728 | tf_op jit(solution)/shard_map/all_to_all | solution.py:402
  9.7 4.6 %collective-permute-start = (bf16[64,4096]{1,0:T(8,128)(2,1)S(1)}, bf16[64,4096]{1,0:T(8,128)(2,1)S(1)}, u32[]{:S(2)}, u32[]{:S(2)}) collective-permute-start(bf16[64,4096]{1,0:T(8,128)(2,1)S(1)} %slice_bitcast_fusion), channel_id=1, source_target_pairs={{0,15},{1,14},{2,13},{3,12},{4,11},{5,10},{6,9},{7,8},{8,7},{9,6},... | collective-permute-start | bytes 1572872 | tf_op jit(solution)/shard_map/ppermute | solution.py:330
  14.3 28.3 %collective-permute-done.recv = bf16[64,4096]{1,0:T(8,128)(2,1)S(1)} collective-permute-done((bf16[64,4096]{1,0:T(8,128)(2,1)S(1)}, bf16[64,4096]{1,0:T(8,128)(2,1)S(1)}, u32[]{:S(2)}, u32[]{:S(2)}) %collective-permute-start) | collective-permute-done | bytes 524320 | tf_op jit(solution)/shard_map/ppermute | solution.py:330
  43.9 2.2 %upstream_rows.1.refs_8_.refs_0_ = bf16[64,4096]{1,0:T(8,128)(2,1)} custom-call(bf16[128,4096]{1,0:T(8,128)(2,1)} %bitcast.25, bf16[64,4096]{1,0:T(8,128)(2,1)} %copy-done.15, bf16[8,3,128,256]{3,2,1,0:T(8,128)(2,1)} %copy-done), custom_call_target="tpu_custom_call" | custom-call | flops 33554432 | bytes 1572864 | tf_op jit(solution)/shard_map/upstream_rows/pallas_call | solution.py:88
  46.1 12.3 %attention_fwd.1 = (bf16[3,1024,256]{2,1,0:T(8,128)(2,1)}, bf16[512,256]{1,0:T(8,128)(2,1)}, bf16[512,256]{1,0:T(8,128)(2,1)}, bf16[2,1024,1024]{2,1,0:T(8,128)(2,1)}) custom-call(s32[1]{0:T(128)} %bitcast.c_ref, bf16[8,3,128,256]{3,2,1,0:T(8,128)(2,1)} %copy-done, bf16[8,3,128,256]{3,2,1,0:T(8,128)(2,1)} %copy-done, bf16[8,3,128,256]{3,2,1,0:T(8,128)(2,1)} %copy-done, ...), custom_call_target="tpu_custom_call" | custom-call | flops 2147483648 | bytes 10485760 | tf_op jit(solution)/shard_map/attention_fwd/pallas_call | solution.py:146
  58.4 1.9 collective-permute-start.11
  60.7 8.7 %collective-permute-done.1.recv = bf16[512,256]{1,0:T(8,128)(2,1)S(1)} collective-permute-done((bf16[512,256]{1,0:T(8,128)(2,1)}, bf16[512,256]{1,0:T(8,128)(2,1)S(1)}, u32[]{:S(2)}, u32[]{:S(2)}) %collective-permute-start.1) | collective-permute-done | bytes 262176 | tf_op jit(solution)/shard_map/ppermute | solution.py:334
  70.1 4.9 %project.1 = (bf16[64,4096]{1,0:T(8,128)(2,1)}, bf16[64,4096]{1,0:T(8,128)(2,1)}, bf16[32,4096]{1,0:T(8,128)(2,1)}, bf16[32,4096]{1,0:T(8,128)(2,1)}, bf16[64,40...) custom-call(bf16[512,256]{1,0:T(8,128)(2,1)} %get-tuple-element.20.o, ...), custom_call_target="tpu_custom_call" | custom-call | flops 1073741824 | bytes 7340032 | tf_op jit(solution)/shard_map/project/pallas_call | solution.py:276
  78.7 2.0 %relay.1 = (bf16[32,4096]{1,0:T(8,128)(2,1)}, bf16[32,4096]{1,0:T(8,128)(2,1)}) custom-call(bf16[64,4096]{1,0:T(8,128)(2,1)} %copy-done.3, bf16[64,4096]{1,0:T(8,128)(2,1)} %copy-done.4, bf16[512,256]{1,0:T(8,128)(2,1)} %get-tuple-element.20.own.after), custom_call_target="tpu_custom_call" | custom-call | bytes 1572864 | tf_op jit(solution)/shard_map/relay/pallas_call | solution.py:354
  81.7 1.5 collective-permute-start.14
  83.2 7.0 %collective-permute-done.8 = bf16[64,4096]{1,0:T(8,128)(2,1)S(1)} collective-permute-done((bf16[64,4096]{1,0:T(8,128)(2,1)}, bf16[64,4096]{1,0:T(8,128)(2,1)S(1)}, u32[]{:S(2)}, u32[]{:S(2)}) %collective-permute-start.8) | collective-permute-done | bytes 524320 | tf_op jit(solution)/shard_map/ppermute | solution.py:326
  90.2 3.0 %collective-permute-start.16 = (bf16[64,4096]{1,0:T(8,128)(2,1)S(1)}, bf16[64,4096]{1,0:T(8,128)(2,1)S(1)}, u32[]{:S(2)}, u32[]{:S(2)}) collective-permute-start(bf16[64,4096]{1,0:T(8,128)(2,1)S(1)} %collective-permute-done.15.refs_5_), channel_id=1, source_target_pairs={{0,1},{1,0},{2,3},{3,2},{4,5},{5,4},{6,7},{7,6},{8,9},{9,8},{10,11... | collective-permute-start | bytes 1572872 | tf_op jit(solution)/shard_map/ppermute | solution.py:326
  93.2 2.1 %add_convert_fusion.2.after2 = bf16[64,4096]{1,0:T(8,128)(2,1)} fusion(bf16[64,4096]{1,0:T(8,128)(2,1)S(1)} %collective-permute-done.8, bf16[64,4096]{1,0:T(8,128)(2,1)S(1)} %collective-permute-done.7, bf16[64,4096]{1,0:T(8,128)(2,1)} %get-tuple-element.28), kind=kLoop, calls=%fused_computation.4 | loop fusion | flops 1572864 | bytes 2097152 | tf_op jit(solution)/shard_map/convert_element_type | solution.py:383
  95.4 1.3 collective-permute-done.13.refs_2_
  97.8 2.4 %collective-permute-start.3 = (bf16[32,4096]{1,0:T(8,128)(2,1)S(1)}, bf16[32,4096]{1,0:T(8,128)(2,1)S(1)}, u32[]{:S(2)}, u32[]{:S(2)}) collective-permute-start(bf16[32,4096]{1,0:T(8,128)(2,1)S(1)} %get-tuple-element.40), channel_id=1, source_target_pairs={{0,3},{1,2},{2,1},{3,0},{4,7},{5,6},{6,5},{7,4},{8,11},{9,10},{10,... | collective-permute-start | bytes 786440 | tf_op jit(solution)/shard_map/ppermute | solution.py:326
  100.2 10.2 %collective-permute-done.5 = bf16[32,4096]{1,0:T(8,128)(2,1)S(1)} collective-permute-done((bf16[32,4096]{1,0:T(8,128)(2,1)S(1)}, bf16[32,4096]{1,0:T(8,128)(2,1)S(1)}, u32[]{:S(2)}, u32[]{:S(2)}) %collective-permute-start.5) | collective-permute-done | bytes 262176 | tf_op jit(solution)/shard_map/ppermute | solution.py:326
  113.1 2.3 %collective-permute-start.4 = (bf16[64,4096]{1,0:T(8,128)(2,1)}, bf16[64,4096]{1,0:T(8,128)(2,1)}, u32[]{:S(2)}, u32[]{:S(2)}) collective-permute-start(bf16[64,4096]{1,0:T(8,128)(2,1)} %add_convert_fusion.4), channel_id=1, source_target_pairs={{0,1},{1,0},{2,3},{3,2},{4,5},{5,4},{6,7},{7,6},{8,9},{9,8},{10,11... | collective-permute-start | bytes 1572872 | tf_op jit(solution)/shard_map/ppermute | solution.py:326
  115.5 5.9 %collective-permute-done.17.refs_7_ = bf16[64,4096]{1,0:T(8,128)(2,1)S(1)} collective-permute-done((bf16[64,4096]{1,0:T(8,128)(2,1)S(1)}, bf16[64,4096]{1,0:T(8,128)(2,1)S(1)}, u32[]{:S(2)}, u32[]{:S(2)}) %collective-permute-start.17) | collective-permute-done | bytes 524320 | tf_op jit(solution)/shard_map/ppermute | solution.py:326
  122.2 5.3 %grad_attended.1.refs_9_.g_own = bf16[512,256]{1,0:T(8,128)(2,1)} custom-call(bf16[64,4096]{1,0:T(8,128)(2,1)} %upstream_rows.1.refs_8_.refs_0_, bf16[64,4096]{1,0:T(8,128)(2,1)} %copy-done.3, bf16[32,4096]{1,0:T(8,128)(2,1)} %copy-done.7, bf16[32,4096]{1,0:T(8,128)(2,1)} %copy-done.8, bf16[64,4096]{1,0:T(8,128)(2,1)} %copy-done.4, ...), custom_call_target="tpu_custom_call" | custom-call | flops 1073741824 | bytes 7340032 | tf_op jit(solution)/shard_map/grad_attended/pallas_call | solution.py:251
  127.5 5.6 %weight_part.1 = (bf16[4,256,512]{2,1,0:T(8,128)(2,1)}, bf16[4,256,512]{2,1,0:T(8,128)(2,1)}) custom-call(s32[1]{0:T(128)} %bitcast.6.d_ref, bf16[512,256]{1,0:T(8,128)(2,1)} %get-tuple-element.20.own.after, bf16[512,256]{1,0:T(8,128)(2,1)} %copy-done.18, bf16[64,4096]{1,0:T(8,128)(2,1)} %upstream_rows.1.refs_8_.refs_0_, bf16[64,4096]{1,0:T(8,128)(2,1)} %copy-done.3, ...), custom_call_target="tpu_custom_call" | custom-call | flops 1073741824 | bytes 7340032 | tf_op jit(solution)/shard_map/weight_part/pallas_call | solution.py:308
  133.2 1.3 collective-permute-start.19
  134.6 1.6 add_convert_fusion.1
  136.2 1.6 collective-permute-start.10
  137.8 1.5 add_convert_fusion
  140.3 2.8 %collective-permute-start.23 = (bf16[256,512]{1,0:T(8,128)(2,1)}, bf16[256,512]{1,0:T(8,128)(2,1)S(1)}, u32[]{:S(2)}, u32[]{:S(2)}) collective-permute-start(bf16[256,512]{1,0:T(8,128)(2,1)} %get-tuple-element.38), channel_id=1, source_target_pairs={{0,96},{16,112},{32,64},{48,80},{64,32},{80,48},{96,0},{112,16},{1... | collective-permute-start | bytes 786440 | tf_op jit(solution)/shard_map/ppermute | solution.py:326
  144.3 1.4 collective-permute-done.19.g_recv
  146.5 13.3 %attention_bwd.1 = bf16[8,3,128,256]{3,2,1,0:T(8,128)(2,1)} custom-call(s32[1]{0:T(128)} %bitcast.c_ref, bf16[3,1024,256]{2,1,0:T(8,128)(2,1)} %get-tuple-element.31.cat, bf16[2,1024,1024]{2,1,0:T(8,128)(2,1)} %get-tuple-element.32.probs_t, bf16[512,256]{1,0:T(8,128)(2,1)} %grad_attended.1.refs_9_.g_own, bf16[512,256]{1,0:T(8,128)(2,1)} %copy-done.19, ...), custom_call_target="tpu_custom_call" | custom-call | flops 2147483648 | bytes 8388608 | tf_op jit(solution)/shard_map/attention_bwd/pallas_call | solution.py:207
  159.8 5.2 %all-to-all-start.1 = ((bf16[8,3,128,256]{3,2,1,0:T(8,128)(2,1)}), bf16[8,3,128,256]{3,2,1,0:T(8,128)(2,1)S(1)}, u32[]{:S(2)}, u32[]{:S(2)}) async-start(bf16[8,3,128,256]{3,2,1,0:T(8,128)(2,1)} %attention_bwd.1), calls=%async_computation.1 | async-start | bytes 3145728 | tf_op jit(solution)/shard_map/all_to_all | solution.py:420
  165.0 1.3 convolution_convert_fusion
  169.5 15.6 %collective-permute-done.24 = bf16[256,256]{1,0:T(8,128)(2,1)S(1)} collective-permute-done((bf16[256,256]{1,0:T(8,128)(2,1)S(1)}, bf16[256,256]{1,0:T(8,128)(2,1)S(1)}, u32[]{:S(2)}, u32[]{:S(2)}) %collective-permute-start.24) | collective-permute-done | bytes 131104 | tf_op jit(solution)/shard_map/ppermute | solution.py:334
  187.1 2.8 %assemble.1 = bf16[3,128,2048]{2,1,0:T(8,128)(2,1)} custom-call(bf16[8,3,128,256]{3,2,1,0:T(8,128)(2,1)} %copy-done.2), custom_call_target="tpu_custom_call" | custom-call | bytes 3145728 | tf_op jit(solution)/shard_map/assemble/pallas_call | solution.py:71
  (89 shorter events, 20.1 us)
Async XLA Ops:
  3.3 39.3 %all-to-all-start = ((bf16[8,3,128,256]{3,2,1,0:T(8,128)(2,1)}), bf16[8,3,128,256]{3,2,1,0:T(8,128)(2,1)S(1)}, u32[]{:S(2)}, u32[]{:S(2)}) async-start(bf16[8,3,128,256]{3,2,1,0:T(8,128)(2,1)} %split.1), calls=%async_computation | async-start | bytes 3145728 | tf_op jit(solution)/shard_map/all_to_all | solution.py:402
  9.7 32.9 %collective-permute-start = (bf16[64,4096]{1,0:T(8,128)(2,1)S(1)}, bf16[64,4096]{1,0:T(8,128)(2,1)S(1)}, u32[]{:S(2)}, u32[]{:S(2)}) collective-permute-start(bf16[64,4096]{1,0:T(8,128)(2,1)S(1)} %slice_bitcast_fusion), channel_id=1, source_target_pairs={{0,15},{1,14},{2,13},{3,12},{4,11},{5,10},{6,9},{7,8},{8,7},{9,6},... | collective-permute-start | bytes 1572872 | tf_op jit(solution)/shard_map/ppermute | solution.py:330
  58.4 11.0 %collective-permute-start.1 = (bf16[512,256]{1,0:T(8,128)(2,1)}, bf16[512,256]{1,0:T(8,128)(2,1)S(1)}, u32[]{:S(2)}, u32[]{:S(2)}) collective-permute-start(bf16[512,256]{1,0:T(8,128)(2,1)} %get-tuple-element.21), channel_id=1, source_target_pairs={{0,8},{8,0},{1,9},{9,1},{2,10},{10,2},{3,11},{11,3},{4,12},{12,4},... | collective-permute-start | bytes 786440 | tf_op jit(solution)/shard_map/ppermute | solution.py:334
  58.4 18.7 %collective-permute-start.11 = (bf16[64,4096]{1,0:T(8,128)(2,1)S(1)}, bf16[64,4096]{1,0:T(8,128)(2,1)S(1)}, u32[]{:S(2)}, u32[]{:S(2)}) collective-permute-start(bf16[64,4096]{1,0:T(8,128)(2,1)S(1)} %copy-done.1), channel_id=1, source_target_pairs={{0,1},{1,0},{2,3},{3,2},{4,5},{5,4},{6,7},{7,6},{8,9},{9,8},{10,11... | collective-permute-start | bytes 1572872 | tf_op jit(solution)/shard_map/ppermute | solution.py:326
  60.3 16.8 %collective-permute-start.12 = (bf16[64,4096]{1,0:T(8,128)(2,1)S(1)}, bf16[64,4096]{1,0:T(8,128)(2,1)S(1)}, u32[]{:S(2)}, u32[]{:S(2)}) collective-permute-start(bf16[64,4096]{1,0:T(8,128)(2,1)S(1)} %copy-done.1), channel_id=1, source_target_pairs={{0,3},{1,2},{2,1},{3,0},{4,7},{5,6},{6,5},{7,4},{8,11},{9,10},{10,... | collective-permute-start | bytes 1572872 | tf_op jit(solution)/shard_map/ppermute | solution.py:326
  60.3 21.4 %collective-permute-start.15 = (bf16[64,4096]{1,0:T(8,128)(2,1)S(1)}, bf16[64,4096]{1,0:T(8,128)(2,1)S(1)}, u32[]{:S(2)}, u32[]{:S(2)}) collective-permute-start(bf16[64,4096]{1,0:T(8,128)(2,1)S(1)} %copy-done.1), channel_id=1, source_target_pairs={{0,4},{1,5},{2,6},{3,7},{4,0},{5,1},{6,2},{7,3},{8,12},{9,13},{10,... | collective-permute-start | bytes 1572872 | tf_op jit(solution)/shard_map/ppermute | solution.py:326
  75.0 20.2 %copy-start.20 = (bf16[32,4096]{1,0:T(8,128)(2,1)S(1)}, bf16[32,4096]{1,0:T(8,128)(2,1)}, u32[]{:S(2)}) copy-start(bf16[32,4096]{1,0:T(8,128)(2,1)} %get-tuple-element.27) | copy-start | bytes 786436
  75.0 20.2 %copy-start.21 = (bf16[32,4096]{1,0:T(8,128)(2,1)S(1)}, bf16[32,4096]{1,0:T(8,128)(2,1)}, u32[]{:S(2)}) copy-start(bf16[32,4096]{1,0:T(8,128)(2,1)} %get-tuple-element.24) | copy-start | bytes 786436
  75.0 15.2 %collective-permute-start.8 = (bf16[64,4096]{1,0:T(8,128)(2,1)}, bf16[64,4096]{1,0:T(8,128)(2,1)S(1)}, u32[]{:S(2)}, u32[]{:S(2)}) collective-permute-start(bf16[64,4096]{1,0:T(8,128)(2,1)} %get-tuple-element.30), channel_id=1, source_target_pairs={{0,3},{1,2},{2,1},{3,0},{4,7},{5,6},{6,5},{7,4},{8,11},{9,10},{10,... | collective-permute-start | bytes 1572872 | tf_op jit(solution)/shard_map/ppermute | solution.py:326
  76.0 17.1 %collective-permute-start.7 = (bf16[64,4096]{1,0:T(8,128)(2,1)}, bf16[64,4096]{1,0:T(8,128)(2,1)S(1)}, u32[]{:S(2)}, u32[]{:S(2)}) collective-permute-start(bf16[64,4096]{1,0:T(8,128)(2,1)} %get-tuple-element.29), channel_id=1, source_target_pairs={{0,1},{1,0},{2,3},{3,2},{4,5},{5,4},{6,7},{7,6},{8,9},{9,8},{10,11... | collective-permute-start | bytes 1572872 | tf_op jit(solution)/shard_map/ppermute | solution.py:326
  77.1 18.1 %collective-permute-start.2 = (bf16[64,4096]{1,0:T(8,128)(2,1)}, bf16[64,4096]{1,0:T(8,128)(2,1)S(1)}, u32[]{:S(2)}, u32[]{:S(2)}) collective-permute-start(bf16[64,4096]{1,0:T(8,128)(2,1)} %get-tuple-element.25), channel_id=1, source_target_pairs={{0,4},{1,5},{2,6},{3,7},{4,0},{5,1},{6,2},{7,3},{8,12},{9,13},{10,... | collective-permute-start | bytes 1572872 | tf_op jit(solution)/shard_map/ppermute | solution.py:326
  80.7 16.0 %collective-permute-start.13 = (bf16[32,4096]{1,0:T(8,128)(2,1)}, bf16[32,4096]{1,0:T(8,128)(2,1)S(1)}, u32[]{:S(2)}, u32[]{:S(2)}) collective-permute-start(bf16[32,4096]{1,0:T(8,128)(2,1)} %get-tuple-element.33), channel_id=1, source_target_pairs={{0,1},{1,0},{2,3},{3,2},{4,5},{5,4},{6,7},{7,6},{8,9},{9,8},{10,11... | collective-permute-start | bytes 786440 | tf_op jit(solution)/shard_map/ppermute | solution.py:326
  81.7 18.6 %copy-start.11 = (bf16[64,4096]{1,0:T(8,128)(2,1)}, bf16[64,4096]{1,0:T(8,128)(2,1)S(1)}, u32[]{:S(2)}) copy-start(bf16[64,4096]{1,0:T(8,128)(2,1)S(1)} %collective-permute-done.15.refs_5_) | copy-start | bytes 1572868
  81.7 16.2 %collective-permute-start.14 = (bf16[32,4096]{1,0:T(8,128)(2,1)}, bf16[32,4096]{1,0:T(8,128)(2,1)S(1)}, u32[]{:S(2)}, u32[]{:S(2)}) collective-permute-start(bf16[32,4096]{1,0:T(8,128)(2,1)} %get-tuple-element.34), channel_id=1, source_target_pairs={{0,3},{1,2},{2,1},{3,0},{4,7},{5,6},{6,5},{7,4},{8,11},{9,10},{10,... | collective-permute-start | bytes 786440 | tf_op jit(solution)/shard_map/ppermute | solution.py:326
  90.2 22.9 %collective-permute-start.16 = (bf16[64,4096]{1,0:T(8,128)(2,1)S(1)}, bf16[64,4096]{1,0:T(8,128)(2,1)S(1)}, u32[]{:S(2)}, u32[]{:S(2)}) collective-permute-start(bf16[64,4096]{1,0:T(8,128)(2,1)S(1)} %collective-permute-done.15.refs_5_), channel_id=1, source_target_pairs={{0,1},{1,0},{2,3},{3,2},{4,5},{5,4},{6,7},{7,6},{8,9},{9,8},{10,11... | collective-permute-start | bytes 1572872 | tf_op jit(solution)/shard_map/ppermute | solution.py:326
  93.1 22.3 %collective-permute-start.18 = (bf16[64,4096]{1,0:T(8,128)(2,1)S(1)}, bf16[64,4096]{1,0:T(8,128)(2,1)S(1)}, u32[]{:S(2)}, u32[]{:S(2)}) collective-permute-start(bf16[64,4096]{1,0:T(8,128)(2,1)S(1)} %collective-permute-done.15.refs_5_), channel_id=1, source_target_pairs={{0,3},{1,2},{2,1},{3,0},{4,7},{5,6},{6,5},{7,4},{8,11},{9,10},{10,... | collective-permute-start | bytes 1572872 | tf_op jit(solution)/shard_map/ppermute | solution.py:326
  95.2 39.3 %collective-permute-start.9 = (bf16[64,4096]{1,0:T(8,128)(2,1)}, bf16[64,4096]{1,0:T(8,128)(2,1)}, u32[]{:S(2)}, u32[]{:S(2)}) collective-permute-start(bf16[64,4096]{1,0:T(8,128)(2,1)} %add_convert_fusion.2.after2), channel_id=1, source_target_pairs={{0,4},{1,5},{2,6},{3,7},{4,0},{5,1},{6,2},{7,3},{8,12},{9,13},{10,... | collective-permute-start | bytes 1572872 | tf_op jit(solution)/shard_map/ppermute | solution.py:326
  96.7 24.6 %copy-start.7 = (bf16[32,4096]{1,0:T(8,128)(2,1)}, bf16[32,4096]{1,0:T(8,128)(2,1)S(1)}, u32[]{:S(2)}) copy-start(bf16[32,4096]{1,0:T(8,128)(2,1)S(1)} %collective-permute-done.13.refs_2_) | copy-start | bytes 786436
  96.7 13.8 %collective-permute-start.5 = (bf16[32,4096]{1,0:T(8,128)(2,1)S(1)}, bf16[32,4096]{1,0:T(8,128)(2,1)S(1)}, u32[]{:S(2)}, u32[]{:S(2)}) collective-permute-start(bf16[32,4096]{1,0:T(8,128)(2,1)S(1)} %get-tuple-element.41), channel_id=1, source_target_pairs={{0,1},{1,0},{2,3},{3,2},{4,5},{5,4},{6,7},{7,6},{8,9},{9,8},{10,11... | collective-permute-start | bytes 786440 | tf_op jit(solution)/shard_map/ppermute | solution.py:326
  97.8 23.5 %copy-start.8 = (bf16[32,4096]{1,0:T(8,128)(2,1)}, bf16[32,4096]{1,0:T(8,128)(2,1)S(1)}, u32[]{:S(2)}) copy-start(bf16[32,4096]{1,0:T(8,128)(2,1)S(1)} %collective-permute-done.14.refs_3_) | copy-start | bytes 786436
  97.8 13.5 %collective-permute-start.3 = (bf16[32,4096]{1,0:T(8,128)(2,1)S(1)}, bf16[32,4096]{1,0:T(8,128)(2,1)S(1)}, u32[]{:S(2)}, u32[]{:S(2)}) collective-permute-start(bf16[32,4096]{1,0:T(8,128)(2,1)S(1)} %get-tuple-element.40), channel_id=1, source_target_pairs={{0,3},{1,2},{2,1},{3,0},{4,7},{5,6},{6,5},{7,4},{8,11},{9,10},{10,... | collective-permute-start | bytes 786440 | tf_op jit(solution)/shard_map/ppermute | solution.py:326
  110.5 10.8 %collective-permute-start.17 = (bf16[64,4096]{1,0:T(8,128)(2,1)S(1)}, bf16[64,4096]{1,0:T(8,128)(2,1)S(1)}, u32[]{:S(2)}, u32[]{:S(2)}) collective-permute-start(bf16[64,4096]{1,0:T(8,128)(2,1)S(1)} %pad_maximum_fusion), channel_id=1, source_target_pairs={{0,4},{1,5},{2,6},{3,7},{4,0},{5,1},{6,2},{7,3},{8,12},{9,13},{10,... | collective-permute-start | bytes 1572872 | tf_op jit(solution)/shard_map/ppermute | solution.py:326
  111.3 23.2 %collective-permute-start.6 = (bf16[64,4096]{1,0:T(8,128)(2,1)}, bf16[64,4096]{1,0:T(8,128)(2,1)}, u32[]{:S(2)}, u32[]{:S(2)}) collective-permute-start(bf16[64,4096]{1,0:T(8,128)(2,1)} %add_convert_fusion.3), channel_id=1, source_target_pairs={{0,3},{1,2},{2,1},{3,0},{4,7},{5,6},{6,5},{7,4},{8,11},{9,10},{10,... | collective-permute-start | bytes 1572872 | tf_op jit(solution)/shard_map/ppermute | solution.py:326
  113.1 21.5 %collective-permute-start.4 = (bf16[64,4096]{1,0:T(8,128)(2,1)}, bf16[64,4096]{1,0:T(8,128)(2,1)}, u32[]{:S(2)}, u32[]{:S(2)}) collective-permute-start(bf16[64,4096]{1,0:T(8,128)(2,1)} %add_convert_fusion.4), channel_id=1, source_target_pairs={{0,1},{1,0},{2,3},{3,2},{4,5},{5,4},{6,7},{7,6},{8,9},{9,8},{10,11... | collective-permute-start | bytes 1572872 | tf_op jit(solution)/shard_map/ppermute | solution.py:326
  133.1 4.7 %collective-permute-start.20 = (bf16[4,256,512]{2,1,0:T(8,128)(2,1)}, bf16[4,256,512]{2,1,0:T(8,128)(2,1)}, u32[]{:S(2)}, u32[]{:S(2)}) collective-permute-start(bf16[4,256,512]{2,1,0:T(8,128)(2,1)} %get-tuple-element.36), channel_id=1, source_target_pairs={{0,16},{16,0},{32,48},{48,32},{64,80},{80,64},{96,112},{112,96},{1... | collective-permute-start | bytes 3145736 | tf_op jit(solution)/shard_map/ppermute | solution.py:326
  133.2 12.5 %collective-permute-start.19 = (bf16[512,256]{1,0:T(8,128)(2,1)S(1)}, bf16[512,256]{1,0:T(8,128)(2,1)S(1)}, u32[]{:S(2)}, u32[]{:S(2)}) collective-permute-start(bf16[512,256]{1,0:T(8,128)(2,1)S(1)} %copy-done.6), channel_id=1, source_target_pairs={{0,8},{8,0},{1,9},{9,1},{2,10},{10,2},{3,11},{11,3},{4,12},{12,4},... | collective-permute-start | bytes 786440 | tf_op jit(solution)/shard_map/ppermute | solution.py:334
  136.2 28.8 %collective-permute-start.10 = (bf16[64,4096]{1,0:T(8,128)(2,1)S(1)}, bf16[64,4096]{1,0:T(8,128)(2,1)}, u32[]{:S(2)}, u32[]{:S(2)}) collective-permute-start(bf16[64,4096]{1,0:T(8,128)(2,1)S(1)} %add_convert_fusion.1), channel_id=1, source_target_pairs={{0,15},{1,14},{2,13},{3,12},{4,11},{5,10},{6,9},{7,8},{8,7},{9,6},... | collective-permute-start | bytes 1572872 | tf_op jit(solution)/shard_map/ppermute | solution.py:330
  140.3 26.0 %collective-permute-start.23 = (bf16[256,512]{1,0:T(8,128)(2,1)}, bf16[256,512]{1,0:T(8,128)(2,1)S(1)}, u32[]{:S(2)}, u32[]{:S(2)}) collective-permute-start(bf16[256,512]{1,0:T(8,128)(2,1)} %get-tuple-element.38), channel_id=1, source_target_pairs={{0,96},{16,112},{32,64},{48,80},{64,32},{80,48},{96,0},{112,16},{1... | collective-permute-start | bytes 786440 | tf_op jit(solution)/shard_map/ppermute | solution.py:326
  143.0 23.3 %collective-permute-start.22 = (bf16[256,512]{1,0:T(8,128)(2,1)}, bf16[256,512]{1,0:T(8,128)(2,1)}, u32[]{:S(2)}, u32[]{:S(2)}) collective-permute-start(bf16[256,512]{1,0:T(8,128)(2,1)} %get-tuple-element.39), channel_id=1, source_target_pairs={{0,64},{16,80},{32,96},{48,112},{64,0},{80,16},{96,32},{112,48},{1... | collective-permute-start | bytes 786440 | tf_op jit(solution)/shard_map/ppermute | solution.py:326
  143.8 22.5 %collective-permute-start.21 = (bf16[256,512]{1,0:T(8,128)(2,1)}, bf16[256,512]{1,0:T(8,128)(2,1)}, u32[]{:S(2)}, u32[]{:S(2)}) collective-permute-start(bf16[256,512]{1,0:T(8,128)(2,1)} %get-tuple-element.37), channel_id=1, source_target_pairs={{0,32},{16,48},{32,0},{48,16},{64,96},{80,112},{96,64},{112,80},{1... | collective-permute-start | bytes 786440 | tf_op jit(solution)/shard_map/ppermute | solution.py:326
  159.8 26.1 %all-to-all-start.1 = ((bf16[8,3,128,256]{3,2,1,0:T(8,128)(2,1)}), bf16[8,3,128,256]{3,2,1,0:T(8,128)(2,1)S(1)}, u32[]{:S(2)}, u32[]{:S(2)}) async-start(bf16[8,3,128,256]{3,2,1,0:T(8,128)(2,1)} %attention_bwd.1), calls=%async_computation.1 | async-start | bytes 3145728 | tf_op jit(solution)/shard_map/all_to_all | solution.py:420
  167.5 17.6 %collective-permute-start.24 = (bf16[256,256]{1,0:T(8,128)(2,1)S(1)}, bf16[256,256]{1,0:T(8,128)(2,1)S(1)}, u32[]{:S(2)}, u32[]{:S(2)}) collective-permute-start(bf16[256,256]{1,0:T(8,128)(2,1)S(1)} %select_convert_fusion), channel_id=1, source_target_pairs={{0,8},{8,0},{1,9},{9,1},{2,10},{10,2},{3,11},{11,3},{4,12},{12,4},... | collective-permute-start | bytes 393224 | tf_op jit(solution)/shard_map/ppermute | solution.py:334
  (17 other events, 91.8 us)

commit v3 on v2

--- a/solution.py
+++ b/solution.py
@@ -45,6 +45,40 @@
 ANY = pl.BlockSpec(memory_space=pl.ANY)
 
 
+def gate_kernel(*refs):
+    pass
+
+
+def gate(xs, after):
+    return pl.pallas_call(
+        gate_kernel,
+        in_specs=[ANY] * (len(xs) + len(after)),
+        out_specs=[ANY] * len(xs),
+        out_shape=[struct(*x.shape) for x in xs],
+        input_output_aliases={i: i for i in range(len(xs))},
+        compiler_params=params(),
+        cost_estimate=cost(0, 0),
+        name="gate",
+    )(*xs, *after)
+
+
+def gate_kernel(*refs):
+    pass
+
+
+def gate(xs, after):
+    return pl.pallas_call(
+        gate_kernel,
+        in_specs=[ANY] * (len(xs) + len(after)),
+        out_specs=[ANY] * len(xs),
+        out_shape=[struct(*x.shape) for x in xs],
+        input_output_aliases={i: i for i in range(len(xs))},
+        compiler_params=params(),
+        cost_estimate=cost(0, 0),
+        name="gate",
+    )(*xs, *after)
+
+
 def split_kernel(x_ref, out):
     for g in range(N):
         out[g] = x_ref[:, :, GW * g : GW * (g + 1)]
@@ -79,37 +113,38 @@
     )(blocks)
 
 
-def upstream_kernel(cot, recv, after, out):
+def upstream_kernel(cot, recv, out):
     flipped = dot(flip_matrix(HALF), recv[...], 1, 0)
     out[...] = (cot[...].astype(F32) + flipped).astype(BF16)
 
 
-def upstream_rows(cot, recv, after):
+def upstream_rows(cot, recv):
     return pl.pallas_call(
         upstream_kernel,
         grid=(2,),
-        in_specs=[pl.BlockSpec((HALF, 2048), lambda k: (0, k))] * 2 + [ANY],
+        in_specs=[pl.BlockSpec((HALF, 2048), lambda k: (0, k))] * 2,
         out_specs=pl.BlockSpec((HALF, 2048), lambda k: (0, k)),
         out_shape=struct(HALF, D),
         compiler_params=params(),
-        cost_estimate=cost(2 * 64 * 64 * D, 3 << 19),
+        cost_estimate=cost(2 * 64 * 64 * D, 2 << 20),
         name="upstream_rows",
-    )(cot, recv, after)
-
-
-def fwd_kernel(c_ref, *refs):
-    blocks = refs[:N]
-    after, cat, att_own, att_send, probs_t = refs[N:]
+    )(cot, recv)
+
+
+def fwd_kernel(c_ref, blocks, *refs):
+    cat, att_own, att_send, probs_t = refs[-4:]
     q = pl.program_id(0)
 
     @pl.when(q == 0)
     def _():
         flip = flip_matrix(HALF)
         for j in range(N):
-            cat[1, ROWS * j : ROWS * (j + 1), :] = blocks[j][0, 1]
-            cat[2, ROWS * j : ROWS * (j + 1), :] = blocks[j][0, 2]
-            cat[0, HALF * j : HALF * (j + 1), :] = blocks[j][0, 0, :HALF, :]
-            mirrored = dot(flip, blocks[N - 1 - j][0, 0, HALF:, :], 1, 0).astype(BF16)
+            of = jnp.bitwise_xor(c_ref[0], j)
+            far = jnp.bitwise_xor(c_ref[0], N - 1 - j)
+            cat[1, ROWS * j : ROWS * (j + 1), :] = blocks[of, 1]
+            cat[2, ROWS * j : ROWS * (j + 1), :] = blocks[of, 2]
+            cat[0, HALF * j : HALF * (j + 1), :] = blocks[of, 0, :HALF, :]
+            mirrored = dot(flip, blocks[far, 0, HALF:, :], 1, 0).astype(BF16)
             cat[0, 512 + HALF * j : 512 + HALF * (j + 1), :] = mirrored
 
     for h in range(2):
@@ -140,15 +175,12 @@
 
 
 def attention_fwd(c, blocks, after):
-    def block(j):
-        return pl.BlockSpec((1, 3, ROWS, GW), lambda q, c_ref: (jnp.bitwise_xor(c_ref[0], j), 0, 0, 0))
-
     return pl.pallas_call(
         fwd_kernel,
         grid_spec=pltpu.PrefetchScalarGridSpec(
             num_scalar_prefetch=1,
             grid=(4,),
-            in_specs=[block(j) for j in range(N)] + [ANY],
+            in_specs=[pl.BlockSpec((N, 3, ROWS, GW), lambda q, c_ref: (0, 0, 0, 0))] + [ANY] * len(after),
             out_specs=[
                 pl.BlockSpec((3, SEQ, GW), lambda q, c_ref: (0, 0, 0)),
                 pl.BlockSpec((256, GW), low_half),
@@ -160,36 +192,35 @@
         compiler_params=params(),
         cost_estimate=cost(4 * 4 * SEQ * SEQ * DH, 10 << 20, 2 * SEQ * SEQ),
         name="attention_fwd",
-    )(c, *([blocks] * N), after)
-
-
-def bwd_kernel(c_ref, cat, probs_t, g_own, g_recv, after, after2, out, dq, dk, dv):
+    )(c, blocks, *after)
+
+
+def bwd_kernel(c_ref, cat, probs_t, g_own, g_recv, *refs):
+    out, dq, dk, dv = refs[-4:]
     q = pl.program_id(0)
     rows = pl.ds(pl.multiple_of(q * 256, 256), 256)
-    for h in range(2):
-        cols = slice(DH * h, DH * (h + 1))
-        queries = cat[0, rows, cols]
-        grad = jnp.where(q < 2, g_own[:, cols], g_recv[:, cols])
-        probs_low = probs_t[h]
-        grad_probs = dot(cat[2, :, cols], grad, 1, 1)
-        probs = probs_low.astype(F32)
-        product = probs * grad_probs
-        centre = jnp.sum(product, axis=0, keepdims=True)
-        grad_scores = ((product - probs * centre) * (1.0 / math.sqrt(DH))).astype(BF16)
-        part_v = dot(probs_low, grad, 1, 0)
-        part_k = dot(grad_scores, queries, 1, 0)
-
-        @pl.when(q == 0)
-        def _():
-            dv[:, cols] = part_v
-            dk[:, cols] = part_k
-
-        @pl.when(q > 0)
-        def _():
-            dv[:, cols] += part_v
-            dk[:, cols] += part_k
-
-        dq[rows, cols] = jnp.transpose(dot(cat[1, :, cols], grad_scores, 0, 0)).astype(BF16)
+    queries = cat[0, rows, :]
+    grad = jnp.where(q < 2, g_own[...], g_recv[...])
+    probs_low = probs_t[0]
+    grad_probs = dot(cat[2], grad, 1, 1)
+    probs = probs_low.astype(F32)
+    product = probs * grad_probs
+    centre = jnp.sum(product, axis=0, keepdims=True)
+    grad_scores = ((product - probs * centre) * (1.0 / math.sqrt(DH))).astype(BF16)
+    part_v = dot(probs_low, grad, 1, 0)
+    part_k = dot(grad_scores, queries, 1, 0)
+
+    @pl.when(q == 0)
+    def _():
+        dv[...] = part_v
+        dk[...] = part_k
+
+    @pl.when(q > 0)
+    def _():
+        dv[...] += part_v
+        dk[...] += part_k
+
+    dq[rows, :] = jnp.transpose(dot(cat[1], grad_scores, 0, 0)).astype(BF16)
 
     @pl.when(q == 3)
     def _():
@@ -203,33 +234,34 @@
             out[to, 2] = dv[ROWS * j : ROWS * (j + 1), :].astype(BF16)
 
 
-def attention_bwd(c, cat, probs_t, g_own, g_recv, after, after2):
+def attention_bwd(c, h, cat, probs_t, g_own, g_recv, filled, after):
     return pl.pallas_call(
         bwd_kernel,
         grid_spec=pltpu.PrefetchScalarGridSpec(
             num_scalar_prefetch=1,
             grid=(4,),
             in_specs=[
-                pl.BlockSpec((3, SEQ, GW), lambda q, c_ref: (0, 0, 0)),
-                pl.BlockSpec((2, SEQ, 256), lambda q, c_ref: (0, 0, q)),
-                pl.BlockSpec((256, GW), low_half),
-                pl.BlockSpec((256, GW), high_half),
-                ANY,
-                ANY,
-            ],
-            out_specs=pl.BlockSpec((N, 3, ROWS, GW), lambda q, c_ref: (0, 0, 0, 0)),
-            scratch_shapes=[pltpu.VMEM((SEQ, GW), BF16), pltpu.VMEM((SEQ, GW), F32), pltpu.VMEM((SEQ, GW), F32)],
+                pl.BlockSpec((3, SEQ, DH), lambda q, c_ref: (0, 0, h)),
+                pl.BlockSpec((1, SEQ, 256), lambda q, c_ref: (h, 0, q)),
+                pl.BlockSpec((256, DH), lambda q, c_ref: (jnp.minimum(q, 1), h)),
+                pl.BlockSpec((256, DH), lambda q, c_ref: (jnp.maximum(q - 2, 0), h)),
+            ]
+            + [ANY] * (len(filled) + len(after)),
+            out_specs=pl.BlockSpec((N, 3, ROWS, DH), lambda q, c_ref: (0, 0, 0, h)),
+            scratch_shapes=[pltpu.VMEM((SEQ, DH), BF16), pltpu.VMEM((SEQ, DH), F32), pltpu.VMEM((SEQ, DH), F32)],
         ),
         out_shape=struct(N, 3, ROWS, GW),
-        compiler_params=params(),
-        cost_estimate=cost(8 * 2 * SEQ * SEQ * DH, 8 << 20),
+        input_output_aliases={5 + i: i for i in range(len(filled))},
+        compiler_params=params(),
+        cost_estimate=cost(4 * 2 * SEQ * SEQ * DH, 4 << 20),
         name="attention_bwd",
-    )(c, cat, probs_t, g_own, g_recv, after, after2)
+    )(c, cat, probs_t, g_own, g_recv, *filled, *after)
 
 
 def grad_kernel(*refs):
-    pieces = refs[:9]
-    w, after, out, acc = refs[9:]
+    pieces = refs[:N]
+    w = refs[N]
+    out, acc = refs[-2:]
     k = pl.program_id(0)
     rows = jnp.concatenate([p[...] for p in pieces], axis=0)
     part = dot(rows, w[...], 1, 1)
@@ -252,14 +284,15 @@
         grad_kernel,
         grid=(4,),
         in_specs=[pl.BlockSpec((p.shape[0], 1024), lambda k: (0, k)) for p in pieces]
-        + [pl.BlockSpec((GW, 1024), lambda k: (0, k)), ANY],
+        + [pl.BlockSpec((GW, 1024), lambda k: (0, k))]
+        + [ANY] * len(after),
         out_specs=pl.BlockSpec((512, GW), lambda k: (0, 0)),
         out_shape=struct(512, GW),
         scratch_shapes=[pltpu.VMEM((512, GW), F32)],
         compiler_params=params(),
         cost_estimate=cost(2 * 512 * GW * D, 7 << 20),
         name="grad_attended",
-    )(*pieces, w, after)
+    )(*pieces, w, *after)
 
 
 def project_kernel(own, recv, w, *outs):
@@ -272,7 +305,7 @@
 
 
 def project(own, recv, w):
-    rows = (64, 64, 32, 32, 64, 64, 64, 64, 64)
+    rows = (HALF,) * N
     return pl.pallas_call(
         project_kernel,
         grid=(4,),
@@ -290,8 +323,8 @@
 
 
 def weight_kernel(d_ref, own, recv, *refs):
-    pieces = refs[:9]
-    out_own, out_other = refs[10:]
+    pieces = refs[:N]
+    out_own, out_other = refs[-2:]
     both = (own[...].astype(F32) + recv[...].astype(F32)).astype(BF16)
     rows = jnp.concatenate([p[...] for p in pieces], axis=0)
     part = dot(both, rows, 0, 0).astype(BF16)
@@ -312,14 +345,14 @@
             grid=(4,),
             in_specs=[pl.BlockSpec((512, GW), lambda x, d_ref: (0, 0))] * 2
             + [pl.BlockSpec((p.shape[0], 1024), columns) for p in pieces]
-            + [ANY],
+            + [ANY] * len(after),
             out_specs=[pl.BlockSpec((1, GW, 512), lambda x, d_ref: (x, 0, 0))] * 2,
         ),
         out_shape=[struct(4, GW, 512)] * 2,
         compiler_params=params(),
         cost_estimate=cost(2 * 512 * GW * D, 7 << 20),
         name="weight_part",
-    )(d, own, recv, *pieces, after)
+    )(d, own, recv, *pieces, *after)
 
 
 def by_xor(x, axis, k):
@@ -345,50 +378,39 @@
     return total
 
 
-def relay_kernel(y1, y3, after, low, high):
-    low[...] = y3[:32, :]
-    high[...] = y1[32:, :]
-
-
-def relay(y1, y3, after):
-    return pl.pallas_call(
-        relay_kernel,
-        in_specs=[pl.BlockSpec(memory_space=pltpu.VMEM)] * 2 + [ANY],
-        out_specs=[pl.BlockSpec(memory_space=pltpu.VMEM)] * 2,
-        out_shape=[struct(32, D)] * 2,
-        compiler_params=params(),
-        cost_estimate=cost(0, 3 << 19),
-        name="relay",
-    )(y1, y3, after)
-
-
-def gather_rows(u, after):
-    y1, y3, z = (by_xor(u, "ctx", k) for k in (1, 3, 4))
-    low, high = relay(y1, y3, after)
-    y2a = by_xor(low, "ctx", 1)
-    y2b = by_xor(high, "ctx", 3)
-    zy1 = by_xor(z, "ctx", 1)
-    zy3 = by_xor(z, "ctx", 3)
-    zy2 = by_xor(jnp.concatenate([y2a, y2b], axis=0), "ctx", 4)
-    return [u, y1, y2a, y2b, y3, z, zy1, zy2, zy3]
-
-
-def scatter_rows(parts):
-    p0, p1, p2a, p2b, p3, p4, p5, p6, p7 = parts
-    r5 = by_xor(p5, "ctx", 1)
-    r7 = by_xor(p7, "ctx", 3)
-    r6 = by_xor(p6, "ctx", 4)
-    p2a = add(p2a, r6[:32]).astype(BF16)
-    p2b = add(p2b, r6[32:]).astype(BF16)
-    p4 = add(p4, r5, r7).astype(BF16)
-    r2a = by_xor(p2a, "ctx", 1)
-    r2b = by_xor(p2b, "ctx", 3)
-    r4 = by_xor(p4, "ctx", 4)
-    p3 = add(p3, jnp.pad(r2a, ((0, 32), (0, 0)))).astype(BF16)
-    p1 = add(p1, jnp.pad(r2b, ((32, 0), (0, 0)))).astype(BF16)
-    r3 = by_xor(p3, "ctx", 3)
-    r1 = by_xor(p1, "ctx", 1)
-    return add(p0, r1, r3, r4), p4
+def mix_sum_kernel(p0, r1, r3, r4, out):
+    out[...] = add(p0[...], r1[...], r3[...], r4[...]).astype(BF16)
+
+
+def mix_sum(*terms):
+    return pl.pallas_call(
+        mix_sum_kernel,
+        grid=(2,),
+        in_specs=[pl.BlockSpec((HALF, 2048), lambda k: (0, k))] * 4,
+        out_specs=pl.BlockSpec((HALF, 2048), lambda k: (0, k)),
+        out_shape=struct(HALF, D),
+        compiler_params=params(),
+        cost_estimate=cost(0, 5 << 19),
+        name="mix_sum",
+    )(*terms)
+
+
+def mix_out_kernel(own, recv, out):
+    out[:HALF, :] = own[...]
+    out[HALF:, :] = dot(flip_matrix(HALF), recv[...], 1, 0).astype(BF16)
+
+
+def mix_out(own, recv):
+    return pl.pallas_call(
+        mix_out_kernel,
+        grid=(2,),
+        in_specs=[pl.BlockSpec((HALF, 2048), lambda k: (0, k))] * 2,
+        out_specs=pl.BlockSpec((ROWS, 2048), lambda k: (0, k)),
+        out_shape=struct(ROWS, D),
+        compiler_params=params(),
+        cost_estimate=cost(0, 2 << 20),
+        name="mix_out",
+    )(own, recv)
 
 
 def body(qkv, out_weight, cotangent):
@@ -399,28 +421,38 @@
     cot = cotangent[0, 0]
 
     cot_recv = mirror(cot[HALF:])
-    blocks = lax.all_to_all(split(mine), "ctx", split_axis=0, concat_axis=0, tiled=True)
-
-    upstream = upstream_rows(cot, cot_recv, blocks)
-    cat, att_own, att_send, probs_t = attention_fwd(c, blocks, upstream)
+    (sent,) = gate([split(mine)], [cot_recv])
+    blocks = lax.all_to_all(sent, "ctx", split_axis=0, concat_axis=0, tiled=True)
+
+    u = upstream_rows(cot, cot_recv)
+    y1, y3, z = by_xor(u, "ctx", 1), by_xor(u, "ctx", 3), by_xor(u, "ctx", 4)
+    y2, zy1, zy3 = by_xor(y3, "ctx", 1), by_xor(z, "ctx", 1), by_xor(z, "ctx", 3)
+    cat, att_own, att_send, probs_t = attention_fwd(c, blocks, [y1, y3, z])
+    (att_send,) = gate([att_send], [y2, zy3])
     att_recv = other_strand(att_send)
-    pieces = gather_rows(upstream, att_own)
-
-    partial = project(att_own, att_recv, out_weight)
-    mixed_rows, relayed = scatter_rows(partial)
-    mixed_own = mixed_rows.astype(BF16)
-    mixed_recv = mirror(mixed_own)
-    mixed = jnp.concatenate([mixed_own, flip_rows(mixed_recv).astype(BF16)], axis=0)
-
-    g_own = grad_attended(pieces, out_weight, partial[0])
+    zy2 = by_xor(y2, "ctx", 4)
+    pieces = [u, y1, y2, y3, z, zy1, zy2, zy3]
+
+    p0, p1, p2, p3, p4, p5, p6, p7 = project(att_own, att_recv, out_weight)
+    r5, r7, r6 = by_xor(p5, "ctx", 1), by_xor(p7, "ctx", 3), by_xor(p6, "ctx", 4)
+    g_own = grad_attended(pieces, out_weight, [p0])
     g_recv = other_strand(g_own)
-    w_own, w_other = weight_part(d, att_own, att_recv, pieces, g_own)
-
-    grads = attention_bwd(c, cat, probs_t, g_own, g_recv, w_own, relayed)
+    p4 = add(p4, r5, r7).astype(BF16)
+    p2 = add(p2, r6).astype(BF16)
+    r4, r2 = by_xor(p4, "ctx", 4), by_xor(p2, "ctx", 1)
+    w_own, w_other = weight_part(d, att_own, att_recv, pieces, [g_own, p4, p2])
+    grads = attention_bwd(c, 0, cat, probs_t, g_own, g_recv, [], [w_own])
+    p3 = add(p3, r2).astype(BF16)
+    p3, p1 = gate([p3, p1], [grads])
+    r3, r1 = by_xor(p3, "ctx", 3), by_xor(p1, "ctx", 1)
+    grads = attention_bwd(c, 1, cat, probs_t, g_own, g_recv, [grads], [p3, p1])
+    mixed_own = mix_sum(p0, r1, r3, r4)
     back = lax.all_to_all(grads, "ctx", split_axis=0, concat_axis=0, tiled=True)
+    mixed = mix_out(mixed_own, mirror(mixed_own))
     qkv_grad = jnp.transpose(assemble(back), (1, 0, 2))
 
     w_sum = add(w_own, by_xor(w_other, "dp", 1)).astype(BF16)
+    (w_sum,) = gate([w_sum], [mixed_own])
     w_chip = add(w_sum[0], *[by_xor(w_sum[x], "dp", 2 * x) for x in range(1, 4)])
     first, second = w_chip[:, :GW], w_chip[:, GW:]
     w_keep = jnp.where(s == 0, first, second)

time: 191 us -> 183 us (0.958)
  waiting for transfers between devices: 78.4 us -> 61.1 us
  starting transfers between devices: 40.7 us -> 48.2 us
  Pallas kernels: 51.1 us -> 55.7 us
  other arithmetic: 10.1 us -> 5.57 us
  local copies, waits for them, and re-layouts: 7.32 us -> 9.62 us
    ppermute x2, waiting for transfers between devices: 28.3 us -> 9.26 us  [mirror(): lax.ppermute(x, ('strand', 'ctx'), [(i, 2 * N - 1 - i) for i in range(2 *...]
    ppermute x20 -> x18, waiting for transfers between devices: 24.4 us -> 39.6 us  [by_xor(): return lax.ppermute(x, axis, [(i, i ^ k) for i in range(N)])]
    ppermute x3, waiting for transfers between devices: 25.7 us -> 12.3 us  [other_strand(): return lax.ppermute(x, 'strand', [(0, 1), (1, 0)])]
    convert_element_type x5 -> x3, other arithmetic: 5.54 us -> 1.24 us  [the longest x1 0.92 us: body(): p3 = add(p3, r2).astype(BF16)]
    ppermute x3, starting transfers between devices: 2.27 us -> 6.29 us  [other_strand(): return lax.ppermute(x, 'strand', [(0, 1), (1, 0)])]
    pallas_call x1 -> x6, Pallas kernels: 2.03 us -> 4.62 us  [the longest x1 2.36 us: mix_sum(): pl.pallas_call(mix_sum_kernel, grid=(2,), in_specs=[pl.BlockSpec((HALF, 2...]
    pallas_call x1 -> x2, Pallas kernels: 13.3 us -> 15.8 us  [attention_bwd(): pl.pallas_call(bwd_kernel, grid_spec=pltpu.PrefetchScalarGridSpec(num_sca...]
    ppermute x20 -> x18, starting transfers between devices: 20.7 us -> 23 us  [by_xor(): return lax.ppermute(x, axis, [(i, i ^ k) for i in range(N)])]
  transfers between devices with their start and end apart: 27 -> 25, of which waited for: 8 -> 10; matrix products, arithmetic and copies ran while one was open for 7% -> 4% of each run, Pallas kernels for 16% -> 29%
where the time goes in v3:
time: 183 us; the launch traced here: 181 us
  waiting for transfers between devices  61.1 us (33%)
  Pallas kernels  55.7 us (30%)
  starting transfers between devices  48.2 us (26%)
  local copies, waits for them, and re-layouts  9.62 us (5%)
  other arithmetic  5.57 us (3%)
    ppermute x18, waiting for transfers between devices, by_xor(): return lax.ppermute(x, axis, [(i, i ^ k) for i in range(N)])  39.6 us
    ppermute x18, starting transfers between devices, by_xor(): return lax.ppermute(x, axis, [(i, i ^ k) for i in range(N)])  23 us
    pallas_call x2, Pallas kernels, attention_bwd(): pl.pallas_call(bwd_kernel, grid_spec=pltpu.PrefetchScalarGridSpec(num_sca...  15.8 us
    ppermute x3, waiting for transfers between devices, other_strand(): return lax.ppermute(x, 'strand', [(0, 1), (1, 0)])  12.3 us
    pallas_call x1, Pallas kernels, attention_fwd(): pl.pallas_call(fwd_kernel, grid_spec=pltpu.PrefetchScalarGridSpec(num_sca...  12 us
    ppermute x2, waiting for transfers between devices, mirror(): lax.ppermute(x, ('strand', 'ctx'), [(i, 2 * N - 1 - i) for i in range(2 *...  9.26 us
    ppermute x2, starting transfers between devices, mirror(): lax.ppermute(x, ('strand', 'ctx'), [(i, 2 * N - 1 - i) for i in range(2 *...  7.51 us
    unnamed x36, local copies, waits for them, and re-layouts  6.62 us
  transfers between devices with their start and end apart: 25, of which 10 were waited for; matrix products, arithmetic and copies ran while one was open for 4% of the time, Pallas kernels for 29%

profile of v3, /device:TPU:8, one launch (start us, length us, event | category | flops | bytes accessed | tf_op | source)
XLA Modules:
  0.0 180.9 jit_solution(7701246361108570464)
XLA Ops:
  1.7 5.1 %collective-permute-start = (bf16[64,4096]{1,0:T(8,128)(2,1)S(1)}, bf16[64,4096]{1,0:T(8,128)(2,1)S(1)}, u32[]{:S(2)}, u32[]{:S(2)}) collective-permute-start(bf16[64,4096]{1,0:T(8,128)(2,1)S(1)} %slice_bitcast_fusion), channel_id=1, source_target_pairs={{0,15},{1,14},{2,13},{3,12},{4,11},{5,10},{6,9},{7,8},{8,7},{9,6},... | collective-permute-start | bytes 1572872 | tf_op jit(solution)/shard_map/ppermute | solution.py:363
  6.8 2.7 %split.1.refs_0_ = bf16[8,3,128,256]{3,2,1,0:T(8,128)(2,1)} custom-call(bf16[3,128,2048]{2,1,0:T(8,128)(2,1)} %bitcast.24), custom_call_target="tpu_custom_call" | custom-call | bytes 3145728 | tf_op jit(solution)/shard_map/split/pallas_call | solution.py:88
  9.5 9.3 %collective-permute-done.refs_1_.recv = bf16[64,4096]{1,0:T(8,128)(2,1)S(1)} collective-permute-done((bf16[64,4096]{1,0:T(8,128)(2,1)S(1)}, bf16[64,4096]{1,0:T(8,128)(2,1)S(1)}, u32[]{:S(2)}, u32[]{:S(2)}) %collective-permute-start) | collective-permute-done | bytes 524320 | tf_op jit(solution)/shard_map/ppermute | solution.py:363
  19.6 6.1 %all-to-all-start = ((bf16[8,3,128,256]{3,2,1,0:T(8,128)(2,1)}), bf16[8,3,128,256]{3,2,1,0:T(8,128)(2,1)}, u32[]{:S(2)}, u32[]{:S(2)}) async-start(bf16[8,3,128,256]{3,2,1,0:T(8,128)(2,1)} %gate.4), calls=%async_computation | async-start | bytes 3145728 | tf_op jit(solution)/shard_map/all_to_all | solution.py:425
  25.6 2.2 %upstream_rows.1.refs_0_ = bf16[64,4096]{1,0:T(8,128)(2,1)} custom-call(bf16[128,4096]{1,0:T(8,128)(2,1)} %bitcast.23, bf16[64,4096]{1,0:T(8,128)(2,1)} %copy-done.11), custom_call_target="tpu_custom_call" | custom-call | flops 33554432 | bytes 2097152 | tf_op jit(solution)/shard_map/upstream_rows/pallas_call | solution.py:122
  30.8 1.8 collective-permute-start.1
  32.5 22.7 %collective-permute-done.2.refs_1_.refs_3_ = bf16[64,4096]{1,0:T(8,128)(2,1)S(1)} collective-permute-done((bf16[64,4096]{1,0:T(8,128)(2,1)}, bf16[64,4096]{1,0:T(8,128)(2,1)S(1)}, u32[]{:S(2)}, u32[]{:S(2)}) %collective-permute-start.2) | collective-permute-done | bytes 524320 | tf_op jit(solution)/shard_map/ppermute | solution.py:359
  55.2 1.8 %collective-permute-start.4 = (bf16[64,4096]{1,0:T(8,128)(2,1)S(1)}, bf16[64,4096]{1,0:T(8,128)(2,1)S(1)}, u32[]{:S(2)}, u32[]{:S(2)}) collective-permute-start(bf16[64,4096]{1,0:T(8,128)(2,1)S(1)} %collective-permute-done.2.refs_1_.refs_3_), channel_id=1, source_target_pairs={{0,1},{1,0},{2,3},{3,2},{4,5},{5,4},{6,7},{7,6},{8,9},{9,8},{10,11... | collective-permute-start | bytes 1572872 | tf_op jit(solution)/shard_map/ppermute | solution.py:359
  57.9 12.0 %attention_fwd.1 = (bf16[3,1024,256]{2,1,0:T(8,128)(2,1)}, bf16[512,256]{1,0:T(8,128)(2,1)}, bf16[512,256]{1,0:T(8,128)(2,1)}, bf16[2,1024,1024]{2,1,0:T(8,128)(2,1)}) custom-call(s32[1]{0:T(128)} %bitcast.c_ref, bf16[8,3,128,256]{3,2,1,0:T(8,128)(2,1)} %all-to-all-done.blocks, bf16[64,4096]{1,0:T(8,128)(2,1)} %copy-done.6, bf16[64,4096]{1,0:T(8,128)(2,1)} %copy-done.5, ...), custom_call_target="tpu_custom_call" | custom-call | flops 2147483648 | bytes 10485760 | tf_op jit(solution)/shard_map/attention_fwd/pallas_call | solution.py:178
  71.3 3.0 %collective-permute-start.6 = (bf16[512,256]{1,0:T(8,128)(2,1)}, bf16[512,256]{1,0:T(8,128)(2,1)S(1)}, u32[]{:S(2)}, u32[]{:S(2)}) collective-permute-start(bf16[512,256]{1,0:T(8,128)(2,1)} %gate.5), channel_id=1, source_target_pairs={{0,8},{8,0},{1,9},{9,1},{2,10},{10,2},{3,11},{11,3},{4,12},{12,4},... | collective-permute-start | bytes 786440 | tf_op jit(solution)/shard_map/ppermute | solution.py:367
  76.8 5.5 %collective-permute-done.6.recv = bf16[512,256]{1,0:T(8,128)(2,1)S(1)} collective-permute-done((bf16[512,256]{1,0:T(8,128)(2,1)}, bf16[512,256]{1,0:T(8,128)(2,1)S(1)}, u32[]{:S(2)}, u32[]{:S(2)}) %collective-permute-start.6) | collective-permute-done | bytes 262176 | tf_op jit(solution)/shard_map/ppermute | solution.py:367
  83.0 4.9 %project.1 = (bf16[64,4096]{1,0:T(8,128)(2,1)}, bf16[64,4096]{1,0:T(8,128)(2,1)}, bf16[64,4096]{1,0:T(8,128)(2,1)}, bf16[64,4096]{1,0:T(8,128)(2,1)}, bf16[64,40...) custom-call(bf16[512,256]{1,0:T(8,128)(2,1)} %get-tuple-element.19.own, ...), custom_call_target="tpu_custom_call" | custom-call | flops 1073741824 | bytes 7340032 | tf_op jit(solution)/shard_map/project/pallas_call | solution.py:309
  92.2 1.6 collective-permute-done.10.refs_6_
  94.7 5.4 %grad_attended.1.refs_8_.g_own = bf16[512,256]{1,0:T(8,128)(2,1)} custom-call(bf16[64,4096]{1,0:T(8,128)(2,1)} %upstream_rows.1.refs_0_, bf16[64,4096]{1,0:T(8,128)(2,1)} %copy-done.6, bf16[64,4096]{1,0:T(8,128)(2,1)} %copy-done.1, bf16[64,4096]{1,0:T(8,128)(2,1)} %copy-done.5, bf16[64,4096]{1,0:T(8,128)(2,1)} %collective-permute-done.3.refs_2_.refs_4_, ...), custom_call_target="tpu_custom_call" | custom-call | flops 1073741824 | bytes 7340032 | tf_op jit(solution)/shard_map/grad_attended/pallas_call | solution.py:283
  100.0 1.8 collective-permute-start.11
  101.8 3.3 %collective-permute-done.7 = bf16[64,4096]{1,0:T(8,128)(2,1)S(1)} collective-permute-done((bf16[64,4096]{1,0:T(8,128)(2,1)}, bf16[64,4096]{1,0:T(8,128)(2,1)S(1)}, u32[]{:S(2)}, u32[]{:S(2)}) %collective-permute-start.7) | collective-permute-done | bytes 524320 | tf_op jit(solution)/shard_map/ppermute | solution.py:359
  105.2 1.7 collective-permute-start.8
  108.4 5.5 %weight_part.1 = (bf16[4,256,512]{2,1,0:T(8,128)(2,1)}, bf16[4,256,512]{2,1,0:T(8,128)(2,1)}) custom-call(s32[1]{0:T(128)} %bitcast.5.d_ref, bf16[512,256]{1,0:T(8,128)(2,1)} %get-tuple-element.19.own, bf16[512,256]{1,0:T(8,128)(2,1)} %copy-done.17, bf16[64,4096]{1,0:T(8,128)(2,1)} %upstream_rows.1.refs_0_, bf16[64,4096]{1,0:T(8,128)(2,1)} %copy-done.6, ...), custom_call_target="tpu_custom_call" | custom-call | flops 1073741824 | bytes 7340032 | tf_op jit(solution)/shard_map/weight_part/pallas_call | solution.py:341
  114.6 7.9 %attention_bwd.2.refs_2_.refs_0_ = bf16[8,3,128,256]{3,2,1,0:T(8,128)(2,1)} custom-call(s32[1]{0:T(128)} %bitcast.c_ref, bf16[3,1024,256]{2,1,0:T(8,128)(2,1)} %get-tuple-element.26.cat, bf16[2,1024,1024]{2,1,0:T(8,128)(2,1)} %get-tuple-element.27.probs_t, bf16[512,256]{1,0:T(8,128)(2,1)} %grad_attended.1.refs_8_.g_own, bf16[512,256]{1,0:T(8,128)(2,1)} %copy-done.12, ...), custom_call_target="tpu_custom_call" | custom-call | flops 1073741824 | bytes 4194304 | tf_op jit(solution)/shard_map/attention_bwd/pallas_call | solution.py:238
  125.4 7.9 %attention_bwd.3 = bf16[8,3,128,256]{3,2,1,0:T(8,128)(2,1)} custom-call(s32[1]{0:T(128)} %bitcast.c_ref, bf16[3,1024,256]{2,1,0:T(8,128)(2,1)} %get-tuple-element.26.cat, bf16[2,1024,1024]{2,1,0:T(8,128)(2,1)} %get-tuple-element.27.probs_t, bf16[512,256]{1,0:T(8,128)(2,1)} %grad_attended.1.refs_8_.g_own, ...), custom_call_target="tpu_custom_call", output_to_operand_aliasing={{}: (5, {})} | custom-call | flops 1073741824 | bytes 4194304 | tf_op jit(solution)/shard_map/attention_bwd/pallas_call | solution.py:238
  133.3 5.4 %all-to-all-start.1 = ((bf16[8,3,128,256]{3,2,1,0:T(8,128)(2,1)}), bf16[8,3,128,256]{3,2,1,0:T(8,128)(2,1)S(1)}, u32[]{:S(2)}, u32[]{:S(2)}) async-start(bf16[8,3,128,256]{3,2,1,0:T(8,128)(2,1)} %attention_bwd.3), calls=%async_computation.1 | async-start | bytes 3145728 | tf_op jit(solution)/shard_map/all_to_all | solution.py:450
  138.7 2.5 %add_convert_fusion.refs_0_ = bf16[4,256,512]{2,1,0:T(8,128)(2,1)} fusion(bf16[4,256,512]{2,1,0:T(8,128)(2,1)} %collective-permute-done.18, bf16[4,256,512]{2,1,0:T(8,128)(2,1)S(1)} %copy-done.4), kind=kLoop, calls=%fused_computation | loop fusion | flops 2097152 | bytes 3145728 | tf_op jit(solution)/shard_map/convert_element_type | solution.py:454
  141.2 2.4 %mix_sum.1.own.refs_1_ = bf16[64,4096]{1,0:T(8,128)(2,1)} custom-call(bf16[64,4096]{1,0:T(8,128)(2,1)} %get-tuple-element.21.refs_9_.p0, bf16[64,4096]{1,0:T(8,128)(2,1)} %collective-permute-done.14.r1, bf16[64,4096]{1,0:T(8,128)(2,1)} %collective-permute-done.15.r3, bf16[64,4096]{1,0:T(8,128)(2,1)} %collective-permute-done.16.r4), custom_call_target="tpu_custom_call" | custom-call | bytes 2621440 | tf_op jit(solution)/shard_map/mix_sum/pallas_call | solution.py:386
  143.5 1.9 %slice_bitcast_fusion.3 = (bf16[256,512]{1,0:T(8,128)(2,1)}, bf16[256,512]{1,0:T(8,128)(2,1)S(1)}, bf16[256,512]{1,0:T(8,128)(2,1)S(1)}) fusion(bf16[4,256,512]{2,1,0:T(8,128)(2,1)} %gate.7), kind=kLoop, calls=%fused_computation.10 | loop fusion | bytes 1572864 | tf_op jit(solution)/shard_map/squeeze | solution.py:456
  146.9 2.7 %collective-permute-start.20 = (bf16[256,512]{1,0:T(8,128)(2,1)S(1)}, bf16[256,512]{1,0:T(8,128)(2,1)S(1)}, u32[]{:S(2)}, u32[]{:S(2)}) collective-permute-start(bf16[256,512]{1,0:T(8,128)(2,1)S(1)} %get-tuple-element.37), channel_id=1, source_target_pairs={{0,64},{16,80},{32,96},{48,112},{64,0},{80,16},{96,32},{112,48},{1... | collective-permute-start | bytes 786440 | tf_op jit(solution)/shard_map/ppermute | solution.py:359
  150.2 2.4 %collective-permute-start.17 = (bf16[64,4096]{1,0:T(8,128)(2,1)S(1)}, bf16[64,4096]{1,0:T(8,128)(2,1)S(1)}, u32[]{:S(2)}, u32[]{:S(2)}) collective-permute-start(bf16[64,4096]{1,0:T(8,128)(2,1)S(1)} %copy-done.3), channel_id=1, source_target_pairs={{0,15},{1,14},{2,13},{3,12},{4,11},{5,10},{6,9},{7,8},{8,7},{9,6},... | collective-permute-start | bytes 1572872 | tf_op jit(solution)/shard_map/ppermute | solution.py:363
  152.5 2.4 %collective-permute-done.19 = bf16[256,512]{1,0:T(8,128)(2,1)S(1)} collective-permute-done((bf16[256,512]{1,0:T(8,128)(2,1)}, bf16[256,512]{1,0:T(8,128)(2,1)S(1)}, u32[]{:S(2)}, u32[]{:S(2)}) %collective-permute-start.19) | collective-permute-done | bytes 262176 | tf_op jit(solution)/shard_map/ppermute | solution.py:359
  154.9 6.6 %collective-permute-done.20 = bf16[256,512]{1,0:T(8,128)(2,1)S(1)} collective-permute-done((bf16[256,512]{1,0:T(8,128)(2,1)S(1)}, bf16[256,512]{1,0:T(8,128)(2,1)S(1)}, u32[]{:S(2)}, u32[]{:S(2)}) %collective-permute-start.20) | collective-permute-done | bytes 262176 | tf_op jit(solution)/shard_map/ppermute | solution.py:359
  161.4 2.4 %collective-permute-done.21 = bf16[256,512]{1,0:T(8,128)(2,1)S(1)} collective-permute-done((bf16[256,512]{1,0:T(8,128)(2,1)S(1)}, bf16[256,512]{1,0:T(8,128)(2,1)S(1)}, u32[]{:S(2)}, u32[]{:S(2)}) %collective-permute-start.21) | collective-permute-done | bytes 262176 | tf_op jit(solution)/shard_map/ppermute | solution.py:359
  166.4 6.7 %collective-permute-done.22 = bf16[256,256]{1,0:T(8,128)(2,1)S(1)} collective-permute-done((bf16[256,256]{1,0:T(8,128)(2,1)S(1)}, bf16[256,256]{1,0:T(8,128)(2,1)S(1)}, u32[]{:S(2)}, u32[]{:S(2)}) %collective-permute-start.22) | collective-permute-done | bytes 131104 | tf_op jit(solution)/shard_map/ppermute | solution.py:367
  174.7 2.3 %mix_out.1 = bf16[128,4096]{1,0:T(8,128)(2,1)} custom-call(bf16[64,4096]{1,0:T(8,128)(2,1)} %mix_sum.1.own.refs_1_, bf16[64,4096]{1,0:T(8,128)(2,1)} %copy-done.16), custom_call_target="tpu_custom_call" | custom-call | bytes 2097152 | tf_op jit(solution)/shard_map/mix_out/pallas_call | solution.py:404
  178.2 2.8 %assemble.1 = bf16[3,128,2048]{2,1,0:T(8,128)(2,1)} custom-call(bf16[8,3,128,256]{3,2,1,0:T(8,128)(2,1)} %copy-done), custom_call_target="tpu_custom_call" | custom-call | bytes 3145728 | tf_op jit(solution)/shard_map/assemble/pallas_call | solution.py:105
  (78 shorter events, 28.0 us)
Async XLA Ops:
  1.7 17.1 %collective-permute-start = (bf16[64,4096]{1,0:T(8,128)(2,1)S(1)}, bf16[64,4096]{1,0:T(8,128)(2,1)S(1)}, u32[]{:S(2)}, u32[]{:S(2)}) collective-permute-start(bf16[64,4096]{1,0:T(8,128)(2,1)S(1)} %slice_bitcast_fusion), channel_id=1, source_target_pairs={{0,15},{1,14},{2,13},{3,12},{4,11},{5,10},{6,9},{7,8},{8,7},{9,6},... | collective-permute-start | bytes 1572872 | tf_op jit(solution)/shard_map/ppermute | solution.py:363
  19.6 37.5 %all-to-all-start = ((bf16[8,3,128,256]{3,2,1,0:T(8,128)(2,1)}), bf16[8,3,128,256]{3,2,1,0:T(8,128)(2,1)}, u32[]{:S(2)}, u32[]{:S(2)}) async-start(bf16[8,3,128,256]{3,2,1,0:T(8,128)(2,1)} %gate.4), calls=%async_computation | async-start | bytes 3145728 | tf_op jit(solution)/shard_map/all_to_all | solution.py:425
  27.8 27.4 %collective-permute-start.2 = (bf16[64,4096]{1,0:T(8,128)(2,1)}, bf16[64,4096]{1,0:T(8,128)(2,1)S(1)}, u32[]{:S(2)}, u32[]{:S(2)}) collective-permute-start(bf16[64,4096]{1,0:T(8,128)(2,1)} %upstream_rows.1.refs_0_), channel_id=1, source_target_pairs={{0,3},{1,2},{2,1},{3,0},{4,7},{5,6},{6,5},{7,4},{8,11},{9,10},{10,... | collective-permute-start | bytes 1572872 | tf_op jit(solution)/shard_map/ppermute | solution.py:359
  29.3 27.8 %collective-permute-start.3 = (bf16[64,4096]{1,0:T(8,128)(2,1)}, bf16[64,4096]{1,0:T(8,128)(2,1)}, u32[]{:S(2)}, u32[]{:S(2)}) collective-permute-start(bf16[64,4096]{1,0:T(8,128)(2,1)} %upstream_rows.1.refs_0_), channel_id=1, source_target_pairs={{0,4},{1,5},{2,6},{3,7},{4,0},{5,1},{6,2},{7,3},{8,12},{9,13},{10,... | collective-permute-start | bytes 1572872 | tf_op jit(solution)/shard_map/ppermute | solution.py:359
  30.8 26.3 %collective-permute-start.1 = (bf16[64,4096]{1,0:T(8,128)(2,1)}, bf16[64,4096]{1,0:T(8,128)(2,1)S(1)}, u32[]{:S(2)}, u32[]{:S(2)}) collective-permute-start(bf16[64,4096]{1,0:T(8,128)(2,1)} %upstream_rows.1.refs_0_), channel_id=1, source_target_pairs={{0,1},{1,0},{2,3},{3,2},{4,5},{5,4},{6,7},{7,6},{8,9},{9,8},{10,11... | collective-permute-start | bytes 1572872 | tf_op jit(solution)/shard_map/ppermute | solution.py:359
  55.2 1.9 %copy-start.5 = (bf16[64,4096]{1,0:T(8,128)(2,1)}, bf16[64,4096]{1,0:T(8,128)(2,1)S(1)}, u32[]{:S(2)}) copy-start(bf16[64,4096]{1,0:T(8,128)(2,1)S(1)} %collective-permute-done.2.refs_1_.refs_3_) | copy-start | bytes 1572868
  55.2 14.6 %collective-permute-start.4 = (bf16[64,4096]{1,0:T(8,128)(2,1)S(1)}, bf16[64,4096]{1,0:T(8,128)(2,1)S(1)}, u32[]{:S(2)}, u32[]{:S(2)}) collective-permute-start(bf16[64,4096]{1,0:T(8,128)(2,1)S(1)} %collective-permute-done.2.refs_1_.refs_3_), channel_id=1, source_target_pairs={{0,1},{1,0},{2,3},{3,2},{4,5},{5,4},{6,7},{7,6},{8,9},{9,8},{10,11... | collective-permute-start | bytes 1572872 | tf_op jit(solution)/shard_map/ppermute | solution.py:359
  57.1 13.4 %collective-permute-start.5 = (bf16[64,4096]{1,0:T(8,128)(2,1)}, bf16[64,4096]{1,0:T(8,128)(2,1)S(1)}, u32[]{:S(2)}, u32[]{:S(2)}) collective-permute-start(bf16[64,4096]{1,0:T(8,128)(2,1)} %collective-permute-done.3.refs_2_.refs_4_), channel_id=1, source_target_pairs={{0,3},{1,2},{2,1},{3,0},{4,7},{5,6},{6,5},{7,4},{8,11},{9,10},{10,... | collective-permute-start | bytes 1572872 | tf_op jit(solution)/shard_map/ppermute | solution.py:359
  71.3 11.0 %collective-permute-start.6 = (bf16[512,256]{1,0:T(8,128)(2,1)}, bf16[512,256]{1,0:T(8,128)(2,1)S(1)}, u32[]{:S(2)}, u32[]{:S(2)}) collective-permute-start(bf16[512,256]{1,0:T(8,128)(2,1)} %gate.5), channel_id=1, source_target_pairs={{0,8},{8,0},{1,9},{9,1},{2,10},{10,2},{3,11},{11,3},{4,12},{12,4},... | collective-permute-start | bytes 786440 | tf_op jit(solution)/shard_map/ppermute | solution.py:367
  74.3 17.9 %collective-permute-start.9 = (bf16[64,4096]{1,0:T(8,128)(2,1)}, bf16[64,4096]{1,0:T(8,128)(2,1)S(1)}, u32[]{:S(2)}, u32[]{:S(2)}) collective-permute-start(bf16[64,4096]{1,0:T(8,128)(2,1)} %collective-permute-done.3.refs_2_.refs_4_), channel_id=1, source_target_pairs={{0,1},{1,0},{2,3},{3,2},{4,5},{5,4},{6,7},{7,6},{8,9},{9,8},{10,11... | collective-permute-start | bytes 1572872 | tf_op jit(solution)/shard_map/ppermute | solution.py:359
  75.9 17.9 %collective-permute-start.10 = (bf16[64,4096]{1,0:T(8,128)(2,1)}, bf16[64,4096]{1,0:T(8,128)(2,1)S(1)}, u32[]{:S(2)}, u32[]{:S(2)}) collective-permute-start(bf16[64,4096]{1,0:T(8,128)(2,1)} %copy-done.1), channel_id=1, source_target_pairs={{0,4},{1,5},{2,6},{3,7},{4,0},{5,1},{6,2},{7,3},{8,12},{9,13},{10,... | collective-permute-start | bytes 1572872 | tf_op jit(solution)/shard_map/ppermute | solution.py:359
  87.9 17.2 %collective-permute-start.7 = (bf16[64,4096]{1,0:T(8,128)(2,1)}, bf16[64,4096]{1,0:T(8,128)(2,1)S(1)}, u32[]{:S(2)}, u32[]{:S(2)}) collective-permute-start(bf16[64,4096]{1,0:T(8,128)(2,1)} %get-tuple-element.24), channel_id=1, source_target_pairs={{0,4},{1,5},{2,6},{3,7},{4,0},{5,1},{6,2},{7,3},{8,12},{9,13},{10,... | collective-permute-start | bytes 1572872 | tf_op jit(solution)/shard_map/ppermute | solution.py:359
  89.4 17.4 %collective-permute-start.12 = (bf16[64,4096]{1,0:T(8,128)(2,1)}, bf16[64,4096]{1,0:T(8,128)(2,1)S(1)}, u32[]{:S(2)}, u32[]{:S(2)}) collective-permute-start(bf16[64,4096]{1,0:T(8,128)(2,1)} %get-tuple-element.29), channel_id=1, source_target_pairs={{0,1},{1,0},{2,3},{3,2},{4,5},{5,4},{6,7},{7,6},{8,9},{9,8},{10,11... | collective-permute-start | bytes 1572872 | tf_op jit(solution)/shard_map/ppermute | solution.py:359
  91.0 15.9 %collective-permute-start.13 = (bf16[64,4096]{1,0:T(8,128)(2,1)}, bf16[64,4096]{1,0:T(8,128)(2,1)S(1)}, u32[]{:S(2)}, u32[]{:S(2)}) collective-permute-start(bf16[64,4096]{1,0:T(8,128)(2,1)} %get-tuple-element.30), channel_id=1, source_target_pairs={{0,3},{1,2},{2,1},{3,0},{4,7},{5,6},{6,5},{7,4},{8,11},{9,10},{10,... | collective-permute-start | bytes 1572872 | tf_op jit(solution)/shard_map/ppermute | solution.py:359
  94.7 10.4 %copy-start.14 = (bf16[64,4096]{1,0:T(8,128)(2,1)S(1)}, bf16[64,4096]{1,0:T(8,128)(2,1)}, u32[]{:S(2)}) copy-start(bf16[64,4096]{1,0:T(8,128)(2,1)} %get-tuple-element.23) | copy-start | bytes 1572868
  100.0 6.9 %copy-start.15 = (bf16[64,4096]{1,0:T(8,128)(2,1)S(1)}, bf16[64,4096]{1,0:T(8,128)(2,1)}, u32[]{:S(2)}) copy-start(bf16[64,4096]{1,0:T(8,128)(2,1)} %get-tuple-element.28) | copy-start | bytes 1572868
  100.0 13.9 %collective-permute-start.11 = (bf16[512,256]{1,0:T(8,128)(2,1)}, bf16[512,256]{1,0:T(8,128)(2,1)S(1)}, u32[]{:S(2)}, u32[]{:S(2)}) collective-permute-start(bf16[512,256]{1,0:T(8,128)(2,1)} %grad_attended.1.refs_8_.g_own), channel_id=1, source_target_pairs={{0,8},{8,0},{1,9},{9,1},{2,10},{10,2},{3,11},{11,3},{4,12},{12,4},... | collective-permute-start | bytes 786440 | tf_op jit(solution)/shard_map/ppermute | solution.py:367
  105.2 3.1 %copy-start.9 = (bf16[64,4096]{1,0:T(8,128)(2,1)}, bf16[64,4096]{1,0:T(8,128)(2,1)S(1)}, u32[]{:S(2)}) copy-start(bf16[64,4096]{1,0:T(8,128)(2,1)S(1)} %add_convert_fusion.3.refs_10_) | copy-start | bytes 1572868
  105.2 17.3 %collective-permute-start.8 = (bf16[64,4096]{1,0:T(8,128)(2,1)S(1)}, bf16[64,4096]{1,0:T(8,128)(2,1)S(1)}, u32[]{:S(2)}, u32[]{:S(2)}) collective-permute-start(bf16[64,4096]{1,0:T(8,128)(2,1)S(1)} %add_convert_fusion.3.refs_10_), channel_id=1, source_target_pairs={{0,1},{1,0},{2,3},{3,2},{4,5},{5,4},{6,7},{7,6},{8,9},{9,8},{10,11... | collective-permute-start | bytes 1572872 | tf_op jit(solution)/shard_map/ppermute | solution.py:359
  107.1 34.1 %collective-permute-start.16 = (bf16[64,4096]{1,0:T(8,128)(2,1)S(1)}, bf16[64,4096]{1,0:T(8,128)(2,1)}, u32[]{:S(2)}, u32[]{:S(2)}) collective-permute-start(bf16[64,4096]{1,0:T(8,128)(2,1)S(1)} %add_convert_fusion.1.refs_9_), channel_id=1, source_target_pairs={{0,4},{1,5},{2,6},{3,7},{4,0},{5,1},{6,2},{7,3},{8,12},{9,13},{10,... | collective-permute-start | bytes 1572872 | tf_op jit(solution)/shard_map/ppermute | solution.py:359
  113.8 24.9 %collective-permute-start.18 = (bf16[4,256,512]{2,1,0:T(8,128)(2,1)}, bf16[4,256,512]{2,1,0:T(8,128)(2,1)}, u32[]{:S(2)}, u32[]{:S(2)}) collective-permute-start(bf16[4,256,512]{2,1,0:T(8,128)(2,1)} %get-tuple-element.34), channel_id=1, source_target_pairs={{0,16},{16,0},{32,48},{48,32},{64,80},{80,64},{96,112},{112,96},{1... | collective-permute-start | bytes 3145736 | tf_op jit(solution)/shard_map/ppermute | solution.py:359
  114.6 7.9 %copy-start.13 = (bf16[64,4096]{1,0:T(8,128)(2,1)S(1)}, bf16[64,4096]{1,0:T(8,128)(2,1)}, u32[]{:S(2)}) copy-start(bf16[64,4096]{1,0:T(8,128)(2,1)} %get-tuple-element.22) | copy-start | bytes 1572868
  123.5 17.7 %collective-permute-start.14 = (bf16[64,4096]{1,0:T(8,128)(2,1)}, bf16[64,4096]{1,0:T(8,128)(2,1)}, u32[]{:S(2)}, u32[]{:S(2)}) collective-permute-start(bf16[64,4096]{1,0:T(8,128)(2,1)} %get-tuple-element.32.refs_2_), channel_id=1, source_target_pairs={{0,1},{1,0},{2,3},{3,2},{4,5},{5,4},{6,7},{7,6},{8,9},{9,8},{10,11... | collective-permute-start | bytes 1572872 | tf_op jit(solution)/shard_map/ppermute | solution.py:359
  123.9 17.3 %collective-permute-start.15 = (bf16[64,4096]{1,0:T(8,128)(2,1)}, bf16[64,4096]{1,0:T(8,128)(2,1)}, u32[]{:S(2)}, u32[]{:S(2)}) collective-permute-start(bf16[64,4096]{1,0:T(8,128)(2,1)} %get-tuple-element.33.refs_1_), channel_id=1, source_target_pairs={{0,3},{1,2},{2,1},{3,0},{4,7},{5,6},{6,5},{7,4},{8,11},{9,10},{10,... | collective-permute-start | bytes 1572872 | tf_op jit(solution)/shard_map/ppermute | solution.py:359
  133.3 5.4 %copy-start.4 = (bf16[4,256,512]{2,1,0:T(8,128)(2,1)S(1)}, bf16[4,256,512]{2,1,0:T(8,128)(2,1)}, u32[]{:S(2)}) copy-start(bf16[4,256,512]{2,1,0:T(8,128)(2,1)} %get-tuple-element.31.refs_0_) | copy-start | bytes 3145732
  133.3 43.7 %all-to-all-start.1 = ((bf16[8,3,128,256]{3,2,1,0:T(8,128)(2,1)}), bf16[8,3,128,256]{3,2,1,0:T(8,128)(2,1)S(1)}, u32[]{:S(2)}, u32[]{:S(2)}) async-start(bf16[8,3,128,256]{3,2,1,0:T(8,128)(2,1)} %attention_bwd.3), calls=%async_computation.1 | async-start | bytes 3145728 | tf_op jit(solution)/shard_map/all_to_all | solution.py:450
  143.5 6.6 %copy-start.3 = (bf16[64,4096]{1,0:T(8,128)(2,1)S(1)}, bf16[64,4096]{1,0:T(8,128)(2,1)}, u32[]{:S(2)}) copy-start(bf16[64,4096]{1,0:T(8,128)(2,1)} %mix_sum.1.own.refs_1_) | copy-start | bytes 1572868
  145.5 9.4 %collective-permute-start.19 = (bf16[256,512]{1,0:T(8,128)(2,1)}, bf16[256,512]{1,0:T(8,128)(2,1)S(1)}, u32[]{:S(2)}, u32[]{:S(2)}) collective-permute-start(bf16[256,512]{1,0:T(8,128)(2,1)} %get-tuple-element.35), channel_id=1, source_target_pairs={{0,32},{16,48},{32,0},{48,16},{64,96},{80,112},{96,64},{112,80},{1... | collective-permute-start | bytes 786440 | tf_op jit(solution)/shard_map/ppermute | solution.py:359
  146.9 14.5 %collective-permute-start.20 = (bf16[256,512]{1,0:T(8,128)(2,1)S(1)}, bf16[256,512]{1,0:T(8,128)(2,1)S(1)}, u32[]{:S(2)}, u32[]{:S(2)}) collective-permute-start(bf16[256,512]{1,0:T(8,128)(2,1)S(1)} %get-tuple-element.37), channel_id=1, source_target_pairs={{0,64},{16,80},{32,96},{48,112},{64,0},{80,16},{96,32},{112,48},{1... | collective-permute-start | bytes 786440 | tf_op jit(solution)/shard_map/ppermute | solution.py:359
  149.7 14.1 %collective-permute-start.21 = (bf16[256,512]{1,0:T(8,128)(2,1)S(1)}, bf16[256,512]{1,0:T(8,128)(2,1)S(1)}, u32[]{:S(2)}, u32[]{:S(2)}) collective-permute-start(bf16[256,512]{1,0:T(8,128)(2,1)S(1)} %get-tuple-element.36), channel_id=1, source_target_pairs={{0,96},{16,112},{32,64},{48,80},{64,32},{80,48},{96,0},{112,16},{1... | collective-permute-start | bytes 786440 | tf_op jit(solution)/shard_map/ppermute | solution.py:359
  150.2 23.8 %collective-permute-start.17 = (bf16[64,4096]{1,0:T(8,128)(2,1)S(1)}, bf16[64,4096]{1,0:T(8,128)(2,1)S(1)}, u32[]{:S(2)}, u32[]{:S(2)}) collective-permute-start(bf16[64,4096]{1,0:T(8,128)(2,1)S(1)} %copy-done.3), channel_id=1, source_target_pairs={{0,15},{1,14},{2,13},{3,12},{4,11},{5,10},{6,9},{7,8},{8,7},{9,6},... | collective-permute-start | bytes 1572872 | tf_op jit(solution)/shard_map/ppermute | solution.py:363
  164.9 8.3 %collective-permute-start.22 = (bf16[256,256]{1,0:T(8,128)(2,1)S(1)}, bf16[256,256]{1,0:T(8,128)(2,1)S(1)}, u32[]{:S(2)}, u32[]{:S(2)}) collective-permute-start(bf16[256,256]{1,0:T(8,128)(2,1)S(1)} %select_convert_fusion), channel_id=1, source_target_pairs={{0,8},{8,0},{1,9},{9,1},{2,10},{10,2},{3,11},{11,3},{4,12},{12,4},... | collective-permute-start | bytes 393224 | tf_op jit(solution)/shard_map/ppermute | solution.py:367
  (11 other events, 10.3 us)

commit v4 on v3

--- a/solution.py
+++ b/solution.py
@@ -17,7 +17,7 @@
 D = 4096
 F32 = jnp.float32
 BF16 = jnp.bfloat16
-VMEM_LIMIT = 56 * 1024 * 1024
+VMEM_LIMIT = 36 * 1024 * 1024
 
 
 def flip_matrix(n):
@@ -30,8 +30,8 @@
     return lax.dot_general(a, b, (((ca,), (cb,)), ((), ())), preferred_element_type=F32)
 
 
-def params(**kw):
-    return pltpu.CompilerParams(vmem_limit_bytes=VMEM_LIMIT, **kw)
+def params(limit=VMEM_LIMIT):
+    return pltpu.CompilerParams(vmem_limit_bytes=limit)
 
 
 def cost(flops, nbytes, trans=0):
@@ -96,21 +96,22 @@
     )(x)
 
 
-def assemble_kernel(blocks, out):
+def assemble_kernel(first, second, out):
     for g in range(N):
-        out[:, :, GW * g : GW * (g + 1)] = blocks[g]
-
-
-def assemble(blocks):
+        out[:, :, GW * g : GW * g + DH] = first[g]
+        out[:, :, GW * g + DH : GW * (g + 1)] = second[g]
+
+
+def assemble(first, second):
     return pl.pallas_call(
         assemble_kernel,
-        in_specs=[pl.BlockSpec(memory_space=pltpu.VMEM)],
+        in_specs=[pl.BlockSpec(memory_space=pltpu.VMEM)] * 2,
         out_specs=pl.BlockSpec(memory_space=pltpu.VMEM),
         out_shape=struct(3, ROWS, 2048),
         compiler_params=params(),
         cost_estimate=cost(0, 2 * 3 * ROWS * 2048 * 2),
         name="assemble",
-    )(blocks)
+    )(first, second)
 
 
 def upstream_kernel(cot, recv, out):
@@ -189,7 +190,7 @@
             ],
         ),
         out_shape=[struct(3, SEQ, GW), struct(512, GW), struct(512, GW), struct(2, SEQ, SEQ)],
-        compiler_params=params(),
+        compiler_params=params(63 * 1024 * 1024),
         cost_estimate=cost(4 * 4 * SEQ * SEQ * DH, 10 << 20, 2 * SEQ * SEQ),
         name="attention_fwd",
     )(c, blocks, *after)
@@ -234,7 +235,7 @@
             out[to, 2] = dv[ROWS * j : ROWS * (j + 1), :].astype(BF16)
 
 
-def attention_bwd(c, h, cat, probs_t, g_own, g_recv, filled, after):
+def attention_bwd(c, h, cat, probs_t, g_own, g_recv, after):
     return pl.pallas_call(
         bwd_kernel,
         grid_spec=pltpu.PrefetchScalarGridSpec(
@@ -246,16 +247,15 @@
                 pl.BlockSpec((256, DH), lambda q, c_ref: (jnp.minimum(q, 1), h)),
                 pl.BlockSpec((256, DH), lambda q, c_ref: (jnp.maximum(q - 2, 0), h)),
             ]
-            + [ANY] * (len(filled) + len(after)),
-            out_specs=pl.BlockSpec((N, 3, ROWS, DH), lambda q, c_ref: (0, 0, 0, h)),
+            + [ANY] * len(after),
+            out_specs=pl.BlockSpec((N, 3, ROWS, DH), lambda q, c_ref: (0, 0, 0, 0)),
             scratch_shapes=[pltpu.VMEM((SEQ, DH), BF16), pltpu.VMEM((SEQ, DH), F32), pltpu.VMEM((SEQ, DH), F32)],
         ),
-        out_shape=struct(N, 3, ROWS, GW),
-        input_output_aliases={5 + i: i for i in range(len(filled))},
+        out_shape=struct(N, 3, ROWS, DH),
         compiler_params=params(),
         cost_estimate=cost(4 * 2 * SEQ * SEQ * DH, 4 << 20),
         name="attention_bwd",
-    )(c, cat, probs_t, g_own, g_recv, *filled, *after)
+    )(c, cat, probs_t, g_own, g_recv, *after)
 
 
 def grad_kernel(*refs):
@@ -316,7 +316,7 @@
         ],
         out_specs=[pl.BlockSpec((r, 1024), lambda k: (0, k)) for r in rows],
         out_shape=[struct(r, D) for r in rows],
-        compiler_params=params(),
+        compiler_params=params(63 * 1024 * 1024),
         cost_estimate=cost(2 * 512 * GW * D, 7 << 20),
         name="project",
     )(own, recv, w)
@@ -355,8 +355,29 @@
     )(d, own, recv, *pieces, *after)
 
 
+def weight_sum_kernel(own, recv, *refs):
+    for x in range(4):
+        refs[x - 4][...] = add(own[x], recv[x]).astype(BF16)
+
+
+def weight_sum(own, recv, after):
+    return pl.pallas_call(
+        weight_sum_kernel,
+        in_specs=[pl.BlockSpec(memory_space=pltpu.VMEM)] * 2 + [ANY] * len(after),
+        out_specs=[pl.BlockSpec(memory_space=pltpu.VMEM)] * 4,
+        out_shape=[struct(GW, 512)] * 4,
+        compiler_params=params(),
+        cost_estimate=cost(0, 3 << 20),
+        name="weight_sum",
+    )(own, recv, *after)
+
+
 def by_xor(x, axis, k):
     return lax.ppermute(x, axis, [(i, i ^ k) for i in range(N)])
+
+
+def exchange(x):
+    return lax.all_to_all(x, "ctx", split_axis=0, concat_axis=0, tiled=True)
 
 
 def mirror(x):
@@ -378,21 +399,22 @@
     return total
 
 
-def mix_sum_kernel(p0, r1, r3, r4, out):
+def mix_sum_kernel(p0, r1, r3, r4, *refs):
+    out = refs[-1]
     out[...] = add(p0[...], r1[...], r3[...], r4[...]).astype(BF16)
 
 
-def mix_sum(*terms):
+def mix_sum(terms, after):
     return pl.pallas_call(
         mix_sum_kernel,
         grid=(2,),
-        in_specs=[pl.BlockSpec((HALF, 2048), lambda k: (0, k))] * 4,
+        in_specs=[pl.BlockSpec((HALF, 2048), lambda k: (0, k))] * 4 + [ANY] * len(after),
         out_specs=pl.BlockSpec((HALF, 2048), lambda k: (0, k)),
         out_shape=struct(HALF, D),
         compiler_params=params(),
         cost_estimate=cost(0, 5 << 19),
         name="mix_sum",
-    )(*terms)
+    )(*terms, *after)
 
 
 def mix_out_kernel(own, recv, out):
@@ -422,38 +444,42 @@
 
     cot_recv = mirror(cot[HALF:])
     (sent,) = gate([split(mine)], [cot_recv])
-    blocks = lax.all_to_all(sent, "ctx", split_axis=0, concat_axis=0, tiled=True)
+    blocks = exchange(sent)
 
     u = upstream_rows(cot, cot_recv)
     y1, y3, z = by_xor(u, "ctx", 1), by_xor(u, "ctx", 3), by_xor(u, "ctx", 4)
-    y2, zy1, zy3 = by_xor(y3, "ctx", 1), by_xor(z, "ctx", 1), by_xor(z, "ctx", 3)
+    y2, zy1, zy3 = by_xor(y3, "ctx", 1), by_xor(y1, "ctx", 4), by_xor(z, "ctx", 3)
     cat, att_own, att_send, probs_t = attention_fwd(c, blocks, [y1, y3, z])
-    (att_send,) = gate([att_send], [y2, zy3])
+    att_send, zy3 = gate([att_send, zy3], [y2, zy1])
     att_recv = other_strand(att_send)
-    zy2 = by_xor(y2, "ctx", 4)
+    zy2 = by_xor(zy3, "ctx", 1)
     pieces = [u, y1, y2, y3, z, zy1, zy2, zy3]
 
     p0, p1, p2, p3, p4, p5, p6, p7 = project(att_own, att_recv, out_weight)
-    r5, r7, r6 = by_xor(p5, "ctx", 1), by_xor(p7, "ctx", 3), by_xor(p6, "ctx", 4)
+    r6, r7, r2 = by_xor(p6, "ctx", 3), by_xor(p7, "ctx", 4), by_xor(p2, "ctx", 1)
     g_own = grad_attended(pieces, out_weight, [p0])
     g_recv = other_strand(g_own)
-    p4 = add(p4, r5, r7).astype(BF16)
-    p2 = add(p2, r6).astype(BF16)
-    r4, r2 = by_xor(p4, "ctx", 4), by_xor(p2, "ctx", 1)
-    w_own, w_other = weight_part(d, att_own, att_recv, pieces, [g_own, p4, p2])
-    grads = attention_bwd(c, 0, cat, probs_t, g_own, g_recv, [], [w_own])
-    p3 = add(p3, r2).astype(BF16)
-    p3, p1 = gate([p3, p1], [grads])
-    r3, r1 = by_xor(p3, "ctx", 3), by_xor(p1, "ctx", 1)
-    grads = attention_bwd(c, 1, cat, probs_t, g_own, g_recv, [grads], [p3, p1])
-    mixed_own = mix_sum(p0, r1, r3, r4)
-    back = lax.all_to_all(grads, "ctx", split_axis=0, concat_axis=0, tiled=True)
-    mixed = mix_out(mixed_own, mirror(mixed_own))
-    qkv_grad = jnp.transpose(assemble(back), (1, 0, 2))
-
-    w_sum = add(w_own, by_xor(w_other, "dp", 1)).astype(BF16)
-    (w_sum,) = gate([w_sum], [mixed_own])
-    w_chip = add(w_sum[0], *[by_xor(w_sum[x], "dp", 2 * x) for x in range(1, 4)])
+    p5 = add(p5, r6).astype(BF16)
+    r5 = by_xor(p5, "ctx", 4)
+    w_own, w_other = weight_part(d, att_own, att_recv, pieces, [g_own, p5])
+    p3 = add(p3, r7, r2).astype(BF16)
+    r3 = by_xor(p3, "ctx", 3)
+    grads0 = attention_bwd(c, 0, cat, probs_t, g_own, g_recv, [w_own, p3])
+    p1 = add(p1, r5).astype(BF16)
+    grads0, p4 = gate([grads0, p4], [p1, r3])
+    r1, r4 = by_xor(p1, "ctx", 1), by_xor(p4, "ctx", 4)
+    back0 = exchange(grads0)
+    grads1 = attention_bwd(c, 1, cat, probs_t, g_own, g_recv, [p1])
+    mixed_own = mix_sum([p0, r1, r3, r4], [grads1])
+    (grads1,) = gate([grads1], [back0])
+    back1 = exchange(grads1)
+    mixed_recv = mirror(mixed_own)
+    mixed = mix_out(mixed_own, mixed_recv)
+    qkv_grad = jnp.transpose(assemble(back0, back1), (1, 0, 2))
+
+    w_sum = weight_sum(w_own, by_xor(w_other, "dp", 1), [mixed_own])
+    w_recv = gate([by_xor(w_sum[x], "dp", 2 * x) for x in range(1, 4)], [mixed_recv])
+    w_chip = add(w_sum[0], *w_recv)
     first, second = w_chip[:, :GW], w_chip[:, GW:]
     w_keep = jnp.where(s == 0, first, second)
     w_send = jnp.where(s == 0, second, first).astype(BF16)

time: 183 us -> 172 us (0.940)
  Pallas kernels: 55.7 us -> 48 us
  waiting for transfers between devices: 61.1 us -> 56.6 us
  other arithmetic: 5.57 us -> 2.3 us
  local copies, waits for them, and re-layouts: 9.62 us -> 12.6 us
  starting transfers between devices: 48.2 us -> 51 us
    unnamed x36 -> x48, local copies, waits for them, and re-layouts: 6.62 us -> 11.5 us
    all_to_all x2 -> x3, starting transfers between devices: 11.4 us -> 16 us  [exchange(): return lax.all_to_all(x, 'ctx', split_axis=0, concat_axis=0, tiled=True)]
    ppermute x18, waiting for transfers between devices: 39.6 us -> 36.2 us  [by_xor(): return lax.ppermute(x, axis, [(i, i ^ k) for i in range(N)])]
    convert_element_type x4 -> x3, other arithmetic: 3.72 us -> 0.45 us  [the longest x1 0.19 us: body(): p3 = add(p3, r7, r2).astype(BF16)]
    ppermute x18, starting transfers between devices: 23 us -> 20.7 us  [by_xor(): return lax.ppermute(x, axis, [(i, i ^ k) for i in range(N)])]
    pallas_call x0 -> x1, Pallas kernels: none -> 2.16 us  [weight_sum(): pl.pallas_call(weight_sum_kernel, in_specs=[pl.BlockSpec(memory_space=plt...]
    pallas_call x2, Pallas kernels: 15.8 us -> 13.8 us  [attention_bwd(): pl.pallas_call(bwd_kernel, grid_spec=pltpu.PrefetchScalarGridSpec(num_sca...]
    squeeze x1 -> x0, local copies, waits for them, and re-layouts: 1.92 us -> none  [body(): w_sum[x]]
  transfers between devices with their start and end apart: 25 -> 26, of which waited for: 10 -> 10; matrix products, arithmetic and copies ran while one was open for 4% -> 1% of each run, Pallas kernels for 29% -> 27%
where the time goes in v4:
time: 172 us; the launch traced here: 171 us
  waiting for transfers between devices  56.6 us (33%)
  starting transfers between devices  51 us (30%)
  Pallas kernels  48 us (28%)
  local copies, waits for them, and re-layouts  12.6 us (7%)
  other arithmetic  2.3 us (1%)
    ppermute x18, waiting for transfers between devices, by_xor(): return lax.ppermute(x, axis, [(i, i ^ k) for i in range(N)])  36.2 us
    ppermute x18, starting transfers between devices, by_xor(): return lax.ppermute(x, axis, [(i, i ^ k) for i in range(N)])  20.7 us
    all_to_all x3, starting transfers between devices, exchange(): return lax.all_to_all(x, 'ctx', split_axis=0, concat_axis=0, tiled=True)  16 us
    pallas_call x2, Pallas kernels, attention_bwd(): pl.pallas_call(bwd_kernel, grid_spec=pltpu.PrefetchScalarGridSpec(num_sca...  13.8 us
    pallas_call x1, Pallas kernels, attention_fwd(): pl.pallas_call(fwd_kernel, grid_spec=pltpu.PrefetchScalarGridSpec(num_sca...  12 us
    unnamed x48, local copies, waits for them, and re-layouts  11.5 us
    ppermute x3, waiting for transfers between devices, other_strand(): return lax.ppermute(x, 'strand', [(0, 1), (1, 0)])  11.1 us
    ppermute x2, waiting for transfers between devices, mirror(): lax.ppermute(x, ('strand', 'ctx'), [(i, 2 * N - 1 - i) for i in range(2 *...  9.25 us
  transfers between devices with their start and end apart: 26, of which 10 were waited for; matrix products, arithmetic and copies ran while one was open for 1% of the time, Pallas kernels for 27%

profile of v4, /device:TPU:8, one launch (start us, length us, event | category | flops | bytes accessed | tf_op | source)
XLA Modules:
  0.0 171.3 jit_solution(14043564887961575612)
XLA Ops:
  1.7 5.1 %collective-permute-start = (bf16[64,4096]{1,0:T(8,128)(2,1)S(1)}, bf16[64,4096]{1,0:T(8,128)(2,1)S(1)}, u32[]{:S(2)}, u32[]{:S(2)}) collective-permute-start(bf16[64,4096]{1,0:T(8,128)(2,1)S(1)} %slice_bitcast_fusion), channel_id=1, source_target_pairs={{0,15},{1,14},{2,13},{3,12},{4,11},{5,10},{6,9},{7,8},{8,7},{9,6},... | collective-permute-start | bytes 1572872 | tf_op jit(solution)/shard_map/ppermute | solution.py:384
  9.5 9.3 %collective-permute-done.refs_1_.recv = bf16[64,4096]{1,0:T(8,128)(2,1)S(1)} collective-permute-done((bf16[64,4096]{1,0:T(8,128)(2,1)S(1)}, bf16[64,4096]{1,0:T(8,128)(2,1)S(1)}, u32[]{:S(2)}, u32[]{:S(2)}) %collective-permute-start) | collective-permute-done | bytes 524320 | tf_op jit(solution)/shard_map/ppermute | solution.py:384
  18.8 6.2 %all-to-all-start = ((bf16[8,3,128,256]{3,2,1,0:T(8,128)(2,1)}), bf16[8,3,128,256]{3,2,1,0:T(8,128)(2,1)}, u32[]{:S(2)}, u32[]{:S(2)}) async-start(bf16[8,3,128,256]{3,2,1,0:T(8,128)(2,1)} %gate.5), calls=%async_computation | async-start | bytes 3145728 | tf_op jit(solution)/shard_map/all_to_all | solution.py:380
  25.5 1.6 collective-permute-start.3
  27.1 1.5 collective-permute-start.2
  28.6 1.8 %collective-permute-start.1 = (bf16[64,4096]{1,0:T(8,128)(2,1)S(1)}, bf16[64,4096]{1,0:T(8,128)(2,1)}, u32[]{:S(2)}, u32[]{:S(2)}) collective-permute-start(bf16[64,4096]{1,0:T(8,128)(2,1)S(1)} %upstream_rows.1.refs_0_), channel_id=1, source_target_pairs={{0,1},{1,0},{2,3},{3,2},{4,5},{5,4},{6,7},{7,6},{8,9},{9,8},{10,11... | collective-permute-start | bytes 1572872 | tf_op jit(solution)/shard_map/ppermute | solution.py:376
  31.2 23.5 %collective-permute-done.3.refs_2_.refs_4_ = bf16[64,4096]{1,0:T(8,128)(2,1)} collective-permute-done((bf16[64,4096]{1,0:T(8,128)(2,1)S(1)}, bf16[64,4096]{1,0:T(8,128)(2,1)}, u32[]{:S(2)}, u32[]{:S(2)}) %collective-permute-start.3) | collective-permute-done | bytes 524320 | tf_op jit(solution)/shard_map/ppermute | solution.py:376
  56.2 1.8 %collective-permute-start.5 = (bf16[64,4096]{1,0:T(8,128)(2,1)}, bf16[64,4096]{1,0:T(8,128)(2,1)S(1)}, u32[]{:S(2)}, u32[]{:S(2)}) collective-permute-start(bf16[64,4096]{1,0:T(8,128)(2,1)} %collective-permute-done.2.refs_1_.refs_3_), channel_id=1, source_target_pairs={{0,1},{1,0},{2,3},{3,2},{4,5},{5,4},{6,7},{7,6},{8,9},{9,8},{10,11... | collective-permute-start | bytes 1572872 | tf_op jit(solution)/shard_map/ppermute | solution.py:376
  58.3 12.0 %attention_fwd.1 = (bf16[3,1024,256]{2,1,0:T(8,128)(2,1)}, bf16[512,256]{1,0:T(8,128)(2,1)}, bf16[512,256]{1,0:T(8,128)(2,1)}, bf16[2,1024,1024]{2,1,0:T(8,128)(2,1)}) custom-call(s32[1]{0:T(128)} %bitcast.c_ref, bf16[8,3,128,256]{3,2,1,0:T(8,128)(2,1)} %all-to-all-done.blocks, bf16[64,4096]{1,0:T(8,128)(2,1)} %collective-permute-done.1.refs_0_.refs_1_, ...), custom_call_target="tpu_custom_call" | custom-call | flops 2147483648 | bytes 10485760 | tf_op jit(solution)/shard_map/attention_fwd/pallas_call | solution.py:179
  72.5 2.9 %collective-permute-start.7 = (bf16[512,256]{1,0:T(8,128)(2,1)S(1)}, bf16[512,256]{1,0:T(8,128)(2,1)S(1)}, u32[]{:S(2)}, u32[]{:S(2)}) collective-permute-start(bf16[512,256]{1,0:T(8,128)(2,1)S(1)} %get-tuple-element.30), channel_id=1, source_target_pairs={{0,8},{8,0},{1,9},{9,1},{2,10},{10,2},{3,11},{11,3},{4,12},{12,4},... | collective-permute-start | bytes 786440 | tf_op jit(solution)/shard_map/ppermute | solution.py:388
  75.8 5.0 %collective-permute-done.7.recv = bf16[512,256]{1,0:T(8,128)(2,1)S(1)} collective-permute-done((bf16[512,256]{1,0:T(8,128)(2,1)S(1)}, bf16[512,256]{1,0:T(8,128)(2,1)S(1)}, u32[]{:S(2)}, u32[]{:S(2)}) %collective-permute-start.7) | collective-permute-done | bytes 262176 | tf_op jit(solution)/shard_map/ppermute | solution.py:388
  81.5 4.9 %project.1 = (bf16[64,4096]{1,0:T(8,128)(2,1)}, bf16[64,4096]{1,0:T(8,128)(2,1)}, bf16[64,4096]{1,0:T(8,128)(2,1)}, bf16[64,4096]{1,0:T(8,128)(2,1)}, bf16[64,40...) custom-call(bf16[512,256]{1,0:T(8,128)(2,1)} %get-tuple-element.28.own, ...), custom_call_target="tpu_custom_call" | custom-call | flops 1073741824 | bytes 7340032 | tf_op jit(solution)/shard_map/project/pallas_call | solution.py:309
  87.5 1.6 collective-permute-start.12
  90.2 1.6 copy-done.8
  92.8 4.2 %grad_attended.1.refs_8_.g_own = bf16[512,256]{1,0:T(8,128)(2,1)S(1)} custom-call(bf16[64,4096]{1,0:T(8,128)(2,1)S(1)} %copy-done.4, bf16[64,4096]{1,0:T(8,128)(2,1)} %collective-permute-done.1.refs_0_.refs_1_, bf16[64,4096]{1,0:T(8,128)(2,1)S(1)} %collective-permute-done.5.refs_2_, bf16[64,4096]{1,0:T(8,128)(2,1)} %collective-permute-done.2.refs_1_.refs_3_, ...), custom_call_target="tpu_custom_call" | custom-call | flops 1073741824 | bytes 7340032 | tf_op jit(solution)/shard_map/grad_attended/pallas_call | solution.py:283
  97.0 2.8 %collective-permute-start.15 = (bf16[512,256]{1,0:T(8,128)(2,1)S(1)}, bf16[512,256]{1,0:T(8,128)(2,1)S(1)}, u32[]{:S(2)}, u32[]{:S(2)}) collective-permute-start(bf16[512,256]{1,0:T(8,128)(2,1)S(1)} %grad_attended.1.refs_8_.g_own), channel_id=1, source_target_pairs={{0,8},{8,0},{1,9},{9,1},{2,10},{10,2},{3,11},{11,3},{4,12},{12,4},... | collective-permute-start | bytes 786440 | tf_op jit(solution)/shard_map/ppermute | solution.py:388
  102.3 4.9 %weight_part.1 = (bf16[4,256,512]{2,1,0:T(8,128)(2,1)S(1)}, bf16[4,256,512]{2,1,0:T(8,128)(2,1)}) custom-call(s32[1]{0:T(128)} %bitcast.5.d_ref, bf16[512,256]{1,0:T(8,128)(2,1)S(1)} %copy-done.16, bf16[512,256]{1,0:T(8,128)(2,1)S(1)} %copy-done.18, bf16[64,4096]{1,0:T(8,128)(2,1)S(1)} %copy-done.4, bf16[64,4096]{1,0:T(8,128)(2,1)} %collective-permute-done.1.refs_0_.refs_1_, ...), custom_call_target="tpu_custom_call" | custom-call | flops 1073741824 | bytes 7340032 | tf_op jit(solution)/shard_map/weight_part/pallas_call | solution.py:341
  108.3 6.9 %attention_bwd.2.refs_0_ = bf16[8,3,128,128]{3,2,1,0:T(8,128)(2,1)} custom-call(s32[1]{0:T(128)} %bitcast.c_ref, bf16[3,1024,256]{2,1,0:T(8,128)(2,1)S(1)} %copy-done.2, bf16[2,1024,1024]{2,1,0:T(8,128)(2,1)S(1)} %copy-done, bf16[512,256]{1,0:T(8,128)(2,1)S(1)} %grad_attended.1.refs_8_.g_own, bf16[512,256]{1,0:T(8,128)(2,1)S(1)} %collective-permute-done.15.g_recv, ...), custom_call_target="tpu_custom_call" | custom-call | flops 1073741824 | bytes 4194304 | tf_op jit(solution)/shard_map/attention_bwd/pallas_call | solution.py:239
  115.8 2.1 %collective-permute-start.10 = (bf16[64,4096]{1,0:T(8,128)(2,1)S(1)}, bf16[64,4096]{1,0:T(8,128)(2,1)}, u32[]{:S(2)}, u32[]{:S(2)}) collective-permute-start(bf16[64,4096]{1,0:T(8,128)(2,1)S(1)} %add_convert_fusion.1.refs_2_.refs_0_), channel_id=1, source_target_pairs={{0,1},{1,0},{2,3},{3,2},{4,5},{5,4},{6,7},{7,6},{8,9},{9,8},{10,11... | collective-permute-start | bytes 1572872 | tf_op jit(solution)/shard_map/ppermute | solution.py:376
  119.0 5.1 %all-to-all-start.1 = ((bf16[8,3,128,128]{3,2,1,0:T(8,128)(2,1)}), bf16[8,3,128,128]{3,2,1,0:T(8,128)(2,1)S(1)}, u32[]{:S(2)}, u32[]{:S(2)}) async-start(bf16[8,3,128,128]{3,2,1,0:T(8,128)(2,1)} %get-tuple-element.44), calls=%async_computation.1 | async-start | bytes 1572864 | tf_op jit(solution)/shard_map/all_to_all | solution.py:380
  124.1 2.2 %copy-done.1 = bf16[2,1024,1024]{2,1,0:T(8,128)(2,1)S(1)} copy-done((bf16[2,1024,1024]{2,1,0:T(8,128)(2,1)S(1)}, bf16[2,1024,1024]{2,1,0:T(8,128)(2,1)}, u32[]{:S(2)}) %copy-start.1) | copy-done | bytes 4194328
  127.2 6.9 %attention_bwd.3.refs_0_ = bf16[8,3,128,128]{3,2,1,0:T(8,128)(2,1)} custom-call(s32[1]{0:T(128)} %bitcast.c_ref, bf16[3,1024,256]{2,1,0:T(8,128)(2,1)S(1)} %copy-done.2, bf16[2,1024,1024]{2,1,0:T(8,128)(2,1)S(1)} %copy-done.1, bf16[512,256]{1,0:T(8,128)(2,1)S(1)} %grad_attended.1.refs_8_.g_own, bf16[512,256]{1,0:T(8,128)(2,1)S(1)} %copy-done.15, ...), custom_call_target="tpu_custom_call" | custom-call | flops 1073741824 | bytes 4194304 | tf_op jit(solution)/shard_map/attention_bwd/pallas_call | solution.py:239
  134.1 4.3 %collective-permute-done.16.r4 = bf16[64,4096]{1,0:T(8,128)(2,1)} collective-permute-done((bf16[64,4096]{1,0:T(8,128)(2,1)}, bf16[64,4096]{1,0:T(8,128)(2,1)}, u32[]{:S(2)}, u32[]{:S(2)}) %collective-permute-start.16) | collective-permute-done | bytes 524320 | tf_op jit(solution)/shard_map/ppermute | solution.py:376
  139.8 3.4 %collective-permute-start.17 = (bf16[64,4096]{1,0:T(8,128)(2,1)S(1)}, bf16[64,4096]{1,0:T(8,128)(2,1)S(1)}, u32[]{:S(2)}, u32[]{:S(2)}) collective-permute-start(bf16[64,4096]{1,0:T(8,128)(2,1)S(1)} %mix_sum.1.own.refs_0_), channel_id=1, source_target_pairs={{0,15},{1,14},{2,13},{3,12},{4,11},{5,10},{6,9},{7,8},{8,7},{9,6},... | collective-permute-start | bytes 1572872 | tf_op jit(solution)/shard_map/ppermute | solution.py:384
  143.2 2.2 %weight_sum.1 = (bf16[256,512]{1,0:T(8,128)(2,1)S(1)}, bf16[256,512]{1,0:T(8,128)(2,1)}, bf16[256,512]{1,0:T(8,128)(2,1)}, bf16[256,512]{1,0:T(8,128)(2,1)}) custom-call(bf16[4,256,512]{2,1,0:T(8,128)(2,1)S(1)} %copy-done.6, bf16[4,256,512]{2,1,0:T(8,128)(2,1)} %collective-permute-done.18.recv, bf16[64,4096]{1,0:T(8,128)(2,1)S(1)} %mix_sum.1.own.refs_0_), custom_call_target="tpu_custom_call" | custom-call | bytes 3145728 | tf_op jit(solution)/shard_map/weight_sum/pallas_call | solution.py:364
  145.4 1.5 collective-permute-start.19
  146.9 2.7 %collective-permute-start.20 = (bf16[256,512]{1,0:T(8,128)(2,1)}, bf16[256,512]{1,0:T(8,128)(2,1)S(1)}, u32[]{:S(2)}, u32[]{:S(2)}) collective-permute-start(bf16[256,512]{1,0:T(8,128)(2,1)} %get-tuple-element.48), channel_id=1, source_target_pairs={{0,64},{16,80},{32,96},{48,112},{64,0},{80,16},{96,32},{112,48},{1... | collective-permute-start | bytes 786440 | tf_op jit(solution)/shard_map/ppermute | solution.py:376
  150.1 4.7 %all-to-all-start.2 = ((bf16[8,3,128,128]{3,2,1,0:T(8,128)(2,1)}), bf16[8,3,128,128]{3,2,1,0:T(8,128)(2,1)S(1)}, u32[]{:S(2)}, u32[]{:S(2)}) async-start(bf16[8,3,128,128]{3,2,1,0:T(8,128)(2,1)} %gate.8), calls=%async_computation.2 | async-start | bytes 1572864 | tf_op jit(solution)/shard_map/all_to_all | solution.py:380
  154.8 4.0 %collective-permute-done.20.refs_1_ = bf16[256,512]{1,0:T(8,128)(2,1)S(1)} collective-permute-done((bf16[256,512]{1,0:T(8,128)(2,1)}, bf16[256,512]{1,0:T(8,128)(2,1)S(1)}, u32[]{:S(2)}, u32[]{:S(2)}) %collective-permute-start.20) | collective-permute-done | bytes 262176 | tf_op jit(solution)/shard_map/ppermute | solution.py:376
  158.8 2.5 %collective-permute-done.21.refs_2_ = bf16[256,512]{1,0:T(8,128)(2,1)S(1)} collective-permute-done((bf16[256,512]{1,0:T(8,128)(2,1)}, bf16[256,512]{1,0:T(8,128)(2,1)S(1)}, u32[]{:S(2)}, u32[]{:S(2)}) %collective-permute-start.21) | collective-permute-done | bytes 262176 | tf_op jit(solution)/shard_map/ppermute | solution.py:376
  163.9 5.1 %collective-permute-done.22 = bf16[256,256]{1,0:T(8,128)(2,1)S(1)} collective-permute-done((bf16[256,256]{1,0:T(8,128)(2,1)S(1)}, bf16[256,256]{1,0:T(8,128)(2,1)S(1)}, u32[]{:S(2)}, u32[]{:S(2)}) %collective-permute-start.22) | collective-permute-done | bytes 131104 | tf_op jit(solution)/shard_map/ppermute | solution.py:388
  169.7 1.6 assemble.1
  (92 shorter events, 24.9 us)
Async XLA Ops:
  1.7 17.1 %collective-permute-start = (bf16[64,4096]{1,0:T(8,128)(2,1)S(1)}, bf16[64,4096]{1,0:T(8,128)(2,1)S(1)}, u32[]{:S(2)}, u32[]{:S(2)}) collective-permute-start(bf16[64,4096]{1,0:T(8,128)(2,1)S(1)} %slice_bitcast_fusion), channel_id=1, source_target_pairs={{0,15},{1,14},{2,13},{3,12},{4,11},{5,10},{6,9},{7,8},{8,7},{9,6},... | collective-permute-start | bytes 1572872 | tf_op jit(solution)/shard_map/ppermute | solution.py:384
  18.8 39.5 %all-to-all-start = ((bf16[8,3,128,256]{3,2,1,0:T(8,128)(2,1)}), bf16[8,3,128,256]{3,2,1,0:T(8,128)(2,1)}, u32[]{:S(2)}, u32[]{:S(2)}) async-start(bf16[8,3,128,256]{3,2,1,0:T(8,128)(2,1)} %gate.5), calls=%async_computation | async-start | bytes 3145728 | tf_op jit(solution)/shard_map/all_to_all | solution.py:380
  25.5 29.2 %collective-permute-start.3 = (bf16[64,4096]{1,0:T(8,128)(2,1)S(1)}, bf16[64,4096]{1,0:T(8,128)(2,1)}, u32[]{:S(2)}, u32[]{:S(2)}) collective-permute-start(bf16[64,4096]{1,0:T(8,128)(2,1)S(1)} %upstream_rows.1.refs_0_), channel_id=1, source_target_pairs={{0,4},{1,5},{2,6},{3,7},{4,0},{5,1},{6,2},{7,3},{8,12},{9,13},{10,... | collective-permute-start | bytes 1572872 | tf_op jit(solution)/shard_map/ppermute | solution.py:376
  27.1 29.1 %collective-permute-start.2 = (bf16[64,4096]{1,0:T(8,128)(2,1)S(1)}, bf16[64,4096]{1,0:T(8,128)(2,1)}, u32[]{:S(2)}, u32[]{:S(2)}) collective-permute-start(bf16[64,4096]{1,0:T(8,128)(2,1)S(1)} %upstream_rows.1.refs_0_), channel_id=1, source_target_pairs={{0,3},{1,2},{2,1},{3,0},{4,7},{5,6},{6,5},{7,4},{8,11},{9,10},{10,... | collective-permute-start | bytes 1572872 | tf_op jit(solution)/shard_map/ppermute | solution.py:376
  28.6 29.4 %collective-permute-start.1 = (bf16[64,4096]{1,0:T(8,128)(2,1)S(1)}, bf16[64,4096]{1,0:T(8,128)(2,1)}, u32[]{:S(2)}, u32[]{:S(2)}) collective-permute-start(bf16[64,4096]{1,0:T(8,128)(2,1)S(1)} %upstream_rows.1.refs_0_), channel_id=1, source_target_pairs={{0,1},{1,0},{2,3},{3,2},{4,5},{5,4},{6,7},{7,6},{8,9},{9,8},{10,11... | collective-permute-start | bytes 1572872 | tf_op jit(solution)/shard_map/ppermute | solution.py:376
  54.7 15.5 %collective-permute-start.4 = (bf16[64,4096]{1,0:T(8,128)(2,1)}, bf16[64,4096]{1,0:T(8,128)(2,1)}, u32[]{:S(2)}, u32[]{:S(2)}) collective-permute-start(bf16[64,4096]{1,0:T(8,128)(2,1)} %collective-permute-done.3.refs_2_.refs_4_), channel_id=1, source_target_pairs={{0,3},{1,2},{2,1},{3,0},{4,7},{5,6},{6,5},{7,4},{8,11},{9,10},{10,... | collective-permute-start | bytes 1572872 | tf_op jit(solution)/shard_map/ppermute | solution.py:376
  56.2 14.1 %collective-permute-start.5 = (bf16[64,4096]{1,0:T(8,128)(2,1)}, bf16[64,4096]{1,0:T(8,128)(2,1)S(1)}, u32[]{:S(2)}, u32[]{:S(2)}) collective-permute-start(bf16[64,4096]{1,0:T(8,128)(2,1)} %collective-permute-done.2.refs_1_.refs_3_), channel_id=1, source_target_pairs={{0,1},{1,0},{2,3},{3,2},{4,5},{5,4},{6,7},{7,6},{8,9},{9,8},{10,11... | collective-permute-start | bytes 1572872 | tf_op jit(solution)/shard_map/ppermute | solution.py:376
  57.9 13.6 %collective-permute-start.6 = (bf16[64,4096]{1,0:T(8,128)(2,1)}, bf16[64,4096]{1,0:T(8,128)(2,1)}, u32[]{:S(2)}, u32[]{:S(2)}) collective-permute-start(bf16[64,4096]{1,0:T(8,128)(2,1)} %collective-permute-done.1.refs_0_.refs_1_), channel_id=1, source_target_pairs={{0,4},{1,5},{2,6},{3,7},{4,0},{5,1},{6,2},{7,3},{8,12},{9,13},{10,... | collective-permute-start | bytes 1572872 | tf_op jit(solution)/shard_map/ppermute | solution.py:376
  72.5 8.3 %collective-permute-start.7 = (bf16[512,256]{1,0:T(8,128)(2,1)S(1)}, bf16[512,256]{1,0:T(8,128)(2,1)S(1)}, u32[]{:S(2)}, u32[]{:S(2)}) collective-permute-start(bf16[512,256]{1,0:T(8,128)(2,1)S(1)} %get-tuple-element.30), channel_id=1, source_target_pairs={{0,8},{8,0},{1,9},{9,1},{2,10},{10,2},{3,11},{11,3},{4,12},{12,4},... | collective-permute-start | bytes 786440 | tf_op jit(solution)/shard_map/ppermute | solution.py:388
  75.4 13.7 %collective-permute-start.14 = (bf16[64,4096]{1,0:T(8,128)(2,1)}, bf16[64,4096]{1,0:T(8,128)(2,1)}, u32[]{:S(2)}, u32[]{:S(2)}) collective-permute-start(bf16[64,4096]{1,0:T(8,128)(2,1)} %get-tuple-element.40.refs_7_), channel_id=1, source_target_pairs={{0,1},{1,0},{2,3},{3,2},{4,5},{5,4},{6,7},{7,6},{8,9},{9,8},{10,11... | collective-permute-start | bytes 1572872 | tf_op jit(solution)/shard_map/ppermute | solution.py:376
  86.3 13.5 %collective-permute-start.8 = (bf16[64,4096]{1,0:T(8,128)(2,1)}, bf16[64,4096]{1,0:T(8,128)(2,1)S(1)}, u32[]{:S(2)}, u32[]{:S(2)}) collective-permute-start(bf16[64,4096]{1,0:T(8,128)(2,1)} %get-tuple-element.34), channel_id=1, source_target_pairs={{0,3},{1,2},{2,1},{3,0},{4,7},{5,6},{6,5},{7,4},{8,11},{9,10},{10,... | collective-permute-start | bytes 1572872 | tf_op jit(solution)/shard_map/ppermute | solution.py:376
  86.4 14.8 %collective-permute-start.11 = (bf16[64,4096]{1,0:T(8,128)(2,1)}, bf16[64,4096]{1,0:T(8,128)(2,1)S(1)}, u32[]{:S(2)}, u32[]{:S(2)}) collective-permute-start(bf16[64,4096]{1,0:T(8,128)(2,1)} %get-tuple-element.36), channel_id=1, source_target_pairs={{0,4},{1,5},{2,6},{3,7},{4,0},{5,1},{6,2},{7,3},{8,12},{9,13},{10,... | collective-permute-start | bytes 1572872 | tf_op jit(solution)/shard_map/ppermute | solution.py:376
  87.5 13.7 %collective-permute-start.12 = (bf16[64,4096]{1,0:T(8,128)(2,1)}, bf16[64,4096]{1,0:T(8,128)(2,1)S(1)}, u32[]{:S(2)}, u32[]{:S(2)}) collective-permute-start(bf16[64,4096]{1,0:T(8,128)(2,1)} %get-tuple-element.37), channel_id=1, source_target_pairs={{0,1},{1,0},{2,3},{3,2},{4,5},{5,4},{6,7},{7,6},{8,9},{9,8},{10,11... | collective-permute-start | bytes 1572872 | tf_op jit(solution)/shard_map/ppermute | solution.py:376
  97.0 11.3 %collective-permute-start.15 = (bf16[512,256]{1,0:T(8,128)(2,1)S(1)}, bf16[512,256]{1,0:T(8,128)(2,1)S(1)}, u32[]{:S(2)}, u32[]{:S(2)}) collective-permute-start(bf16[512,256]{1,0:T(8,128)(2,1)S(1)} %grad_attended.1.refs_8_.g_own), channel_id=1, source_target_pairs={{0,8},{8,0},{1,9},{9,1},{2,10},{10,2},{3,11},{11,3},{4,12},{12,4},... | collective-permute-start | bytes 786440 | tf_op jit(solution)/shard_map/ppermute | solution.py:388
  99.9 15.8 %collective-permute-start.9 = (bf16[64,4096]{1,0:T(8,128)(2,1)S(1)}, bf16[64,4096]{1,0:T(8,128)(2,1)S(1)}, u32[]{:S(2)}, u32[]{:S(2)}) collective-permute-start(bf16[64,4096]{1,0:T(8,128)(2,1)S(1)} %add_convert_fusion.2.refs_9_), channel_id=1, source_target_pairs={{0,4},{1,5},{2,6},{3,7},{4,0},{5,1},{6,2},{7,3},{8,12},{9,13},{10,... | collective-permute-start | bytes 1572872 | tf_op jit(solution)/shard_map/ppermute | solution.py:376
  101.2 7.1 %copy-start.2 = (bf16[3,1024,256]{2,1,0:T(8,128)(2,1)S(1)}, bf16[3,1024,256]{2,1,0:T(8,128)(2,1)}, u32[]{:S(2)}) copy-start(bf16[3,1024,256]{2,1,0:T(8,128)(2,1)} %get-tuple-element.38.cat) | copy-start | bytes 4718596
  101.4 16.5 %collective-permute-start.13 = (bf16[64,4096]{1,0:T(8,128)(2,1)S(1)}, bf16[64,4096]{1,0:T(8,128)(2,1)S(1)}, u32[]{:S(2)}, u32[]{:S(2)}) collective-permute-start(bf16[64,4096]{1,0:T(8,128)(2,1)S(1)} %add_convert_fusion.refs_1_), channel_id=1, source_target_pairs={{0,3},{1,2},{2,1},{3,0},{4,7},{5,6},{6,5},{7,4},{8,11},{9,10},{10,... | collective-permute-start | bytes 1572872 | tf_op jit(solution)/shard_map/ppermute | solution.py:376
  107.3 7.9 %copy-start.5 = (bf16[4,256,512]{2,1,0:T(8,128)(2,1)}, bf16[4,256,512]{2,1,0:T(8,128)(2,1)S(1)}, u32[]{:S(2)}) copy-start(bf16[4,256,512]{2,1,0:T(8,128)(2,1)S(1)} %get-tuple-element.41.refs_0_.own) | copy-start | bytes 3145732
  107.3 36.0 %collective-permute-start.18 = (bf16[4,256,512]{2,1,0:T(8,128)(2,1)}, bf16[4,256,512]{2,1,0:T(8,128)(2,1)}, u32[]{:S(2)}, u32[]{:S(2)}) collective-permute-start(bf16[4,256,512]{2,1,0:T(8,128)(2,1)} %get-tuple-element.45), channel_id=1, source_target_pairs={{0,16},{16,0},{32,48},{48,32},{64,80},{80,64},{96,112},{112,96},{1... | collective-permute-start | bytes 3145736 | tf_op jit(solution)/shard_map/ppermute | solution.py:376
  108.3 7.4 %copy-start.21 = (bf16[64,4096]{1,0:T(8,128)(2,1)S(1)}, bf16[64,4096]{1,0:T(8,128)(2,1)}, u32[]{:S(2)}) copy-start(bf16[64,4096]{1,0:T(8,128)(2,1)} %get-tuple-element.32) | copy-start | bytes 1572868
  115.8 18.3 %collective-permute-start.10 = (bf16[64,4096]{1,0:T(8,128)(2,1)S(1)}, bf16[64,4096]{1,0:T(8,128)(2,1)}, u32[]{:S(2)}, u32[]{:S(2)}) collective-permute-start(bf16[64,4096]{1,0:T(8,128)(2,1)S(1)} %add_convert_fusion.1.refs_2_.refs_0_), channel_id=1, source_target_pairs={{0,1},{1,0},{2,3},{3,2},{4,5},{5,4},{6,7},{7,6},{8,9},{9,8},{10,11... | collective-permute-start | bytes 1572872 | tf_op jit(solution)/shard_map/ppermute | solution.py:376
  118.7 19.7 %collective-permute-start.16 = (bf16[64,4096]{1,0:T(8,128)(2,1)}, bf16[64,4096]{1,0:T(8,128)(2,1)}, u32[]{:S(2)}, u32[]{:S(2)}) collective-permute-start(bf16[64,4096]{1,0:T(8,128)(2,1)} %get-tuple-element.43), channel_id=1, source_target_pairs={{0,4},{1,5},{2,6},{3,7},{4,0},{5,1},{6,2},{7,3},{8,12},{9,13},{10,... | collective-permute-start | bytes 1572872 | tf_op jit(solution)/shard_map/ppermute | solution.py:376
  119.0 31.1 %all-to-all-start.1 = ((bf16[8,3,128,128]{3,2,1,0:T(8,128)(2,1)}), bf16[8,3,128,128]{3,2,1,0:T(8,128)(2,1)S(1)}, u32[]{:S(2)}, u32[]{:S(2)}) async-start(bf16[8,3,128,128]{3,2,1,0:T(8,128)(2,1)} %get-tuple-element.44), calls=%async_computation.1 | async-start | bytes 1572864 | tf_op jit(solution)/shard_map/all_to_all | solution.py:380
  127.2 11.2 %copy-start.10 = (bf16[64,4096]{1,0:T(8,128)(2,1)S(1)}, bf16[64,4096]{1,0:T(8,128)(2,1)}, u32[]{:S(2)}) copy-start(bf16[64,4096]{1,0:T(8,128)(2,1)} %get-tuple-element.31.refs_9_.p0) | copy-start | bytes 1572868
  127.2 11.2 %copy-start.12 = (bf16[64,4096]{1,0:T(8,128)(2,1)S(1)}, bf16[64,4096]{1,0:T(8,128)(2,1)}, u32[]{:S(2)}) copy-start(bf16[64,4096]{1,0:T(8,128)(2,1)} %copy-done.11) | copy-start | bytes 1572868
  134.1 9.1 %copy-start.6 = (bf16[4,256,512]{2,1,0:T(8,128)(2,1)S(1)}, bf16[4,256,512]{2,1,0:T(8,128)(2,1)}, u32[]{:S(2)}) copy-start(bf16[4,256,512]{2,1,0:T(8,128)(2,1)} %copy-done.5) | copy-start | bytes 3145732
  139.8 21.5 %collective-permute-start.17 = (bf16[64,4096]{1,0:T(8,128)(2,1)S(1)}, bf16[64,4096]{1,0:T(8,128)(2,1)S(1)}, u32[]{:S(2)}, u32[]{:S(2)}) collective-permute-start(bf16[64,4096]{1,0:T(8,128)(2,1)S(1)} %mix_sum.1.own.refs_0_), channel_id=1, source_target_pairs={{0,15},{1,14},{2,13},{3,12},{4,11},{5,10},{6,9},{7,8},{8,7},{9,6},... | collective-permute-start | bytes 1572872 | tf_op jit(solution)/shard_map/ppermute | solution.py:384
  145.4 9.4 %collective-permute-start.19 = (bf16[256,512]{1,0:T(8,128)(2,1)}, bf16[256,512]{1,0:T(8,128)(2,1)S(1)}, u32[]{:S(2)}, u32[]{:S(2)}) collective-permute-start(bf16[256,512]{1,0:T(8,128)(2,1)} %get-tuple-element.47), channel_id=1, source_target_pairs={{0,32},{16,48},{32,0},{48,16},{64,96},{80,112},{96,64},{112,80},{1... | collective-permute-start | bytes 786440 | tf_op jit(solution)/shard_map/ppermute | solution.py:376
  146.9 11.9 %collective-permute-start.20 = (bf16[256,512]{1,0:T(8,128)(2,1)}, bf16[256,512]{1,0:T(8,128)(2,1)S(1)}, u32[]{:S(2)}, u32[]{:S(2)}) collective-permute-start(bf16[256,512]{1,0:T(8,128)(2,1)} %get-tuple-element.48), channel_id=1, source_target_pairs={{0,64},{16,80},{32,96},{48,112},{64,0},{80,16},{96,32},{112,48},{1... | collective-permute-start | bytes 786440 | tf_op jit(solution)/shard_map/ppermute | solution.py:376
  149.6 11.7 %collective-permute-start.21 = (bf16[256,512]{1,0:T(8,128)(2,1)}, bf16[256,512]{1,0:T(8,128)(2,1)S(1)}, u32[]{:S(2)}, u32[]{:S(2)}) collective-permute-start(bf16[256,512]{1,0:T(8,128)(2,1)} %get-tuple-element.49), channel_id=1, source_target_pairs={{0,96},{16,112},{32,64},{48,80},{64,32},{80,48},{96,0},{112,16},{1... | collective-permute-start | bytes 786440 | tf_op jit(solution)/shard_map/ppermute | solution.py:376
  150.1 19.6 %all-to-all-start.2 = ((bf16[8,3,128,128]{3,2,1,0:T(8,128)(2,1)}), bf16[8,3,128,128]{3,2,1,0:T(8,128)(2,1)S(1)}, u32[]{:S(2)}, u32[]{:S(2)}) async-start(bf16[8,3,128,128]{3,2,1,0:T(8,128)(2,1)} %gate.8), calls=%async_computation.2 | async-start | bytes 1572864 | tf_op jit(solution)/shard_map/all_to_all | solution.py:380
  162.5 6.6 %collective-permute-start.22 = (bf16[256,256]{1,0:T(8,128)(2,1)S(1)}, bf16[256,256]{1,0:T(8,128)(2,1)S(1)}, u32[]{:S(2)}, u32[]{:S(2)}) collective-permute-start(bf16[256,256]{1,0:T(8,128)(2,1)S(1)} %select_convert_fusion), channel_id=1, source_target_pairs={{0,8},{8,0},{1,9},{9,1},{2,10},{10,2},{3,11},{11,3},{4,12},{12,4},... | collective-permute-start | bytes 393224 | tf_op jit(solution)/shard_map/ppermute | solution.py:388
  (18 other events, 51.1 us)

commit v5 on v4

--- a/solution.py
+++ b/solution.py
@@ -96,22 +96,21 @@
     )(x)
 
 
-def assemble_kernel(first, second, out):
+def assemble_kernel(blocks, out):
     for g in range(N):
-        out[:, :, GW * g : GW * g + DH] = first[g]
-        out[:, :, GW * g + DH : GW * (g + 1)] = second[g]
-
-
-def assemble(first, second):
+        out[:, :, GW * g : GW * (g + 1)] = blocks[g]
+
+
+def assemble(blocks):
     return pl.pallas_call(
         assemble_kernel,
-        in_specs=[pl.BlockSpec(memory_space=pltpu.VMEM)] * 2,
+        in_specs=[pl.BlockSpec(memory_space=pltpu.VMEM)],
         out_specs=pl.BlockSpec(memory_space=pltpu.VMEM),
         out_shape=struct(3, ROWS, 2048),
         compiler_params=params(),
         cost_estimate=cost(0, 2 * 3 * ROWS * 2048 * 2),
         name="assemble",
-    )(first, second)
+    )(blocks)
 
 
 def upstream_kernel(cot, recv, out):
@@ -133,7 +132,7 @@
 
 
 def fwd_kernel(c_ref, blocks, *refs):
-    cat, att_own, att_send, probs_t = refs[-4:]
+    cat, att_own, att_send, *probs_t = refs[-5:]
     q = pl.program_id(0)
 
     @pl.when(q == 0)
@@ -155,7 +154,7 @@
         peak = jnp.max(scores, axis=0, keepdims=True)
         expo = jnp.exp(scores - peak)
         probs = (expo * (1.0 / jnp.sum(expo, axis=0, keepdims=True))).astype(BF16)
-        probs_t[h] = probs
+        probs_t[h][...] = probs
         att = jnp.transpose(dot(cat[2, :, cols], probs, 0, 0)).astype(BF16)
 
         @pl.when(q < 2)
@@ -186,10 +185,11 @@
                 pl.BlockSpec((3, SEQ, GW), lambda q, c_ref: (0, 0, 0)),
                 pl.BlockSpec((256, GW), low_half),
                 pl.BlockSpec((256, GW), high_half),
-                pl.BlockSpec((2, SEQ, 256), lambda q, c_ref: (0, 0, q)),
+                pl.BlockSpec((SEQ, 256), lambda q, c_ref: (0, q)),
+                pl.BlockSpec((SEQ, 256), lambda q, c_ref: (0, q)),
             ],
         ),
-        out_shape=[struct(3, SEQ, GW), struct(512, GW), struct(512, GW), struct(2, SEQ, SEQ)],
+        out_shape=[struct(3, SEQ, GW), struct(512, GW), struct(512, GW), struct(SEQ, SEQ), struct(SEQ, SEQ)],
         compiler_params=params(63 * 1024 * 1024),
         cost_estimate=cost(4 * 4 * SEQ * SEQ * DH, 10 << 20, 2 * SEQ * SEQ),
         name="attention_fwd",
@@ -202,7 +202,7 @@
     rows = pl.ds(pl.multiple_of(q * 256, 256), 256)
     queries = cat[0, rows, :]
     grad = jnp.where(q < 2, g_own[...], g_recv[...])
-    probs_low = probs_t[0]
+    probs_low = probs_t[...]
     grad_probs = dot(cat[2], grad, 1, 1)
     probs = probs_low.astype(F32)
     product = probs * grad_probs
@@ -235,7 +235,7 @@
             out[to, 2] = dv[ROWS * j : ROWS * (j + 1), :].astype(BF16)
 
 
-def attention_bwd(c, h, cat, probs_t, g_own, g_recv, after):
+def attention_bwd(c, h, cat, probs_t, g_own, g_recv, filled, after):
     return pl.pallas_call(
         bwd_kernel,
         grid_spec=pltpu.PrefetchScalarGridSpec(
@@ -243,19 +243,20 @@
             grid=(4,),
             in_specs=[
                 pl.BlockSpec((3, SEQ, DH), lambda q, c_ref: (0, 0, h)),
-                pl.BlockSpec((1, SEQ, 256), lambda q, c_ref: (h, 0, q)),
+                pl.BlockSpec((SEQ, 256), lambda q, c_ref: (0, q)),
                 pl.BlockSpec((256, DH), lambda q, c_ref: (jnp.minimum(q, 1), h)),
                 pl.BlockSpec((256, DH), lambda q, c_ref: (jnp.maximum(q - 2, 0), h)),
             ]
-            + [ANY] * len(after),
-            out_specs=pl.BlockSpec((N, 3, ROWS, DH), lambda q, c_ref: (0, 0, 0, 0)),
+            + [ANY] * (len(filled) + len(after)),
+            out_specs=pl.BlockSpec((N, 3, ROWS, DH), lambda q, c_ref: (0, 0, 0, h)),
             scratch_shapes=[pltpu.VMEM((SEQ, DH), BF16), pltpu.VMEM((SEQ, DH), F32), pltpu.VMEM((SEQ, DH), F32)],
         ),
-        out_shape=struct(N, 3, ROWS, DH),
+        out_shape=struct(N, 3, ROWS, GW),
+        input_output_aliases={5 + i: i for i in range(len(filled))},
         compiler_params=params(),
         cost_estimate=cost(4 * 2 * SEQ * SEQ * DH, 4 << 20),
         name="attention_bwd",
-    )(c, cat, probs_t, g_own, g_recv, *after)
+    )(c, cat, probs_t, g_own, g_recv, *filled, *after)
 
 
 def grad_kernel(*refs):
@@ -449,7 +450,7 @@
     u = upstream_rows(cot, cot_recv)
     y1, y3, z = by_xor(u, "ctx", 1), by_xor(u, "ctx", 3), by_xor(u, "ctx", 4)
     y2, zy1, zy3 = by_xor(y3, "ctx", 1), by_xor(y1, "ctx", 4), by_xor(z, "ctx", 3)
-    cat, att_own, att_send, probs_t = attention_fwd(c, blocks, [y1, y3, z])
+    cat, att_own, att_send, *probs_t = attention_fwd(c, blocks, [y1, y3, z])
     att_send, zy3 = gate([att_send, zy3], [y2, zy1])
     att_recv = other_strand(att_send)
     zy2 = by_xor(zy3, "ctx", 1)
@@ -464,21 +465,20 @@
     w_own, w_other = weight_part(d, att_own, att_recv, pieces, [g_own, p5])
     p3 = add(p3, r7, r2).astype(BF16)
     r3 = by_xor(p3, "ctx", 3)
-    grads0 = attention_bwd(c, 0, cat, probs_t, g_own, g_recv, [w_own, p3])
+    grads = attention_bwd(c, 0, cat, probs_t[0], g_own, g_recv, [], [w_own, p3])
     p1 = add(p1, r5).astype(BF16)
-    grads0, p4 = gate([grads0, p4], [p1, r3])
+    grads, p4, p1 = gate([grads, p4, p1], [r3])
     r1, r4 = by_xor(p1, "ctx", 1), by_xor(p4, "ctx", 4)
-    back0 = exchange(grads0)
-    grads1 = attention_bwd(c, 1, cat, probs_t, g_own, g_recv, [p1])
-    mixed_own = mix_sum([p0, r1, r3, r4], [grads1])
-    (grads1,) = gate([grads1], [back0])
-    back1 = exchange(grads1)
+    grads = attention_bwd(c, 1, cat, probs_t[1], g_own, g_recv, [grads], [])
+    mixed_own = mix_sum([p0, r1, r3, r4], [grads])
+    back = exchange(grads)
     mixed_recv = mirror(mixed_own)
     mixed = mix_out(mixed_own, mixed_recv)
-    qkv_grad = jnp.transpose(assemble(back0, back1), (1, 0, 2))
+    qkv_grad = jnp.transpose(assemble(back), (1, 0, 2))
 
     w_sum = weight_sum(w_own, by_xor(w_other, "dp", 1), [mixed_own])
-    w_recv = gate([by_xor(w_sum[x], "dp", 2 * x) for x in range(1, 4)], [mixed_recv])
+    w_recv = [by_xor(w_sum[x], "dp", 2 * x) for x in range(1, 4)]
+    w_recv = gate(w_recv, [mixed_recv])
     w_chip = add(w_sum[0], *w_recv)
     first, second = w_chip[:, :GW], w_chip[:, GW:]
     w_keep = jnp.where(s == 0, first, second)

time: 172 us -> 171 us (level)
  waiting for transfers between devices: 56.6 us -> 60.7 us
  local copies, waits for them, and re-layouts: 12.6 us -> 9.44 us
  starting transfers between devices: 51 us -> 48.9 us
    ppermute x18, waiting for transfers between devices: 36.2 us -> 42.9 us  [by_xor(): return lax.ppermute(x, axis, [(i, i ^ k) for i in range(N)])]
    all_to_all x3 -> x2, starting transfers between devices: 16 us -> 10.6 us  [exchange(): return lax.all_to_all(x, 'ctx', split_axis=0, concat_axis=0, tiled=True)]
    unnamed x48 -> x40, local copies, waits for them, and re-layouts: 11.5 us -> 8.36 us
    ppermute x3, waiting for transfers between devices: 11.1 us -> 8.55 us  [other_strand(): return lax.ppermute(x, 'strand', [(0, 1), (1, 0)])]
    ppermute x18, starting transfers between devices: 20.7 us -> 22.6 us  [by_xor(): return lax.ppermute(x, axis, [(i, i ^ k) for i in range(N)])]
  transfers between devices with their start and end apart: 26 -> 25, of which waited for: 10 -> 12; matrix products, arithmetic and copies ran while one was open for 1% -> 1% of each run, Pallas kernels for 27% -> 27%
where the time goes in v5:
time: 171 us; the launch traced here: 169 us
  waiting for transfers between devices  60.7 us (35%)
  starting transfers between devices  48.9 us (29%)
  Pallas kernels  47.8 us (28%)
  local copies, waits for them, and re-layouts  9.44 us (6%)
    ppermute x18, waiting for transfers between devices, by_xor(): return lax.ppermute(x, axis, [(i, i ^ k) for i in range(N)])  42.9 us
    ppermute x18, starting transfers between devices, by_xor(): return lax.ppermute(x, axis, [(i, i ^ k) for i in range(N)])  22.6 us
    pallas_call x2, Pallas kernels, attention_bwd(): pl.pallas_call(bwd_kernel, grid_spec=pltpu.PrefetchScalarGridSpec(num_sca...  13.7 us
    pallas_call x1, Pallas kernels, attention_fwd(): pl.pallas_call(fwd_kernel, grid_spec=pltpu.PrefetchScalarGridSpec(num_sca...  12.1 us
    all_to_all x2, starting transfers between devices, exchange(): return lax.all_to_all(x, 'ctx', split_axis=0, concat_axis=0, tiled=True)  10.6 us
    ppermute x2, starting transfers between devices, mirror(): lax.ppermute(x, ('strand', 'ctx'), [(i, 2 * N - 1 - i) for i in range(2 *...  9.65 us
    ppermute x2, waiting for transfers between devices, mirror(): lax.ppermute(x, ('strand', 'ctx'), [(i, 2 * N - 1 - i) for i in range(2 *...  9.25 us
    ppermute x3, waiting for transfers between devices, other_strand(): return lax.ppermute(x, 'strand', [(0, 1), (1, 0)])  8.55 us
  transfers between devices with their start and end apart: 25, of which 12 were waited for; matrix products, arithmetic and copies ran while one was open for 1% of the time, Pallas kernels for 27%

profile of v5, /device:TPU:8, one launch (start us, length us, event | category | flops | bytes accessed | tf_op | source)
XLA Modules:
  0.0 169.0 jit_solution(6982182588114372977)
XLA Ops:
  1.7 5.1 %collective-permute-start = (bf16[64,4096]{1,0:T(8,128)(2,1)S(1)}, bf16[64,4096]{1,0:T(8,128)(2,1)S(1)}, u32[]{:S(2)}, u32[]{:S(2)}) collective-permute-start(bf16[64,4096]{1,0:T(8,128)(2,1)S(1)} %slice_bitcast_fusion), channel_id=1, source_target_pairs={{0,15},{1,14},{2,13},{3,12},{4,11},{5,10},{6,9},{7,8},{8,7},{9,6},... | collective-permute-start | bytes 1572872 | tf_op jit(solution)/shard_map/ppermute | solution.py:385
  9.5 9.3 %collective-permute-done.refs_1_.recv = bf16[64,4096]{1,0:T(8,128)(2,1)S(1)} collective-permute-done((bf16[64,4096]{1,0:T(8,128)(2,1)S(1)}, bf16[64,4096]{1,0:T(8,128)(2,1)S(1)}, u32[]{:S(2)}, u32[]{:S(2)}) %collective-permute-start) | collective-permute-done | bytes 524320 | tf_op jit(solution)/shard_map/ppermute | solution.py:385
  18.8 6.2 %all-to-all-start = ((bf16[8,3,128,256]{3,2,1,0:T(8,128)(2,1)}), bf16[8,3,128,256]{3,2,1,0:T(8,128)(2,1)}, u32[]{:S(2)}, u32[]{:S(2)}) async-start(bf16[8,3,128,256]{3,2,1,0:T(8,128)(2,1)} %gate.4), calls=%async_computation | async-start | bytes 3145728 | tf_op jit(solution)/shard_map/all_to_all | solution.py:381
  25.5 1.5 collective-permute-start.2
  27.1 1.8 %collective-permute-start.1 = (bf16[64,4096]{1,0:T(8,128)(2,1)S(1)}, bf16[64,4096]{1,0:T(8,128)(2,1)}, u32[]{:S(2)}, u32[]{:S(2)}) collective-permute-start(bf16[64,4096]{1,0:T(8,128)(2,1)S(1)} %upstream_rows.1.refs_0_), channel_id=1, source_target_pairs={{0,1},{1,0},{2,3},{3,2},{4,5},{5,4},{6,7},{7,6},{8,9},{9,8},{10,11... | collective-permute-start | bytes 1572872 | tf_op jit(solution)/shard_map/ppermute | solution.py:377
  31.2 23.5 %collective-permute-done.2.refs_1_.refs_3_ = bf16[64,4096]{1,0:T(8,128)(2,1)} collective-permute-done((bf16[64,4096]{1,0:T(8,128)(2,1)S(1)}, bf16[64,4096]{1,0:T(8,128)(2,1)}, u32[]{:S(2)}, u32[]{:S(2)}) %collective-permute-start.2) | collective-permute-done | bytes 524320 | tf_op jit(solution)/shard_map/ppermute | solution.py:377
  54.7 1.8 %collective-permute-start.5 = (bf16[64,4096]{1,0:T(8,128)(2,1)}, bf16[64,4096]{1,0:T(8,128)(2,1)S(1)}, u32[]{:S(2)}, u32[]{:S(2)}) collective-permute-start(bf16[64,4096]{1,0:T(8,128)(2,1)} %collective-permute-done.2.refs_1_.refs_3_), channel_id=1, source_target_pairs={{0,1},{1,0},{2,3},{3,2},{4,5},{5,4},{6,7},{7,6},{8,9},{9,8},{10,11... | collective-permute-start | bytes 1572872 | tf_op jit(solution)/shard_map/ppermute | solution.py:377
  56.5 1.5 collective-permute-start.6
  58.0 12.1 %attention_fwd.1 = (bf16[3,1024,256]{2,1,0:T(8,128)(2,1)}, bf16[512,256]{1,0:T(8,128)(2,1)}, bf16[512,256]{1,0:T(8,128)(2,1)}, bf16[1024,1024]{1,0:T(8,128)(2,1)}, bf16[1024,1024]{1,0:T(8,128)(2,1)}) custom-call(s32[1]{0:T(128)} %bitcast.c_ref, bf16[8,3,128,256]{3,2,1,0:T(8,128)(2,1)} %all-to-all-done.blocks, ...), custom_call_target="tpu_custom_call" | custom-call | flops 2147483648 | bytes 10485760 | tf_op jit(solution)/shard_map/attention_fwd/pallas_call | solution.py:178
  72.2 3.0 %collective-permute-start.7 = (bf16[512,256]{1,0:T(8,128)(2,1)S(1)}, bf16[512,256]{1,0:T(8,128)(2,1)S(1)}, u32[]{:S(2)}, u32[]{:S(2)}) collective-permute-start(bf16[512,256]{1,0:T(8,128)(2,1)S(1)} %get-tuple-element.32), channel_id=1, source_target_pairs={{0,8},{8,0},{1,9},{9,1},{2,10},{10,2},{3,11},{11,3},{4,12},{12,4},... | collective-permute-start | bytes 786440 | tf_op jit(solution)/shard_map/ppermute | solution.py:389
  75.2 1.5 collective-permute-start.8
  76.7 3.4 %collective-permute-done.7.recv = bf16[512,256]{1,0:T(8,128)(2,1)S(1)} collective-permute-done((bf16[512,256]{1,0:T(8,128)(2,1)S(1)}, bf16[512,256]{1,0:T(8,128)(2,1)S(1)}, u32[]{:S(2)}, u32[]{:S(2)}) %collective-permute-start.7) | collective-permute-done | bytes 262176 | tf_op jit(solution)/shard_map/ppermute | solution.py:389
  80.8 4.9 %project.1 = (bf16[64,4096]{1,0:T(8,128)(2,1)}, bf16[64,4096]{1,0:T(8,128)(2,1)}, bf16[64,4096]{1,0:T(8,128)(2,1)}, bf16[64,4096]{1,0:T(8,128)(2,1)}, bf16[64,40...) custom-call(bf16[512,256]{1,0:T(8,128)(2,1)} %get-tuple-element.30.own, ...), custom_call_target="tpu_custom_call" | custom-call | flops 1073741824 | bytes 7340032 | tf_op jit(solution)/shard_map/project/pallas_call | solution.py:310
  85.7 1.5 collective-permute-start.10
  87.7 2.3 %collective-permute-start.12 = (bf16[64,4096]{1,0:T(8,128)(2,1)}, bf16[64,4096]{1,0:T(8,128)(2,1)S(1)}, u32[]{:S(2)}, u32[]{:S(2)}) collective-permute-start(bf16[64,4096]{1,0:T(8,128)(2,1)} %get-tuple-element.42), channel_id=1, source_target_pairs={{0,1},{1,0},{2,3},{3,2},{4,5},{5,4},{6,7},{7,6},{8,9},{9,8},{10,11... | collective-permute-start | bytes 1572872 | tf_op jit(solution)/shard_map/ppermute | solution.py:377
  91.1 1.6 copy-done.6
  93.7 4.2 %grad_attended.1.refs_8_.g_own = bf16[512,256]{1,0:T(8,128)(2,1)S(1)} custom-call(bf16[64,4096]{1,0:T(8,128)(2,1)S(1)} %copy-done.2, bf16[64,4096]{1,0:T(8,128)(2,1)} %collective-permute-done.1.refs_0_.refs_1_, bf16[64,4096]{1,0:T(8,128)(2,1)S(1)} %collective-permute-done.5.refs_2_, bf16[64,4096]{1,0:T(8,128)(2,1)} %collective-permute-done.2.refs_1_.refs_3_, ...), custom_call_target="tpu_custom_call" | custom-call | flops 1073741824 | bytes 7340032 | tf_op jit(solution)/shard_map/grad_attended/pallas_call | solution.py:284
  97.9 2.8 %collective-permute-start.9 = (bf16[512,256]{1,0:T(8,128)(2,1)S(1)}, bf16[512,256]{1,0:T(8,128)(2,1)S(1)}, u32[]{:S(2)}, u32[]{:S(2)}) collective-permute-start(bf16[512,256]{1,0:T(8,128)(2,1)S(1)} %grad_attended.1.refs_8_.g_own), channel_id=1, source_target_pairs={{0,8},{8,0},{1,9},{9,1},{2,10},{10,2},{3,11},{11,3},{4,12},{12,4},... | collective-permute-start | bytes 786440 | tf_op jit(solution)/shard_map/ppermute | solution.py:389
  102.8 5.0 %weight_part.1 = (bf16[4,256,512]{2,1,0:T(8,128)(2,1)S(1)}, bf16[4,256,512]{2,1,0:T(8,128)(2,1)}) custom-call(s32[1]{0:T(128)} %bitcast.5.d_ref, bf16[512,256]{1,0:T(8,128)(2,1)S(1)} %copy-done.13, bf16[512,256]{1,0:T(8,128)(2,1)S(1)} %copy-done.15, bf16[64,4096]{1,0:T(8,128)(2,1)S(1)} %copy-done.2, bf16[64,4096]{1,0:T(8,128)(2,1)} %collective-permute-done.1.refs_0_.refs_1_, ...), custom_call_target="tpu_custom_call" | custom-call | flops 1073741824 | bytes 7340032 | tf_op jit(solution)/shard_map/weight_part/pallas_call | solution.py:342
  108.7 6.9 %attention_bwd.2.refs_0_ = bf16[8,3,128,256]{3,2,1,0:T(8,128)(2,1)} custom-call(s32[1]{0:T(128)} %bitcast.c_ref, bf16[3,1024,256]{2,1,0:T(8,128)(2,1)S(1)} %copy-done, bf16[1024,1024]{1,0:T(8,128)(2,1)S(1)} %copy-done.8, bf16[512,256]{1,0:T(8,128)(2,1)S(1)} %grad_attended.1.refs_8_.g_own, bf16[512,256]{1,0:T(8,128)(2,1)S(1)} %collective-permute-done.9.g_recv, ...), custom_call_target="tpu_custom_call" | custom-call | flops 1073741824 | bytes 4194304 | tf_op jit(solution)/shard_map/attention_bwd/pallas_call | solution.py:239
  116.6 1.8 %collective-permute-start.15 = (bf16[64,4096]{1,0:T(8,128)(2,1)S(1)}, bf16[64,4096]{1,0:T(8,128)(2,1)S(1)}, u32[]{:S(2)}, u32[]{:S(2)}) collective-permute-start(bf16[64,4096]{1,0:T(8,128)(2,1)S(1)} %get-tuple-element.45), channel_id=1, source_target_pairs={{0,1},{1,0},{2,3},{3,2},{4,5},{5,4},{6,7},{7,6},{8,9},{9,8},{10,11... | collective-permute-start | bytes 1572872 | tf_op jit(solution)/shard_map/ppermute | solution.py:377
  118.8 6.9 %attention_bwd.3.refs_0_ = bf16[8,3,128,256]{3,2,1,0:T(8,128)(2,1)} custom-call(s32[1]{0:T(128)} %bitcast.c_ref, bf16[3,1024,256]{2,1,0:T(8,128)(2,1)S(1)} %copy-done, bf16[1024,1024]{1,0:T(8,128)(2,1)S(1)} %copy-done.7, bf16[512,256]{1,0:T(8,128)(2,1)S(1)} %grad_attended.1.refs_8_.g_own, ...), custom_call_target="tpu_custom_call", output_to_operand_aliasing={{}: (5, {})} | custom-call | flops 1073741824 | bytes 4194304 | tf_op jit(solution)/shard_map/attention_bwd/pallas_call | solution.py:239
  125.6 4.4 %collective-permute-done.15.r1 = bf16[64,4096]{1,0:T(8,128)(2,1)S(1)} collective-permute-done((bf16[64,4096]{1,0:T(8,128)(2,1)S(1)}, bf16[64,4096]{1,0:T(8,128)(2,1)S(1)}, u32[]{:S(2)}, u32[]{:S(2)}) %collective-permute-start.15) | collective-permute-done | bytes 524320 | tf_op jit(solution)/shard_map/ppermute | solution.py:377
  130.9 4.5 %collective-permute-start.17 = (bf16[64,4096]{1,0:T(8,128)(2,1)S(1)}, bf16[64,4096]{1,0:T(8,128)(2,1)}, u32[]{:S(2)}, u32[]{:S(2)}) collective-permute-start(bf16[64,4096]{1,0:T(8,128)(2,1)S(1)} %mix_sum.1.own.refs_0_), channel_id=1, source_target_pairs={{0,15},{1,14},{2,13},{3,12},{4,11},{5,10},{6,9},{7,8},{8,7},{9,6},... | collective-permute-start | bytes 1572872 | tf_op jit(solution)/shard_map/ppermute | solution.py:385
  135.4 4.4 %all-to-all-start.1 = ((bf16[8,3,128,256]{3,2,1,0:T(8,128)(2,1)}), bf16[8,3,128,256]{3,2,1,0:T(8,128)(2,1)S(1)}, u32[]{:S(2)}, u32[]{:S(2)}) async-start(bf16[8,3,128,256]{3,2,1,0:T(8,128)(2,1)} %attention_bwd.3.refs_0_), calls=%async_computation.1 | async-start | bytes 3145728 | tf_op jit(solution)/shard_map/all_to_all | solution.py:381
  139.8 2.2 %weight_sum.1 = (bf16[256,512]{1,0:T(8,128)(2,1)S(1)}, bf16[256,512]{1,0:T(8,128)(2,1)}, bf16[256,512]{1,0:T(8,128)(2,1)}, bf16[256,512]{1,0:T(8,128)(2,1)}) custom-call(bf16[4,256,512]{2,1,0:T(8,128)(2,1)S(1)} %copy-done.4, bf16[4,256,512]{2,1,0:T(8,128)(2,1)} %collective-permute-done.18.recv, bf16[64,4096]{1,0:T(8,128)(2,1)S(1)} %mix_sum.1.own.refs_0_), custom_call_target="tpu_custom_call" | custom-call | bytes 3145728 | tf_op jit(solution)/shard_map/weight_sum/pallas_call | solution.py:365
  143.4 2.7 %collective-permute-start.20 = (bf16[256,512]{1,0:T(8,128)(2,1)}, bf16[256,512]{1,0:T(8,128)(2,1)S(1)}, u32[]{:S(2)}, u32[]{:S(2)}) collective-permute-start(bf16[256,512]{1,0:T(8,128)(2,1)} %get-tuple-element.52), channel_id=1, source_target_pairs={{0,64},{16,80},{32,96},{48,112},{64,0},{80,16},{96,32},{112,48},{1... | collective-permute-start | bytes 786440 | tf_op jit(solution)/shard_map/ppermute | solution.py:377
  146.6 4.8 %collective-permute-done.19.refs_0_ = bf16[256,512]{1,0:T(8,128)(2,1)S(1)} collective-permute-done((bf16[256,512]{1,0:T(8,128)(2,1)}, bf16[256,512]{1,0:T(8,128)(2,1)S(1)}, u32[]{:S(2)}, u32[]{:S(2)}) %collective-permute-start.19) | collective-permute-done | bytes 262176 | tf_op jit(solution)/shard_map/ppermute | solution.py:377
  151.4 6.0 %collective-permute-done.20.refs_1_ = bf16[256,512]{1,0:T(8,128)(2,1)S(1)} collective-permute-done((bf16[256,512]{1,0:T(8,128)(2,1)}, bf16[256,512]{1,0:T(8,128)(2,1)S(1)}, u32[]{:S(2)}, u32[]{:S(2)}) %collective-permute-start.20) | collective-permute-done | bytes 262176 | tf_op jit(solution)/shard_map/ppermute | solution.py:377
  157.4 2.6 %collective-permute-done.21.refs_2_ = bf16[256,512]{1,0:T(8,128)(2,1)S(1)} collective-permute-done((bf16[256,512]{1,0:T(8,128)(2,1)}, bf16[256,512]{1,0:T(8,128)(2,1)S(1)}, u32[]{:S(2)}, u32[]{:S(2)}) %collective-permute-start.21) | collective-permute-done | bytes 262176 | tf_op jit(solution)/shard_map/ppermute | solution.py:377
  160.5 2.2 %mix_out.1 = bf16[128,4096]{1,0:T(8,128)(2,1)} custom-call(bf16[64,4096]{1,0:T(8,128)(2,1)S(1)} %mix_sum.1.own.refs_0_, bf16[64,4096]{1,0:T(8,128)(2,1)} %collective-permute-done.17.recv.refs_3_), custom_call_target="tpu_custom_call" | custom-call | bytes 2097152 | tf_op jit(solution)/shard_map/mix_out/pallas_call | solution.py:427
  162.7 4.2 %collective-permute-done.22 = bf16[256,256]{1,0:T(8,128)(2,1)S(1)} collective-permute-done((bf16[256,256]{1,0:T(8,128)(2,1)S(1)}, bf16[256,256]{1,0:T(8,128)(2,1)S(1)}, u32[]{:S(2)}, u32[]{:S(2)}) %collective-permute-start.22) | collective-permute-done | bytes 131104 | tf_op jit(solution)/shard_map/ppermute | solution.py:389
  (81 shorter events, 21.8 us)
Async XLA Ops:
  1.7 17.1 %collective-permute-start = (bf16[64,4096]{1,0:T(8,128)(2,1)S(1)}, bf16[64,4096]{1,0:T(8,128)(2,1)S(1)}, u32[]{:S(2)}, u32[]{:S(2)}) collective-permute-start(bf16[64,4096]{1,0:T(8,128)(2,1)S(1)} %slice_bitcast_fusion), channel_id=1, source_target_pairs={{0,15},{1,14},{2,13},{3,12},{4,11},{5,10},{6,9},{7,8},{8,7},{9,6},... | collective-permute-start | bytes 1572872 | tf_op jit(solution)/shard_map/ppermute | solution.py:385
  18.8 6.2 %copy-start.5 = (bf16[1,1,128,4096]{3,2,1,0:T(8,128)(2,1)S(1)}, bf16[1,1,128,4096]{3,2,1,0:T(8,128)(2,1)}, u32[]{:S(2)}) copy-start(bf16[1,1,128,4096]{3,2,1,0:T(8,128)(2,1)} %param.5) | copy-start | bytes 3145732
  18.8 39.2 %all-to-all-start = ((bf16[8,3,128,256]{3,2,1,0:T(8,128)(2,1)}), bf16[8,3,128,256]{3,2,1,0:T(8,128)(2,1)}, u32[]{:S(2)}, u32[]{:S(2)}) async-start(bf16[8,3,128,256]{3,2,1,0:T(8,128)(2,1)} %gate.4), calls=%async_computation | async-start | bytes 3145728 | tf_op jit(solution)/shard_map/all_to_all | solution.py:381
  25.5 29.1 %collective-permute-start.2 = (bf16[64,4096]{1,0:T(8,128)(2,1)S(1)}, bf16[64,4096]{1,0:T(8,128)(2,1)}, u32[]{:S(2)}, u32[]{:S(2)}) collective-permute-start(bf16[64,4096]{1,0:T(8,128)(2,1)S(1)} %upstream_rows.1.refs_0_), channel_id=1, source_target_pairs={{0,3},{1,2},{2,1},{3,0},{4,7},{5,6},{6,5},{7,4},{8,11},{9,10},{10,... | collective-permute-start | bytes 1572872 | tf_op jit(solution)/shard_map/ppermute | solution.py:377
  27.1 29.4 %collective-permute-start.1 = (bf16[64,4096]{1,0:T(8,128)(2,1)S(1)}, bf16[64,4096]{1,0:T(8,128)(2,1)}, u32[]{:S(2)}, u32[]{:S(2)}) collective-permute-start(bf16[64,4096]{1,0:T(8,128)(2,1)S(1)} %upstream_rows.1.refs_0_), channel_id=1, source_target_pairs={{0,1},{1,0},{2,3},{3,2},{4,5},{5,4},{6,7},{7,6},{8,9},{9,8},{10,11... | collective-permute-start | bytes 1572872 | tf_op jit(solution)/shard_map/ppermute | solution.py:377
  28.9 29.1 %collective-permute-start.3 = (bf16[64,4096]{1,0:T(8,128)(2,1)S(1)}, bf16[64,4096]{1,0:T(8,128)(2,1)}, u32[]{:S(2)}, u32[]{:S(2)}) collective-permute-start(bf16[64,4096]{1,0:T(8,128)(2,1)S(1)} %upstream_rows.1.refs_0_), channel_id=1, source_target_pairs={{0,4},{1,5},{2,6},{3,7},{4,0},{5,1},{6,2},{7,3},{8,12},{9,13},{10,... | collective-permute-start | bytes 1572872 | tf_op jit(solution)/shard_map/ppermute | solution.py:377
  54.7 15.4 %collective-permute-start.5 = (bf16[64,4096]{1,0:T(8,128)(2,1)}, bf16[64,4096]{1,0:T(8,128)(2,1)S(1)}, u32[]{:S(2)}, u32[]{:S(2)}) collective-permute-start(bf16[64,4096]{1,0:T(8,128)(2,1)} %collective-permute-done.2.refs_1_.refs_3_), channel_id=1, source_target_pairs={{0,1},{1,0},{2,3},{3,2},{4,5},{5,4},{6,7},{7,6},{8,9},{9,8},{10,11... | collective-permute-start | bytes 1572872 | tf_op jit(solution)/shard_map/ppermute | solution.py:377
  56.5 13.6 %collective-permute-start.6 = (bf16[64,4096]{1,0:T(8,128)(2,1)}, bf16[64,4096]{1,0:T(8,128)(2,1)}, u32[]{:S(2)}, u32[]{:S(2)}) collective-permute-start(bf16[64,4096]{1,0:T(8,128)(2,1)} %collective-permute-done.1.refs_0_.refs_1_), channel_id=1, source_target_pairs={{0,4},{1,5},{2,6},{3,7},{4,0},{5,1},{6,2},{7,3},{8,12},{9,13},{10,... | collective-permute-start | bytes 1572872 | tf_op jit(solution)/shard_map/ppermute | solution.py:377
  58.0 13.2 %collective-permute-start.4 = (bf16[64,4096]{1,0:T(8,128)(2,1)}, bf16[64,4096]{1,0:T(8,128)(2,1)}, u32[]{:S(2)}, u32[]{:S(2)}) collective-permute-start(bf16[64,4096]{1,0:T(8,128)(2,1)} %collective-permute-done.3.refs_2_.refs_4_), channel_id=1, source_target_pairs={{0,3},{1,2},{2,1},{3,0},{4,7},{5,6},{6,5},{7,4},{8,11},{9,10},{10,... | collective-permute-start | bytes 1572872 | tf_op jit(solution)/shard_map/ppermute | solution.py:377
  72.2 7.9 %collective-permute-start.7 = (bf16[512,256]{1,0:T(8,128)(2,1)S(1)}, bf16[512,256]{1,0:T(8,128)(2,1)S(1)}, u32[]{:S(2)}, u32[]{:S(2)}) collective-permute-start(bf16[512,256]{1,0:T(8,128)(2,1)S(1)} %get-tuple-element.32), channel_id=1, source_target_pairs={{0,8},{8,0},{1,9},{9,1},{2,10},{10,2},{3,11},{11,3},{4,12},{12,4},... | collective-permute-start | bytes 786440 | tf_op jit(solution)/shard_map/ppermute | solution.py:389
  75.2 14.8 %collective-permute-start.8 = (bf16[64,4096]{1,0:T(8,128)(2,1)}, bf16[64,4096]{1,0:T(8,128)(2,1)}, u32[]{:S(2)}, u32[]{:S(2)}) collective-permute-start(bf16[64,4096]{1,0:T(8,128)(2,1)} %get-tuple-element.36.refs_7_), channel_id=1, source_target_pairs={{0,1},{1,0},{2,3},{3,2},{4,5},{5,4},{6,7},{7,6},{8,9},{9,8},{10,11... | collective-permute-start | bytes 1572872 | tf_op jit(solution)/shard_map/ppermute | solution.py:377
  85.7 15.0 %collective-permute-start.10 = (bf16[64,4096]{1,0:T(8,128)(2,1)}, bf16[64,4096]{1,0:T(8,128)(2,1)S(1)}, u32[]{:S(2)}, u32[]{:S(2)}) collective-permute-start(bf16[64,4096]{1,0:T(8,128)(2,1)} %get-tuple-element.38), channel_id=1, source_target_pairs={{0,3},{1,2},{2,1},{3,0},{4,7},{5,6},{6,5},{7,4},{8,11},{9,10},{10,... | collective-permute-start | bytes 1572872 | tf_op jit(solution)/shard_map/ppermute | solution.py:377
  87.2 14.6 %collective-permute-start.11 = (bf16[64,4096]{1,0:T(8,128)(2,1)}, bf16[64,4096]{1,0:T(8,128)(2,1)S(1)}, u32[]{:S(2)}, u32[]{:S(2)}) collective-permute-start(bf16[64,4096]{1,0:T(8,128)(2,1)} %get-tuple-element.41), channel_id=1, source_target_pairs={{0,4},{1,5},{2,6},{3,7},{4,0},{5,1},{6,2},{7,3},{8,12},{9,13},{10,... | collective-permute-start | bytes 1572872 | tf_op jit(solution)/shard_map/ppermute | solution.py:377
  87.7 14.1 %collective-permute-start.12 = (bf16[64,4096]{1,0:T(8,128)(2,1)}, bf16[64,4096]{1,0:T(8,128)(2,1)S(1)}, u32[]{:S(2)}, u32[]{:S(2)}) collective-permute-start(bf16[64,4096]{1,0:T(8,128)(2,1)} %get-tuple-element.42), channel_id=1, source_target_pairs={{0,1},{1,0},{2,3},{3,2},{4,5},{5,4},{6,7},{7,6},{8,9},{9,8},{10,11... | collective-permute-start | bytes 1572872 | tf_op jit(solution)/shard_map/ppermute | solution.py:377
  93.7 7.0 %copy-start.18 = (bf16[64,4096]{1,0:T(8,128)(2,1)S(1)}, bf16[64,4096]{1,0:T(8,128)(2,1)}, u32[]{:S(2)}) copy-start(bf16[64,4096]{1,0:T(8,128)(2,1)} %get-tuple-element.37) | copy-start | bytes 1572868
  97.9 10.8 %collective-permute-start.9 = (bf16[512,256]{1,0:T(8,128)(2,1)S(1)}, bf16[512,256]{1,0:T(8,128)(2,1)S(1)}, u32[]{:S(2)}, u32[]{:S(2)}) collective-permute-start(bf16[512,256]{1,0:T(8,128)(2,1)S(1)} %grad_attended.1.refs_8_.g_own), channel_id=1, source_target_pairs={{0,8},{8,0},{1,9},{9,1},{2,10},{10,2},{3,11},{11,3},{4,12},{12,4},... | collective-permute-start | bytes 786440 | tf_op jit(solution)/shard_map/ppermute | solution.py:389
  100.8 14.9 %collective-permute-start.13 = (bf16[64,4096]{1,0:T(8,128)(2,1)S(1)}, bf16[64,4096]{1,0:T(8,128)(2,1)S(1)}, u32[]{:S(2)}, u32[]{:S(2)}) collective-permute-start(bf16[64,4096]{1,0:T(8,128)(2,1)S(1)} %add_convert_fusion.2.refs_9_), channel_id=1, source_target_pairs={{0,4},{1,5},{2,6},{3,7},{4,0},{5,1},{6,2},{7,3},{8,12},{9,13},{10,... | collective-permute-start | bytes 1572872 | tf_op jit(solution)/shard_map/ppermute | solution.py:377
  102.0 13.9 %collective-permute-start.14 = (bf16[64,4096]{1,0:T(8,128)(2,1)S(1)}, bf16[64,4096]{1,0:T(8,128)(2,1)S(1)}, u32[]{:S(2)}, u32[]{:S(2)}) collective-permute-start(bf16[64,4096]{1,0:T(8,128)(2,1)S(1)} %add_convert_fusion.1.refs_1_), channel_id=1, source_target_pairs={{0,3},{1,2},{2,1},{3,0},{4,7},{5,6},{6,5},{7,4},{8,11},{9,10},{10,... | collective-permute-start | bytes 1572872 | tf_op jit(solution)/shard_map/ppermute | solution.py:377
  102.8 5.9 %copy-start.8 = (bf16[1024,1024]{1,0:T(8,128)(2,1)S(1)}, bf16[1024,1024]{1,0:T(8,128)(2,1)}, u32[]{:S(2)}) copy-start(bf16[1024,1024]{1,0:T(8,128)(2,1)} %get-tuple-element.35.probs_t) | copy-start | bytes 6291460
  107.8 7.8 %copy-start.3 = (bf16[4,256,512]{2,1,0:T(8,128)(2,1)}, bf16[4,256,512]{2,1,0:T(8,128)(2,1)S(1)}, u32[]{:S(2)}) copy-start(bf16[4,256,512]{2,1,0:T(8,128)(2,1)S(1)} %get-tuple-element.39.refs_0_.own) | copy-start | bytes 3145732
  107.8 32.0 %collective-permute-start.18 = (bf16[4,256,512]{2,1,0:T(8,128)(2,1)}, bf16[4,256,512]{2,1,0:T(8,128)(2,1)}, u32[]{:S(2)}, u32[]{:S(2)}) collective-permute-start(bf16[4,256,512]{2,1,0:T(8,128)(2,1)} %get-tuple-element.49), channel_id=1, source_target_pairs={{0,16},{16,0},{32,48},{48,32},{64,80},{80,64},{96,112},{112,96},{1... | collective-permute-start | bytes 3145736 | tf_op jit(solution)/shard_map/ppermute | solution.py:377
  108.7 7.0 %copy-start.17 = (bf16[64,4096]{1,0:T(8,128)(2,1)S(1)}, bf16[64,4096]{1,0:T(8,128)(2,1)}, u32[]{:S(2)}) copy-start(bf16[64,4096]{1,0:T(8,128)(2,1)} %get-tuple-element.44) | copy-start | bytes 1572868
  116.6 13.4 %collective-permute-start.15 = (bf16[64,4096]{1,0:T(8,128)(2,1)S(1)}, bf16[64,4096]{1,0:T(8,128)(2,1)S(1)}, u32[]{:S(2)}, u32[]{:S(2)}) collective-permute-start(bf16[64,4096]{1,0:T(8,128)(2,1)S(1)} %get-tuple-element.45), channel_id=1, source_target_pairs={{0,1},{1,0},{2,3},{3,2},{4,5},{5,4},{6,7},{7,6},{8,9},{9,8},{10,11... | collective-permute-start | bytes 1572872 | tf_op jit(solution)/shard_map/ppermute | solution.py:377
  118.5 11.9 %collective-permute-start.16 = (bf16[64,4096]{1,0:T(8,128)(2,1)S(1)}, bf16[64,4096]{1,0:T(8,128)(2,1)S(1)}, u32[]{:S(2)}, u32[]{:S(2)}) collective-permute-start(bf16[64,4096]{1,0:T(8,128)(2,1)S(1)} %get-tuple-element.46), channel_id=1, source_target_pairs={{0,4},{1,5},{2,6},{3,7},{4,0},{5,1},{6,2},{7,3},{8,12},{9,13},{10,... | collective-permute-start | bytes 1572872 | tf_op jit(solution)/shard_map/ppermute | solution.py:377
  118.8 11.6 %copy-start.10 = (bf16[64,4096]{1,0:T(8,128)(2,1)S(1)}, bf16[64,4096]{1,0:T(8,128)(2,1)}, u32[]{:S(2)}) copy-start(bf16[64,4096]{1,0:T(8,128)(2,1)} %get-tuple-element.33.refs_9_.p0) | copy-start | bytes 1572868
  130.9 8.9 %copy-start.4 = (bf16[4,256,512]{2,1,0:T(8,128)(2,1)S(1)}, bf16[4,256,512]{2,1,0:T(8,128)(2,1)}, u32[]{:S(2)}) copy-start(bf16[4,256,512]{2,1,0:T(8,128)(2,1)} %copy-done.3) | copy-start | bytes 3145732
  130.9 29.1 %collective-permute-start.17 = (bf16[64,4096]{1,0:T(8,128)(2,1)S(1)}, bf16[64,4096]{1,0:T(8,128)(2,1)}, u32[]{:S(2)}, u32[]{:S(2)}) collective-permute-start(bf16[64,4096]{1,0:T(8,128)(2,1)S(1)} %mix_sum.1.own.refs_0_), channel_id=1, source_target_pairs={{0,15},{1,14},{2,13},{3,12},{4,11},{5,10},{6,9},{7,8},{8,7},{9,6},... | collective-permute-start | bytes 1572872 | tf_op jit(solution)/shard_map/ppermute | solution.py:385
  135.4 32.2 %all-to-all-start.1 = ((bf16[8,3,128,256]{3,2,1,0:T(8,128)(2,1)}), bf16[8,3,128,256]{3,2,1,0:T(8,128)(2,1)S(1)}, u32[]{:S(2)}, u32[]{:S(2)}) async-start(bf16[8,3,128,256]{3,2,1,0:T(8,128)(2,1)} %attention_bwd.3.refs_0_), calls=%async_computation.1 | async-start | bytes 3145728 | tf_op jit(solution)/shard_map/all_to_all | solution.py:381
  141.9 9.5 %collective-permute-start.19 = (bf16[256,512]{1,0:T(8,128)(2,1)}, bf16[256,512]{1,0:T(8,128)(2,1)S(1)}, u32[]{:S(2)}, u32[]{:S(2)}) collective-permute-start(bf16[256,512]{1,0:T(8,128)(2,1)} %get-tuple-element.51), channel_id=1, source_target_pairs={{0,32},{16,48},{32,0},{48,16},{64,96},{80,112},{96,64},{112,80},{1... | collective-permute-start | bytes 786440 | tf_op jit(solution)/shard_map/ppermute | solution.py:377
  143.4 14.0 %collective-permute-start.20 = (bf16[256,512]{1,0:T(8,128)(2,1)}, bf16[256,512]{1,0:T(8,128)(2,1)S(1)}, u32[]{:S(2)}, u32[]{:S(2)}) collective-permute-start(bf16[256,512]{1,0:T(8,128)(2,1)} %get-tuple-element.52), channel_id=1, source_target_pairs={{0,64},{16,80},{32,96},{48,112},{64,0},{80,16},{96,32},{112,48},{1... | collective-permute-start | bytes 786440 | tf_op jit(solution)/shard_map/ppermute | solution.py:377
  146.2 13.8 %collective-permute-start.21 = (bf16[256,512]{1,0:T(8,128)(2,1)}, bf16[256,512]{1,0:T(8,128)(2,1)S(1)}, u32[]{:S(2)}, u32[]{:S(2)}) collective-permute-start(bf16[256,512]{1,0:T(8,128)(2,1)} %get-tuple-element.53), channel_id=1, source_target_pairs={{0,96},{16,112},{32,64},{48,80},{64,32},{80,48},{96,0},{112,16},{1... | collective-permute-start | bytes 786440 | tf_op jit(solution)/shard_map/ppermute | solution.py:377
  160.2 6.7 %collective-permute-start.22 = (bf16[256,256]{1,0:T(8,128)(2,1)S(1)}, bf16[256,256]{1,0:T(8,128)(2,1)S(1)}, u32[]{:S(2)}, u32[]{:S(2)}) collective-permute-start(bf16[256,256]{1,0:T(8,128)(2,1)S(1)} %select_convert_fusion), channel_id=1, source_target_pairs={{0,8},{8,0},{1,9},{9,1},{2,10},{10,2},{3,11},{11,3},{4,12},{12,4},... | collective-permute-start | bytes 393224 | tf_op jit(solution)/shard_map/ppermute | solution.py:389
  (13 other events, 24.8 us)

commit v6 on v5

--- a/solution.py
+++ b/solution.py
@@ -470,13 +470,13 @@
     grads, p4, p1 = gate([grads, p4, p1], [r3])
     r1, r4 = by_xor(p1, "ctx", 1), by_xor(p4, "ctx", 4)
     grads = attention_bwd(c, 1, cat, probs_t[1], g_own, g_recv, [grads], [])
-    mixed_own = mix_sum([p0, r1, r3, r4], [grads])
+    w_sum = weight_sum(w_own, by_xor(w_other, "dp", 1), [grads])
+    mixed_own = mix_sum([p0, r1, r3, r4], [w_sum[0]])
     back = exchange(grads)
     mixed_recv = mirror(mixed_own)
     mixed = mix_out(mixed_own, mixed_recv)
     qkv_grad = jnp.transpose(assemble(back), (1, 0, 2))
 
-    w_sum = weight_sum(w_own, by_xor(w_other, "dp", 1), [mixed_own])
     w_recv = [by_xor(w_sum[x], "dp", 2 * x) for x in range(1, 4)]
     w_recv = gate(w_recv, [mixed_recv])
     w_chip = add(w_sum[0], *w_recv)

time: 171 us -> 169 us (0.988)
  Pallas kernels: 47.8 us -> 45 us
    ppermute x3, waiting for transfers between devices: 8.55 us -> 11.4 us  [other_strand(): return lax.ppermute(x, 'strand', [(0, 1), (1, 0)])]
  transfers between devices with their start and end apart: 25 -> 25, of which waited for: 12 -> 12; matrix products, arithmetic and copies ran while one was open for 1% -> 1% of each run, Pallas kernels for 27% -> 26%
where the time goes in v6:
time: 169 us; the launch traced here: 168 us
  waiting for transfers between devices  61.9 us (37%)
  starting transfers between devices  48.8 us (29%)
  Pallas kernels  45 us (27%)
  local copies, waits for them, and re-layouts  9.47 us (6%)
  other arithmetic  2.29 us (1%)
    ppermute x18, waiting for transfers between devices, by_xor(): return lax.ppermute(x, axis, [(i, i ^ k) for i in range(N)])  41.3 us
    ppermute x18, starting transfers between devices, by_xor(): return lax.ppermute(x, axis, [(i, i ^ k) for i in range(N)])  22.6 us
    pallas_call x2, Pallas kernels, attention_bwd(): pl.pallas_call(bwd_kernel, grid_spec=pltpu.PrefetchScalarGridSpec(num_sca...  13.7 us
    pallas_call x1, Pallas kernels, attention_fwd(): pl.pallas_call(fwd_kernel, grid_spec=pltpu.PrefetchScalarGridSpec(num_sca...  12.1 us
    ppermute x3, waiting for transfers between devices, other_strand(): return lax.ppermute(x, 'strand', [(0, 1), (1, 0)])  11.4 us
    all_to_all x2, starting transfers between devices, exchange(): return lax.all_to_all(x, 'ctx', split_axis=0, concat_axis=0, tiled=True)  10.6 us
    ppermute x2, starting transfers between devices, mirror(): lax.ppermute(x, ('strand', 'ctx'), [(i, 2 * N - 1 - i) for i in range(2 *...  9.65 us
    ppermute x2, waiting for transfers between devices, mirror(): lax.ppermute(x, ('strand', 'ctx'), [(i, 2 * N - 1 - i) for i in range(2 *...  9.25 us
  transfers between devices with their start and end apart: 25, of which 12 were waited for; matrix products, arithmetic and copies ran while one was open for 1% of the time, Pallas kernels for 26%

profile of v6, /device:TPU:8, one launch (start us, length us, event | category | flops | bytes accessed | tf_op | source)
XLA Modules:
  0.0 168.3 jit_solution(11999294190683622857)
XLA Ops:
  1.7 5.1 %collective-permute-start = (bf16[64,4096]{1,0:T(8,128)(2,1)S(1)}, bf16[64,4096]{1,0:T(8,128)(2,1)S(1)}, u32[]{:S(2)}, u32[]{:S(2)}) collective-permute-start(bf16[64,4096]{1,0:T(8,128)(2,1)S(1)} %slice_bitcast_fusion), channel_id=1, source_target_pairs={{0,15},{1,14},{2,13},{3,12},{4,11},{5,10},{6,9},{7,8},{8,7},{9,6},... | collective-permute-start | bytes 1572872 | tf_op jit(solution)/shard_map/ppermute | solution.py:385
  9.5 9.3 %collective-permute-done.refs_1_.recv = bf16[64,4096]{1,0:T(8,128)(2,1)S(1)} collective-permute-done((bf16[64,4096]{1,0:T(8,128)(2,1)S(1)}, bf16[64,4096]{1,0:T(8,128)(2,1)S(1)}, u32[]{:S(2)}, u32[]{:S(2)}) %collective-permute-start) | collective-permute-done | bytes 524320 | tf_op jit(solution)/shard_map/ppermute | solution.py:385
  18.8 6.2 %all-to-all-start = ((bf16[8,3,128,256]{3,2,1,0:T(8,128)(2,1)}), bf16[8,3,128,256]{3,2,1,0:T(8,128)(2,1)}, u32[]{:S(2)}, u32[]{:S(2)}) async-start(bf16[8,3,128,256]{3,2,1,0:T(8,128)(2,1)} %gate.4), calls=%async_computation | async-start | bytes 3145728 | tf_op jit(solution)/shard_map/all_to_all | solution.py:381
  25.5 1.5 collective-permute-start.2
  27.1 1.8 %collective-permute-start.1 = (bf16[64,4096]{1,0:T(8,128)(2,1)S(1)}, bf16[64,4096]{1,0:T(8,128)(2,1)}, u32[]{:S(2)}, u32[]{:S(2)}) collective-permute-start(bf16[64,4096]{1,0:T(8,128)(2,1)S(1)} %upstream_rows.1.refs_0_), channel_id=1, source_target_pairs={{0,1},{1,0},{2,3},{3,2},{4,5},{5,4},{6,7},{7,6},{8,9},{9,8},{10,11... | collective-permute-start | bytes 1572872 | tf_op jit(solution)/shard_map/ppermute | solution.py:377
  31.2 23.5 %collective-permute-done.2.refs_1_.refs_3_ = bf16[64,4096]{1,0:T(8,128)(2,1)} collective-permute-done((bf16[64,4096]{1,0:T(8,128)(2,1)S(1)}, bf16[64,4096]{1,0:T(8,128)(2,1)}, u32[]{:S(2)}, u32[]{:S(2)}) %collective-permute-start.2) | collective-permute-done | bytes 524320 | tf_op jit(solution)/shard_map/ppermute | solution.py:377
  54.7 1.8 %collective-permute-start.5 = (bf16[64,4096]{1,0:T(8,128)(2,1)}, bf16[64,4096]{1,0:T(8,128)(2,1)S(1)}, u32[]{:S(2)}, u32[]{:S(2)}) collective-permute-start(bf16[64,4096]{1,0:T(8,128)(2,1)} %collective-permute-done.2.refs_1_.refs_3_), channel_id=1, source_target_pairs={{0,1},{1,0},{2,3},{3,2},{4,5},{5,4},{6,7},{7,6},{8,9},{9,8},{10,11... | collective-permute-start | bytes 1572872 | tf_op jit(solution)/shard_map/ppermute | solution.py:377
  56.5 1.5 collective-permute-start.6
  58.0 12.1 %attention_fwd.1 = (bf16[3,1024,256]{2,1,0:T(8,128)(2,1)}, bf16[512,256]{1,0:T(8,128)(2,1)}, bf16[512,256]{1,0:T(8,128)(2,1)}, bf16[1024,1024]{1,0:T(8,128)(2,1)}, bf16[1024,1024]{1,0:T(8,128)(2,1)}) custom-call(s32[1]{0:T(128)} %bitcast.c_ref, bf16[8,3,128,256]{3,2,1,0:T(8,128)(2,1)} %all-to-all-done.blocks, ...), custom_call_target="tpu_custom_call" | custom-call | flops 2147483648 | bytes 10485760 | tf_op jit(solution)/shard_map/attention_fwd/pallas_call | solution.py:178
  72.2 3.0 %collective-permute-start.7 = (bf16[512,256]{1,0:T(8,128)(2,1)S(1)}, bf16[512,256]{1,0:T(8,128)(2,1)S(1)}, u32[]{:S(2)}, u32[]{:S(2)}) collective-permute-start(bf16[512,256]{1,0:T(8,128)(2,1)S(1)} %get-tuple-element.32), channel_id=1, source_target_pairs={{0,8},{8,0},{1,9},{9,1},{2,10},{10,2},{3,11},{11,3},{4,12},{12,4},... | collective-permute-start | bytes 786440 | tf_op jit(solution)/shard_map/ppermute | solution.py:389
  75.2 1.5 collective-permute-start.8
  76.7 3.4 %collective-permute-done.7.recv = bf16[512,256]{1,0:T(8,128)(2,1)S(1)} collective-permute-done((bf16[512,256]{1,0:T(8,128)(2,1)S(1)}, bf16[512,256]{1,0:T(8,128)(2,1)S(1)}, u32[]{:S(2)}, u32[]{:S(2)}) %collective-permute-start.7) | collective-permute-done | bytes 262176 | tf_op jit(solution)/shard_map/ppermute | solution.py:389
  80.8 4.9 %project.1 = (bf16[64,4096]{1,0:T(8,128)(2,1)}, bf16[64,4096]{1,0:T(8,128)(2,1)}, bf16[64,4096]{1,0:T(8,128)(2,1)}, bf16[64,4096]{1,0:T(8,128)(2,1)}, bf16[64,40...) custom-call(bf16[512,256]{1,0:T(8,128)(2,1)} %get-tuple-element.30.own, ...), custom_call_target="tpu_custom_call" | custom-call | flops 1073741824 | bytes 7340032 | tf_op jit(solution)/shard_map/project/pallas_call | solution.py:310
  85.7 1.5 collective-permute-start.10
  87.7 2.3 %collective-permute-start.12 = (bf16[64,4096]{1,0:T(8,128)(2,1)}, bf16[64,4096]{1,0:T(8,128)(2,1)S(1)}, u32[]{:S(2)}, u32[]{:S(2)}) collective-permute-start(bf16[64,4096]{1,0:T(8,128)(2,1)} %get-tuple-element.42), channel_id=1, source_target_pairs={{0,1},{1,0},{2,3},{3,2},{4,5},{5,4},{6,7},{7,6},{8,9},{9,8},{10,11... | collective-permute-start | bytes 1572872 | tf_op jit(solution)/shard_map/ppermute | solution.py:377
  91.1 1.6 copy-done.4
  93.7 4.2 %grad_attended.1.refs_8_.g_own = bf16[512,256]{1,0:T(8,128)(2,1)S(1)} custom-call(bf16[64,4096]{1,0:T(8,128)(2,1)S(1)} %copy-done.2, bf16[64,4096]{1,0:T(8,128)(2,1)} %collective-permute-done.1.refs_0_.refs_1_, bf16[64,4096]{1,0:T(8,128)(2,1)S(1)} %collective-permute-done.5.refs_2_, bf16[64,4096]{1,0:T(8,128)(2,1)} %collective-permute-done.2.refs_1_.refs_3_, ...), custom_call_target="tpu_custom_call" | custom-call | flops 1073741824 | bytes 7340032 | tf_op jit(solution)/shard_map/grad_attended/pallas_call | solution.py:284
  97.9 2.8 %collective-permute-start.9 = (bf16[512,256]{1,0:T(8,128)(2,1)S(1)}, bf16[512,256]{1,0:T(8,128)(2,1)S(1)}, u32[]{:S(2)}, u32[]{:S(2)}) collective-permute-start(bf16[512,256]{1,0:T(8,128)(2,1)S(1)} %grad_attended.1.refs_8_.g_own), channel_id=1, source_target_pairs={{0,8},{8,0},{1,9},{9,1},{2,10},{10,2},{3,11},{11,3},{4,12},{12,4},... | collective-permute-start | bytes 786440 | tf_op jit(solution)/shard_map/ppermute | solution.py:389
  102.8 4.2 %weight_part.1 = (bf16[4,256,512]{2,1,0:T(8,128)(2,1)S(1)}, bf16[4,256,512]{2,1,0:T(8,128)(2,1)S(1)}) custom-call(s32[1]{0:T(128)} %bitcast.5.d_ref, bf16[512,256]{1,0:T(8,128)(2,1)S(1)} %copy-done.12, bf16[512,256]{1,0:T(8,128)(2,1)S(1)} %copy-done.14, bf16[64,4096]{1,0:T(8,128)(2,1)S(1)} %copy-done.2, ...), custom_call_target="tpu_custom_call" | custom-call | flops 1073741824 | bytes 7340032 | tf_op jit(solution)/shard_map/weight_part/pallas_call | solution.py:342
  107.1 1.6 collective-permute-done.9.g_recv
  108.7 6.9 %attention_bwd.2.refs_0_ = bf16[8,3,128,256]{3,2,1,0:T(8,128)(2,1)} custom-call(s32[1]{0:T(128)} %bitcast.c_ref, bf16[3,1024,256]{2,1,0:T(8,128)(2,1)S(1)} %copy-done, bf16[1024,1024]{1,0:T(8,128)(2,1)S(1)} %copy-done.8, bf16[512,256]{1,0:T(8,128)(2,1)S(1)} %grad_attended.1.refs_8_.g_own, bf16[512,256]{1,0:T(8,128)(2,1)S(1)} %collective-permute-done.9.g_recv, ...), custom_call_target="tpu_custom_call" | custom-call | flops 1073741824 | bytes 4194304 | tf_op jit(solution)/shard_map/attention_bwd/pallas_call | solution.py:239
  116.6 1.8 %collective-permute-start.15 = (bf16[64,4096]{1,0:T(8,128)(2,1)S(1)}, bf16[64,4096]{1,0:T(8,128)(2,1)S(1)}, u32[]{:S(2)}, u32[]{:S(2)}) collective-permute-start(bf16[64,4096]{1,0:T(8,128)(2,1)S(1)} %get-tuple-element.45), channel_id=1, source_target_pairs={{0,1},{1,0},{2,3},{3,2},{4,5},{5,4},{6,7},{7,6},{8,9},{9,8},{10,11... | collective-permute-start | bytes 1572872 | tf_op jit(solution)/shard_map/ppermute | solution.py:377
  118.8 6.9 %attention_bwd.3.refs_0_ = bf16[8,3,128,256]{3,2,1,0:T(8,128)(2,1)} custom-call(s32[1]{0:T(128)} %bitcast.c_ref, bf16[3,1024,256]{2,1,0:T(8,128)(2,1)S(1)} %copy-done, bf16[1024,1024]{1,0:T(8,128)(2,1)S(1)} %copy-done.7, bf16[512,256]{1,0:T(8,128)(2,1)S(1)} %grad_attended.1.refs_8_.g_own, ...), custom_call_target="tpu_custom_call", output_to_operand_aliasing={{}: (5, {})} | custom-call | flops 1073741824 | bytes 4194304 | tf_op jit(solution)/shard_map/attention_bwd/pallas_call | solution.py:239
  126.6 2.8 %collective-permute-done.15.r1 = bf16[64,4096]{1,0:T(8,128)(2,1)S(1)} collective-permute-done((bf16[64,4096]{1,0:T(8,128)(2,1)S(1)}, bf16[64,4096]{1,0:T(8,128)(2,1)S(1)}, u32[]{:S(2)}, u32[]{:S(2)}) %collective-permute-start.15) | collective-permute-done | bytes 524320 | tf_op jit(solution)/shard_map/ppermute | solution.py:377
  130.2 4.5 %collective-permute-start.18 = (bf16[64,4096]{1,0:T(8,128)(2,1)S(1)}, bf16[64,4096]{1,0:T(8,128)(2,1)S(1)}, u32[]{:S(2)}, u32[]{:S(2)}) collective-permute-start(bf16[64,4096]{1,0:T(8,128)(2,1)S(1)} %mix_sum.1.own), channel_id=1, source_target_pairs={{0,15},{1,14},{2,13},{3,12},{4,11},{5,10},{6,9},{7,8},{8,7},{9,6},... | collective-permute-start | bytes 1572872 | tf_op jit(solution)/shard_map/ppermute | solution.py:385
  134.8 4.4 %all-to-all-start.1 = ((bf16[8,3,128,256]{3,2,1,0:T(8,128)(2,1)}), bf16[8,3,128,256]{3,2,1,0:T(8,128)(2,1)S(1)}, u32[]{:S(2)}, u32[]{:S(2)}) async-start(bf16[8,3,128,256]{3,2,1,0:T(8,128)(2,1)} %attention_bwd.3.refs_0_), calls=%async_computation.1 | async-start | bytes 3145728 | tf_op jit(solution)/shard_map/all_to_all | solution.py:381
  139.1 1.5 collective-permute-start.19
  140.6 2.7 %collective-permute-start.20 = (bf16[256,512]{1,0:T(8,128)(2,1)}, bf16[256,512]{1,0:T(8,128)(2,1)S(1)}, u32[]{:S(2)}, u32[]{:S(2)}) collective-permute-start(bf16[256,512]{1,0:T(8,128)(2,1)} %get-tuple-element.52), channel_id=1, source_target_pairs={{0,64},{16,80},{32,96},{48,112},{64,0},{80,16},{96,32},{112,48},{1... | collective-permute-start | bytes 786440 | tf_op jit(solution)/shard_map/ppermute | solution.py:377
  143.8 4.8 %collective-permute-done.19.refs_0_ = bf16[256,512]{1,0:T(8,128)(2,1)S(1)} collective-permute-done((bf16[256,512]{1,0:T(8,128)(2,1)}, bf16[256,512]{1,0:T(8,128)(2,1)S(1)}, u32[]{:S(2)}, u32[]{:S(2)}) %collective-permute-start.19) | collective-permute-done | bytes 262176 | tf_op jit(solution)/shard_map/ppermute | solution.py:377
  148.6 6.0 %collective-permute-done.20.refs_1_ = bf16[256,512]{1,0:T(8,128)(2,1)S(1)} collective-permute-done((bf16[256,512]{1,0:T(8,128)(2,1)}, bf16[256,512]{1,0:T(8,128)(2,1)S(1)}, u32[]{:S(2)}, u32[]{:S(2)}) %collective-permute-start.20) | collective-permute-done | bytes 262176 | tf_op jit(solution)/shard_map/ppermute | solution.py:377
  154.6 2.6 %collective-permute-done.21.refs_2_ = bf16[256,512]{1,0:T(8,128)(2,1)S(1)} collective-permute-done((bf16[256,512]{1,0:T(8,128)(2,1)}, bf16[256,512]{1,0:T(8,128)(2,1)S(1)}, u32[]{:S(2)}, u32[]{:S(2)}) %collective-permute-start.21) | collective-permute-done | bytes 262176 | tf_op jit(solution)/shard_map/ppermute | solution.py:377
  159.8 6.4 %collective-permute-done.22 = bf16[256,256]{1,0:T(8,128)(2,1)S(1)} collective-permute-done((bf16[256,256]{1,0:T(8,128)(2,1)S(1)}, bf16[256,256]{1,0:T(8,128)(2,1)S(1)}, u32[]{:S(2)}, u32[]{:S(2)}) %collective-permute-start.22) | collective-permute-done | bytes 131104 | tf_op jit(solution)/shard_map/ppermute | solution.py:389
  (81 shorter events, 22.6 us)
Async XLA Ops:
  1.7 17.1 %collective-permute-start = (bf16[64,4096]{1,0:T(8,128)(2,1)S(1)}, bf16[64,4096]{1,0:T(8,128)(2,1)S(1)}, u32[]{:S(2)}, u32[]{:S(2)}) collective-permute-start(bf16[64,4096]{1,0:T(8,128)(2,1)S(1)} %slice_bitcast_fusion), channel_id=1, source_target_pairs={{0,15},{1,14},{2,13},{3,12},{4,11},{5,10},{6,9},{7,8},{8,7},{9,6},... | collective-permute-start | bytes 1572872 | tf_op jit(solution)/shard_map/ppermute | solution.py:385
  18.8 6.2 %copy-start.3 = (bf16[1,1,128,4096]{3,2,1,0:T(8,128)(2,1)S(1)}, bf16[1,1,128,4096]{3,2,1,0:T(8,128)(2,1)}, u32[]{:S(2)}) copy-start(bf16[1,1,128,4096]{3,2,1,0:T(8,128)(2,1)} %param.5) | copy-start | bytes 3145732
  18.8 39.2 %all-to-all-start = ((bf16[8,3,128,256]{3,2,1,0:T(8,128)(2,1)}), bf16[8,3,128,256]{3,2,1,0:T(8,128)(2,1)}, u32[]{:S(2)}, u32[]{:S(2)}) async-start(bf16[8,3,128,256]{3,2,1,0:T(8,128)(2,1)} %gate.4), calls=%async_computation | async-start | bytes 3145728 | tf_op jit(solution)/shard_map/all_to_all | solution.py:381
  25.5 29.1 %collective-permute-start.2 = (bf16[64,4096]{1,0:T(8,128)(2,1)S(1)}, bf16[64,4096]{1,0:T(8,128)(2,1)}, u32[]{:S(2)}, u32[]{:S(2)}) collective-permute-start(bf16[64,4096]{1,0:T(8,128)(2,1)S(1)} %upstream_rows.1.refs_0_), channel_id=1, source_target_pairs={{0,3},{1,2},{2,1},{3,0},{4,7},{5,6},{6,5},{7,4},{8,11},{9,10},{10,... | collective-permute-start | bytes 1572872 | tf_op jit(solution)/shard_map/ppermute | solution.py:377
  27.1 29.4 %collective-permute-start.1 = (bf16[64,4096]{1,0:T(8,128)(2,1)S(1)}, bf16[64,4096]{1,0:T(8,128)(2,1)}, u32[]{:S(2)}, u32[]{:S(2)}) collective-permute-start(bf16[64,4096]{1,0:T(8,128)(2,1)S(1)} %upstream_rows.1.refs_0_), channel_id=1, source_target_pairs={{0,1},{1,0},{2,3},{3,2},{4,5},{5,4},{6,7},{7,6},{8,9},{9,8},{10,11... | collective-permute-start | bytes 1572872 | tf_op jit(solution)/shard_map/ppermute | solution.py:377
  28.9 29.1 %collective-permute-start.3 = (bf16[64,4096]{1,0:T(8,128)(2,1)S(1)}, bf16[64,4096]{1,0:T(8,128)(2,1)}, u32[]{:S(2)}, u32[]{:S(2)}) collective-permute-start(bf16[64,4096]{1,0:T(8,128)(2,1)S(1)} %upstream_rows.1.refs_0_), channel_id=1, source_target_pairs={{0,4},{1,5},{2,6},{3,7},{4,0},{5,1},{6,2},{7,3},{8,12},{9,13},{10,... | collective-permute-start | bytes 1572872 | tf_op jit(solution)/shard_map/ppermute | solution.py:377
  54.7 15.4 %collective-permute-start.5 = (bf16[64,4096]{1,0:T(8,128)(2,1)}, bf16[64,4096]{1,0:T(8,128)(2,1)S(1)}, u32[]{:S(2)}, u32[]{:S(2)}) collective-permute-start(bf16[64,4096]{1,0:T(8,128)(2,1)} %collective-permute-done.2.refs_1_.refs_3_), channel_id=1, source_target_pairs={{0,1},{1,0},{2,3},{3,2},{4,5},{5,4},{6,7},{7,6},{8,9},{9,8},{10,11... | collective-permute-start | bytes 1572872 | tf_op jit(solution)/shard_map/ppermute | solution.py:377
  56.5 13.6 %collective-permute-start.6 = (bf16[64,4096]{1,0:T(8,128)(2,1)}, bf16[64,4096]{1,0:T(8,128)(2,1)}, u32[]{:S(2)}, u32[]{:S(2)}) collective-permute-start(bf16[64,4096]{1,0:T(8,128)(2,1)} %collective-permute-done.1.refs_0_.refs_1_), channel_id=1, source_target_pairs={{0,4},{1,5},{2,6},{3,7},{4,0},{5,1},{6,2},{7,3},{8,12},{9,13},{10,... | collective-permute-start | bytes 1572872 | tf_op jit(solution)/shard_map/ppermute | solution.py:377
  58.0 13.2 %collective-permute-start.4 = (bf16[64,4096]{1,0:T(8,128)(2,1)}, bf16[64,4096]{1,0:T(8,128)(2,1)}, u32[]{:S(2)}, u32[]{:S(2)}) collective-permute-start(bf16[64,4096]{1,0:T(8,128)(2,1)} %collective-permute-done.3.refs_2_.refs_4_), channel_id=1, source_target_pairs={{0,3},{1,2},{2,1},{3,0},{4,7},{5,6},{6,5},{7,4},{8,11},{9,10},{10,... | collective-permute-start | bytes 1572872 | tf_op jit(solution)/shard_map/ppermute | solution.py:377
  72.2 7.9 %collective-permute-start.7 = (bf16[512,256]{1,0:T(8,128)(2,1)S(1)}, bf16[512,256]{1,0:T(8,128)(2,1)S(1)}, u32[]{:S(2)}, u32[]{:S(2)}) collective-permute-start(bf16[512,256]{1,0:T(8,128)(2,1)S(1)} %get-tuple-element.32), channel_id=1, source_target_pairs={{0,8},{8,0},{1,9},{9,1},{2,10},{10,2},{3,11},{11,3},{4,12},{12,4},... | collective-permute-start | bytes 786440 | tf_op jit(solution)/shard_map/ppermute | solution.py:389
  75.2 14.8 %collective-permute-start.8 = (bf16[64,4096]{1,0:T(8,128)(2,1)}, bf16[64,4096]{1,0:T(8,128)(2,1)}, u32[]{:S(2)}, u32[]{:S(2)}) collective-permute-start(bf16[64,4096]{1,0:T(8,128)(2,1)} %get-tuple-element.36.refs_7_), channel_id=1, source_target_pairs={{0,1},{1,0},{2,3},{3,2},{4,5},{5,4},{6,7},{7,6},{8,9},{9,8},{10,11... | collective-permute-start | bytes 1572872 | tf_op jit(solution)/shard_map/ppermute | solution.py:377
  85.7 15.0 %collective-permute-start.10 = (bf16[64,4096]{1,0:T(8,128)(2,1)}, bf16[64,4096]{1,0:T(8,128)(2,1)S(1)}, u32[]{:S(2)}, u32[]{:S(2)}) collective-permute-start(bf16[64,4096]{1,0:T(8,128)(2,1)} %get-tuple-element.38), channel_id=1, source_target_pairs={{0,3},{1,2},{2,1},{3,0},{4,7},{5,6},{6,5},{7,4},{8,11},{9,10},{10,... | collective-permute-start | bytes 1572872 | tf_op jit(solution)/shard_map/ppermute | solution.py:377
  87.2 14.6 %collective-permute-start.11 = (bf16[64,4096]{1,0:T(8,128)(2,1)}, bf16[64,4096]{1,0:T(8,128)(2,1)S(1)}, u32[]{:S(2)}, u32[]{:S(2)}) collective-permute-start(bf16[64,4096]{1,0:T(8,128)(2,1)} %get-tuple-element.41), channel_id=1, source_target_pairs={{0,4},{1,5},{2,6},{3,7},{4,0},{5,1},{6,2},{7,3},{8,12},{9,13},{10,... | collective-permute-start | bytes 1572872 | tf_op jit(solution)/shard_map/ppermute | solution.py:377
  87.7 14.1 %collective-permute-start.12 = (bf16[64,4096]{1,0:T(8,128)(2,1)}, bf16[64,4096]{1,0:T(8,128)(2,1)S(1)}, u32[]{:S(2)}, u32[]{:S(2)}) collective-permute-start(bf16[64,4096]{1,0:T(8,128)(2,1)} %get-tuple-element.42), channel_id=1, source_target_pairs={{0,1},{1,0},{2,3},{3,2},{4,5},{5,4},{6,7},{7,6},{8,9},{9,8},{10,11... | collective-permute-start | bytes 1572872 | tf_op jit(solution)/shard_map/ppermute | solution.py:377
  93.7 7.0 %copy-start.18 = (bf16[64,4096]{1,0:T(8,128)(2,1)S(1)}, bf16[64,4096]{1,0:T(8,128)(2,1)}, u32[]{:S(2)}) copy-start(bf16[64,4096]{1,0:T(8,128)(2,1)} %get-tuple-element.37) | copy-start | bytes 1572868
  97.9 3.9 %copy-start.19 = (bf16[64,4096]{1,0:T(8,128)(2,1)S(1)}, bf16[64,4096]{1,0:T(8,128)(2,1)}, u32[]{:S(2)}) copy-start(bf16[64,4096]{1,0:T(8,128)(2,1)} %get-tuple-element.40) | copy-start | bytes 1572868
  97.9 10.8 %collective-permute-start.9 = (bf16[512,256]{1,0:T(8,128)(2,1)S(1)}, bf16[512,256]{1,0:T(8,128)(2,1)S(1)}, u32[]{:S(2)}, u32[]{:S(2)}) collective-permute-start(bf16[512,256]{1,0:T(8,128)(2,1)S(1)} %grad_attended.1.refs_8_.g_own), channel_id=1, source_target_pairs={{0,8},{8,0},{1,9},{9,1},{2,10},{10,2},{3,11},{11,3},{4,12},{12,4},... | collective-permute-start | bytes 786440 | tf_op jit(solution)/shard_map/ppermute | solution.py:389
  100.8 14.9 %collective-permute-start.13 = (bf16[64,4096]{1,0:T(8,128)(2,1)S(1)}, bf16[64,4096]{1,0:T(8,128)(2,1)S(1)}, u32[]{:S(2)}, u32[]{:S(2)}) collective-permute-start(bf16[64,4096]{1,0:T(8,128)(2,1)S(1)} %add_convert_fusion.2.refs_9_), channel_id=1, source_target_pairs={{0,4},{1,5},{2,6},{3,7},{4,0},{5,1},{6,2},{7,3},{8,12},{9,13},{10,... | collective-permute-start | bytes 1572872 | tf_op jit(solution)/shard_map/ppermute | solution.py:377
  102.0 13.9 %collective-permute-start.14 = (bf16[64,4096]{1,0:T(8,128)(2,1)S(1)}, bf16[64,4096]{1,0:T(8,128)(2,1)S(1)}, u32[]{:S(2)}, u32[]{:S(2)}) collective-permute-start(bf16[64,4096]{1,0:T(8,128)(2,1)S(1)} %add_convert_fusion.1.refs_1_), channel_id=1, source_target_pairs={{0,3},{1,2},{2,1},{3,0},{4,7},{5,6},{6,5},{7,4},{8,11},{9,10},{10,... | collective-permute-start | bytes 1572872 | tf_op jit(solution)/shard_map/ppermute | solution.py:377
  102.8 5.9 %copy-start = (bf16[3,1024,256]{2,1,0:T(8,128)(2,1)S(1)}, bf16[3,1024,256]{2,1,0:T(8,128)(2,1)}, u32[]{:S(2)}) copy-start(bf16[3,1024,256]{2,1,0:T(8,128)(2,1)} %get-tuple-element.34.cat) | copy-start | bytes 4718596
  102.8 5.9 %copy-start.8 = (bf16[1024,1024]{1,0:T(8,128)(2,1)S(1)}, bf16[1024,1024]{1,0:T(8,128)(2,1)}, u32[]{:S(2)}) copy-start(bf16[1024,1024]{1,0:T(8,128)(2,1)} %get-tuple-element.35.probs_t) | copy-start | bytes 6291460
  107.1 18.6 %collective-permute-start.17 = (bf16[4,256,512]{2,1,0:T(8,128)(2,1)S(1)}, bf16[4,256,512]{2,1,0:T(8,128)(2,1)S(1)}, u32[]{:S(2)}, u32[]{:S(2)}) collective-permute-start(bf16[4,256,512]{2,1,0:T(8,128)(2,1)S(1)} %get-tuple-element.47), channel_id=1, source_target_pairs={{0,16},{16,0},{32,48},{48,32},{64,80},{80,64},{96,112},{112,96},{1... | collective-permute-start | bytes 3145736 | tf_op jit(solution)/shard_map/ppermute | solution.py:377
  108.7 7.0 %copy-start.17 = (bf16[64,4096]{1,0:T(8,128)(2,1)S(1)}, bf16[64,4096]{1,0:T(8,128)(2,1)}, u32[]{:S(2)}) copy-start(bf16[64,4096]{1,0:T(8,128)(2,1)} %get-tuple-element.44) | copy-start | bytes 1572868
  116.6 12.8 %collective-permute-start.15 = (bf16[64,4096]{1,0:T(8,128)(2,1)S(1)}, bf16[64,4096]{1,0:T(8,128)(2,1)S(1)}, u32[]{:S(2)}, u32[]{:S(2)}) collective-permute-start(bf16[64,4096]{1,0:T(8,128)(2,1)S(1)} %get-tuple-element.45), channel_id=1, source_target_pairs={{0,1},{1,0},{2,3},{3,2},{4,5},{5,4},{6,7},{7,6},{8,9},{9,8},{10,11... | collective-permute-start | bytes 1572872 | tf_op jit(solution)/shard_map/ppermute | solution.py:377
  118.5 11.3 %collective-permute-start.16 = (bf16[64,4096]{1,0:T(8,128)(2,1)S(1)}, bf16[64,4096]{1,0:T(8,128)(2,1)S(1)}, u32[]{:S(2)}, u32[]{:S(2)}) collective-permute-start(bf16[64,4096]{1,0:T(8,128)(2,1)S(1)} %get-tuple-element.46), channel_id=1, source_target_pairs={{0,4},{1,5},{2,6},{3,7},{4,0},{5,1},{6,2},{7,3},{8,12},{9,13},{10,... | collective-permute-start | bytes 1572872 | tf_op jit(solution)/shard_map/ppermute | solution.py:377
  125.6 4.1 %copy-start.6 = (bf16[64,4096]{1,0:T(8,128)(2,1)S(1)}, bf16[64,4096]{1,0:T(8,128)(2,1)}, u32[]{:S(2)}) copy-start(bf16[64,4096]{1,0:T(8,128)(2,1)} %get-tuple-element.33.refs_9_.p0) | copy-start | bytes 1572868
  130.2 26.9 %collective-permute-start.18 = (bf16[64,4096]{1,0:T(8,128)(2,1)S(1)}, bf16[64,4096]{1,0:T(8,128)(2,1)S(1)}, u32[]{:S(2)}, u32[]{:S(2)}) collective-permute-start(bf16[64,4096]{1,0:T(8,128)(2,1)S(1)} %mix_sum.1.own), channel_id=1, source_target_pairs={{0,15},{1,14},{2,13},{3,12},{4,11},{5,10},{6,9},{7,8},{8,7},{9,6},... | collective-permute-start | bytes 1572872 | tf_op jit(solution)/shard_map/ppermute | solution.py:385
  134.8 32.2 %all-to-all-start.1 = ((bf16[8,3,128,256]{3,2,1,0:T(8,128)(2,1)}), bf16[8,3,128,256]{3,2,1,0:T(8,128)(2,1)S(1)}, u32[]{:S(2)}, u32[]{:S(2)}) async-start(bf16[8,3,128,256]{3,2,1,0:T(8,128)(2,1)} %attention_bwd.3.refs_0_), calls=%async_computation.1 | async-start | bytes 3145728 | tf_op jit(solution)/shard_map/all_to_all | solution.py:381
  139.1 9.5 %collective-permute-start.19 = (bf16[256,512]{1,0:T(8,128)(2,1)}, bf16[256,512]{1,0:T(8,128)(2,1)S(1)}, u32[]{:S(2)}, u32[]{:S(2)}) collective-permute-start(bf16[256,512]{1,0:T(8,128)(2,1)} %get-tuple-element.51), channel_id=1, source_target_pairs={{0,32},{16,48},{32,0},{48,16},{64,96},{80,112},{96,64},{112,80},{1... | collective-permute-start | bytes 786440 | tf_op jit(solution)/shard_map/ppermute | solution.py:377
  140.6 14.0 %collective-permute-start.20 = (bf16[256,512]{1,0:T(8,128)(2,1)}, bf16[256,512]{1,0:T(8,128)(2,1)S(1)}, u32[]{:S(2)}, u32[]{:S(2)}) collective-permute-start(bf16[256,512]{1,0:T(8,128)(2,1)} %get-tuple-element.52), channel_id=1, source_target_pairs={{0,64},{16,80},{32,96},{48,112},{64,0},{80,16},{96,32},{112,48},{1... | collective-permute-start | bytes 786440 | tf_op jit(solution)/shard_map/ppermute | solution.py:377
  143.4 13.8 %collective-permute-start.21 = (bf16[256,512]{1,0:T(8,128)(2,1)}, bf16[256,512]{1,0:T(8,128)(2,1)S(1)}, u32[]{:S(2)}, u32[]{:S(2)}) collective-permute-start(bf16[256,512]{1,0:T(8,128)(2,1)} %copy-done.16), channel_id=1, source_target_pairs={{0,96},{16,112},{32,64},{48,80},{64,32},{80,48},{96,0},{112,16},{1... | collective-permute-start | bytes 786440 | tf_op jit(solution)/shard_map/ppermute | solution.py:377
  158.3 7.9 %collective-permute-start.22 = (bf16[256,256]{1,0:T(8,128)(2,1)S(1)}, bf16[256,256]{1,0:T(8,128)(2,1)S(1)}, u32[]{:S(2)}, u32[]{:S(2)}) collective-permute-start(bf16[256,256]{1,0:T(8,128)(2,1)S(1)} %select_convert_fusion), channel_id=1, source_target_pairs={{0,8},{8,0},{1,9},{9,1},{2,10},{10,2},{3,11},{11,3},{4,12},{12,4},... | collective-permute-start | bytes 393224 | tf_op jit(solution)/shard_map/ppermute | solution.py:389
  (13 other events, 22.3 us)

commit v7 on v6

--- a/solution.py
+++ b/solution.py
@@ -275,7 +275,7 @@
     def _():
         acc[...] += part
 
-    @pl.when(k == 3)
+    @pl.when(k == 1)
     def _():
         out[...] = acc[...].astype(BF16)
 
@@ -283,9 +283,9 @@
 def grad_attended(pieces, w, after):
     return pl.pallas_call(
         grad_kernel,
-        grid=(4,),
-        in_specs=[pl.BlockSpec((p.shape[0], 1024), lambda k: (0, k)) for p in pieces]
-        + [pl.BlockSpec((GW, 1024), lambda k: (0, k))]
+        grid=(2,),
+        in_specs=[pl.BlockSpec((p.shape[0], 2048), lambda k: (0, k)) for p in pieces]
+        + [pl.BlockSpec((GW, 2048), lambda k: (0, k))]
         + [ANY] * len(after),
         out_specs=pl.BlockSpec((512, GW), lambda k: (0, 0)),
         out_shape=struct(512, GW),
@@ -309,15 +309,15 @@
     rows = (HALF,) * N
     return pl.pallas_call(
         project_kernel,
-        grid=(4,),
+        grid=(2,),
         in_specs=[
             pl.BlockSpec((512, GW), lambda k: (0, 0)),
             pl.BlockSpec((512, GW), lambda k: (0, 0)),
-            pl.BlockSpec((GW, 1024), lambda k: (0, k)),
+            pl.BlockSpec((GW, 2048), lambda k: (0, k)),
         ],
-        out_specs=[pl.BlockSpec((r, 1024), lambda k: (0, k)) for r in rows],
+        out_specs=[pl.BlockSpec((r, 2048), lambda k: (0, k)) for r in rows],
         out_shape=[struct(r, D) for r in rows],
-        compiler_params=params(63 * 1024 * 1024),
+        compiler_params=params(63 * 2048 * 2048),
         cost_estimate=cost(2 * 512 * GW * D, 7 << 20),
         name="project",
     )(own, recv, w)

time: 169 us -> 169 us (level)
  Pallas kernels: 45 us -> 43.2 us
    pallas_call x2, Pallas kernels: 9.05 us -> 7.09 us  [the longest x1 4.04 us: project(): pl.pallas_call(project_kernel, grid=(2,), in_specs=[pl.BlockSpec((512, GW...]
    unnamed x40 -> x42, local copies, waits for them, and re-layouts: 8.39 us -> 9.52 us
  transfers between devices with their start and end apart: 25 -> 25, of which waited for: 12 -> 12; matrix products, arithmetic and copies ran while one was open for 1% -> 1% of each run, Pallas kernels for 26% -> 25%
where the time goes in v7:
time: 169 us; the launch traced here: 168 us
  waiting for transfers between devices  62.4 us (37%)
  starting transfers between devices  48.6 us (29%)
  Pallas kernels  43.2 us (26%)
  local copies, waits for them, and re-layouts  10.6 us (6%)
  other arithmetic  2.29 us (1%)
    ppermute x18, waiting for transfers between devices, by_xor(): return lax.ppermute(x, axis, [(i, i ^ k) for i in range(N)])  41.6 us
    ppermute x18, starting transfers between devices, by_xor(): return lax.ppermute(x, axis, [(i, i ^ k) for i in range(N)])  22.8 us
    pallas_call x2, Pallas kernels, attention_bwd(): pl.pallas_call(bwd_kernel, grid_spec=pltpu.PrefetchScalarGridSpec(num_sca...  13.7 us
    pallas_call x1, Pallas kernels, attention_fwd(): pl.pallas_call(fwd_kernel, grid_spec=pltpu.PrefetchScalarGridSpec(num_sca...  12.1 us
    ppermute x3, waiting for transfers between devices, other_strand(): return lax.ppermute(x, 'strand', [(0, 1), (1, 0)])  11.6 us
    all_to_all x2, starting transfers between devices, exchange(): return lax.all_to_all(x, 'ctx', split_axis=0, concat_axis=0, tiled=True)  10.6 us
    unnamed x42, local copies, waits for them, and re-layouts  9.52 us
    ppermute x2, starting transfers between devices, mirror(): lax.ppermute(x, ('strand', 'ctx'), [(i, 2 * N - 1 - i) for i in range(2 *...  9.3 us
  transfers between devices with their start and end apart: 25, of which 12 were waited for; matrix products, arithmetic and copies ran while one was open for 1% of the time, Pallas kernels for 25%

profile of v7, /device:TPU:8, one launch (start us, length us, event | category | flops | bytes accessed | tf_op | source)
XLA Modules:
  0.0 167.9 jit_solution(12043921068481384399)
XLA Ops:
  1.7 5.1 %collective-permute-start = (bf16[64,4096]{1,0:T(8,128)(2,1)S(1)}, bf16[64,4096]{1,0:T(8,128)(2,1)S(1)}, u32[]{:S(2)}, u32[]{:S(2)}) collective-permute-start(bf16[64,4096]{1,0:T(8,128)(2,1)S(1)} %slice_bitcast_fusion), channel_id=1, source_target_pairs={{0,15},{1,14},{2,13},{3,12},{4,11},{5,10},{6,9},{7,8},{8,7},{9,6},... | collective-permute-start | bytes 1572872 | tf_op jit(solution)/shard_map/ppermute | solution.py:385
  9.5 9.3 %collective-permute-done.refs_1_.recv = bf16[64,4096]{1,0:T(8,128)(2,1)S(1)} collective-permute-done((bf16[64,4096]{1,0:T(8,128)(2,1)S(1)}, bf16[64,4096]{1,0:T(8,128)(2,1)S(1)}, u32[]{:S(2)}, u32[]{:S(2)}) %collective-permute-start) | collective-permute-done | bytes 524320 | tf_op jit(solution)/shard_map/ppermute | solution.py:385
  18.8 6.2 %all-to-all-start = ((bf16[8,3,128,256]{3,2,1,0:T(8,128)(2,1)}), bf16[8,3,128,256]{3,2,1,0:T(8,128)(2,1)}, u32[]{:S(2)}, u32[]{:S(2)}) async-start(bf16[8,3,128,256]{3,2,1,0:T(8,128)(2,1)} %gate.4), calls=%async_computation | async-start | bytes 3145728 | tf_op jit(solution)/shard_map/all_to_all | solution.py:381
  25.5 1.5 collective-permute-start.2
  27.1 1.8 %collective-permute-start.1 = (bf16[64,4096]{1,0:T(8,128)(2,1)S(1)}, bf16[64,4096]{1,0:T(8,128)(2,1)}, u32[]{:S(2)}, u32[]{:S(2)}) collective-permute-start(bf16[64,4096]{1,0:T(8,128)(2,1)S(1)} %upstream_rows.1.refs_0_), channel_id=1, source_target_pairs={{0,1},{1,0},{2,3},{3,2},{4,5},{5,4},{6,7},{7,6},{8,9},{9,8},{10,11... | collective-permute-start | bytes 1572872 | tf_op jit(solution)/shard_map/ppermute | solution.py:377
  28.9 1.5 collective-permute-start.3
  31.2 23.5 %collective-permute-done.2.refs_1_.refs_3_ = bf16[64,4096]{1,0:T(8,128)(2,1)} collective-permute-done((bf16[64,4096]{1,0:T(8,128)(2,1)S(1)}, bf16[64,4096]{1,0:T(8,128)(2,1)}, u32[]{:S(2)}, u32[]{:S(2)}) %collective-permute-start.2) | collective-permute-done | bytes 524320 | tf_op jit(solution)/shard_map/ppermute | solution.py:377
  54.7 1.8 %collective-permute-start.5 = (bf16[64,4096]{1,0:T(8,128)(2,1)}, bf16[64,4096]{1,0:T(8,128)(2,1)S(1)}, u32[]{:S(2)}, u32[]{:S(2)}) collective-permute-start(bf16[64,4096]{1,0:T(8,128)(2,1)} %collective-permute-done.2.refs_1_.refs_3_), channel_id=1, source_target_pairs={{0,1},{1,0},{2,3},{3,2},{4,5},{5,4},{6,7},{7,6},{8,9},{9,8},{10,11... | collective-permute-start | bytes 1572872 | tf_op jit(solution)/shard_map/ppermute | solution.py:377
  56.5 1.5 collective-permute-start.6
  58.0 12.1 %attention_fwd.1 = (bf16[3,1024,256]{2,1,0:T(8,128)(2,1)}, bf16[512,256]{1,0:T(8,128)(2,1)}, bf16[512,256]{1,0:T(8,128)(2,1)}, bf16[1024,1024]{1,0:T(8,128)(2,1)}, bf16[1024,1024]{1,0:T(8,128)(2,1)}) custom-call(s32[1]{0:T(128)} %bitcast.c_ref, bf16[8,3,128,256]{3,2,1,0:T(8,128)(2,1)} %all-to-all-done.blocks, ...), custom_call_target="tpu_custom_call" | custom-call | flops 2147483648 | bytes 10485760 | tf_op jit(solution)/shard_map/attention_fwd/pallas_call | solution.py:178
  73.0 3.0 %collective-permute-start.7 = (bf16[512,256]{1,0:T(8,128)(2,1)S(1)}, bf16[512,256]{1,0:T(8,128)(2,1)}, u32[]{:S(2)}, u32[]{:S(2)}) collective-permute-start(bf16[512,256]{1,0:T(8,128)(2,1)S(1)} %get-tuple-element.32), channel_id=1, source_target_pairs={{0,8},{8,0},{1,9},{9,1},{2,10},{10,2},{3,11},{11,3},{4,12},{12,4},... | collective-permute-start | bytes 786440 | tf_op jit(solution)/shard_map/ppermute | solution.py:389
  76.0 1.5 collective-permute-start.8
  77.5 3.5 %collective-permute-done.7.recv = bf16[512,256]{1,0:T(8,128)(2,1)} collective-permute-done((bf16[512,256]{1,0:T(8,128)(2,1)S(1)}, bf16[512,256]{1,0:T(8,128)(2,1)}, u32[]{:S(2)}, u32[]{:S(2)}) %collective-permute-start.7) | collective-permute-done | bytes 262176 | tf_op jit(solution)/shard_map/ppermute | solution.py:389
  81.0 4.0 %project.1 = (bf16[64,4096]{1,0:T(8,128)(2,1)}, bf16[64,4096]{1,0:T(8,128)(2,1)}, bf16[64,4096]{1,0:T(8,128)(2,1)}, bf16[64,4096]{1,0:T(8,128)(2,1)}, bf16[64,40...) custom-call(bf16[512,256]{1,0:T(8,128)(2,1)} %get-tuple-element.30.own, ...), custom_call_target="tpu_custom_call" | custom-call | flops 1073741824 | bytes 7340032 | tf_op jit(solution)/shard_map/project/pallas_call | solution.py:310
  85.1 1.5 collective-permute-start.10
  87.1 2.3 %collective-permute-start.12 = (bf16[64,4096]{1,0:T(8,128)(2,1)}, bf16[64,4096]{1,0:T(8,128)(2,1)S(1)}, u32[]{:S(2)}, u32[]{:S(2)}) collective-permute-start(bf16[64,4096]{1,0:T(8,128)(2,1)} %get-tuple-element.42), channel_id=1, source_target_pairs={{0,1},{1,0},{2,3},{3,2},{4,5},{5,4},{6,7},{7,6},{8,9},{9,8},{10,11... | collective-permute-start | bytes 1572872 | tf_op jit(solution)/shard_map/ppermute | solution.py:377
  91.5 1.6 copy-done.7
  94.1 3.0 %grad_attended.1.refs_8_.g_own = bf16[512,256]{1,0:T(8,128)(2,1)S(1)} custom-call(bf16[64,4096]{1,0:T(8,128)(2,1)S(1)} %copy-done.5, bf16[64,4096]{1,0:T(8,128)(2,1)} %collective-permute-done.1.refs_0_.refs_1_, bf16[64,4096]{1,0:T(8,128)(2,1)S(1)} %copy-done.2, bf16[64,4096]{1,0:T(8,128)(2,1)} %collective-permute-done.2.refs_1_.refs_3_, ...), custom_call_target="tpu_custom_call" | custom-call | flops 1073741824 | bytes 7340032 | tf_op jit(solution)/shard_map/grad_attended/pallas_call | solution.py:284
  97.2 2.8 %collective-permute-start.9 = (bf16[512,256]{1,0:T(8,128)(2,1)S(1)}, bf16[512,256]{1,0:T(8,128)(2,1)S(1)}, u32[]{:S(2)}, u32[]{:S(2)}) collective-permute-start(bf16[512,256]{1,0:T(8,128)(2,1)S(1)} %grad_attended.1.refs_8_.g_own), channel_id=1, source_target_pairs={{0,8},{8,0},{1,9},{9,1},{2,10},{10,2},{3,11},{11,3},{4,12},{12,4},... | collective-permute-start | bytes 786440 | tf_op jit(solution)/shard_map/ppermute | solution.py:389
  102.1 4.4 %weight_part.1 = (bf16[4,256,512]{2,1,0:T(8,128)(2,1)S(1)}, bf16[4,256,512]{2,1,0:T(8,128)(2,1)S(1)}) custom-call(s32[1]{0:T(128)} %bitcast.5.d_ref, bf16[512,256]{1,0:T(8,128)(2,1)S(1)} %copy-done.15, bf16[512,256]{1,0:T(8,128)(2,1)} %collective-permute-done.7.recv, bf16[64,4096]{1,0:T(8,128)(2,1)S(1)} %copy-done.5, ...), custom_call_target="tpu_custom_call" | custom-call | flops 1073741824 | bytes 7340032 | tf_op jit(solution)/shard_map/weight_part/pallas_call | solution.py:342
  108.0 6.9 %attention_bwd.2.refs_0_ = bf16[8,3,128,256]{3,2,1,0:T(8,128)(2,1)} custom-call(s32[1]{0:T(128)} %bitcast.c_ref, bf16[3,1024,256]{2,1,0:T(8,128)(2,1)S(1)} %copy-done, bf16[1024,1024]{1,0:T(8,128)(2,1)S(1)} %copy-done.11, bf16[512,256]{1,0:T(8,128)(2,1)S(1)} %grad_attended.1.refs_8_.g_own, bf16[512,256]{1,0:T(8,128)(2,1)S(1)} %collective-permute-done.9.g_recv, ...), custom_call_target="tpu_custom_call" | custom-call | flops 1073741824 | bytes 4194304 | tf_op jit(solution)/shard_map/attention_bwd/pallas_call | solution.py:239
  115.9 1.7 %collective-permute-start.15 = (bf16[64,4096]{1,0:T(8,128)(2,1)S(1)}, bf16[64,4096]{1,0:T(8,128)(2,1)S(1)}, u32[]{:S(2)}, u32[]{:S(2)}) collective-permute-start(bf16[64,4096]{1,0:T(8,128)(2,1)S(1)} %get-tuple-element.45), channel_id=1, source_target_pairs={{0,1},{1,0},{2,3},{3,2},{4,5},{5,4},{6,7},{7,6},{8,9},{9,8},{10,11... | collective-permute-start | bytes 1572872 | tf_op jit(solution)/shard_map/ppermute | solution.py:377
  118.2 6.9 %attention_bwd.3.refs_0_ = bf16[8,3,128,256]{3,2,1,0:T(8,128)(2,1)} custom-call(s32[1]{0:T(128)} %bitcast.c_ref, bf16[3,1024,256]{2,1,0:T(8,128)(2,1)S(1)} %copy-done, bf16[1024,1024]{1,0:T(8,128)(2,1)S(1)} %copy-done.10, bf16[512,256]{1,0:T(8,128)(2,1)S(1)} %grad_attended.1.refs_8_.g_own, ...), custom_call_target="tpu_custom_call", output_to_operand_aliasing={{}: (5, {})} | custom-call | flops 1073741824 | bytes 4194304 | tf_op jit(solution)/shard_map/attention_bwd/pallas_call | solution.py:239
  126.0 2.8 %collective-permute-done.15.r1 = bf16[64,4096]{1,0:T(8,128)(2,1)S(1)} collective-permute-done((bf16[64,4096]{1,0:T(8,128)(2,1)S(1)}, bf16[64,4096]{1,0:T(8,128)(2,1)S(1)}, u32[]{:S(2)}, u32[]{:S(2)}) %collective-permute-start.15) | collective-permute-done | bytes 524320 | tf_op jit(solution)/shard_map/ppermute | solution.py:377
  129.9 4.2 %collective-permute-start.18 = (bf16[64,4096]{1,0:T(8,128)(2,1)S(1)}, bf16[64,4096]{1,0:T(8,128)(2,1)S(1)}, u32[]{:S(2)}, u32[]{:S(2)}) collective-permute-start(bf16[64,4096]{1,0:T(8,128)(2,1)S(1)} %mix_sum.1.own), channel_id=1, source_target_pairs={{0,15},{1,14},{2,13},{3,12},{4,11},{5,10},{6,9},{7,8},{8,7},{9,6},... | collective-permute-start | bytes 1572872 | tf_op jit(solution)/shard_map/ppermute | solution.py:385
  134.1 4.4 %all-to-all-start.1 = ((bf16[8,3,128,256]{3,2,1,0:T(8,128)(2,1)}), bf16[8,3,128,256]{3,2,1,0:T(8,128)(2,1)S(1)}, u32[]{:S(2)}, u32[]{:S(2)}) async-start(bf16[8,3,128,256]{3,2,1,0:T(8,128)(2,1)} %attention_bwd.3.refs_0_), calls=%async_computation.1 | async-start | bytes 3145728 | tf_op jit(solution)/shard_map/all_to_all | solution.py:381
  138.5 1.5 collective-permute-start.19
  139.9 2.7 %collective-permute-start.20 = (bf16[256,512]{1,0:T(8,128)(2,1)}, bf16[256,512]{1,0:T(8,128)(2,1)S(1)}, u32[]{:S(2)}, u32[]{:S(2)}) collective-permute-start(bf16[256,512]{1,0:T(8,128)(2,1)} %get-tuple-element.52), channel_id=1, source_target_pairs={{0,64},{16,80},{32,96},{48,112},{64,0},{80,16},{96,32},{112,48},{1... | collective-permute-start | bytes 786440 | tf_op jit(solution)/shard_map/ppermute | solution.py:377
  143.2 4.8 %collective-permute-done.19.refs_0_ = bf16[256,512]{1,0:T(8,128)(2,1)S(1)} collective-permute-done((bf16[256,512]{1,0:T(8,128)(2,1)}, bf16[256,512]{1,0:T(8,128)(2,1)S(1)}, u32[]{:S(2)}, u32[]{:S(2)}) %collective-permute-start.19) | collective-permute-done | bytes 262176 | tf_op jit(solution)/shard_map/ppermute | solution.py:377
  147.9 6.0 %collective-permute-done.20.refs_1_ = bf16[256,512]{1,0:T(8,128)(2,1)S(1)} collective-permute-done((bf16[256,512]{1,0:T(8,128)(2,1)}, bf16[256,512]{1,0:T(8,128)(2,1)S(1)}, u32[]{:S(2)}, u32[]{:S(2)}) %collective-permute-start.20) | collective-permute-done | bytes 262176 | tf_op jit(solution)/shard_map/ppermute | solution.py:377
  153.9 2.6 %collective-permute-done.21.refs_2_ = bf16[256,512]{1,0:T(8,128)(2,1)S(1)} collective-permute-done((bf16[256,512]{1,0:T(8,128)(2,1)}, bf16[256,512]{1,0:T(8,128)(2,1)S(1)}, u32[]{:S(2)}, u32[]{:S(2)}) %collective-permute-start.21) | collective-permute-done | bytes 262176 | tf_op jit(solution)/shard_map/ppermute | solution.py:377
  159.2 6.6 %collective-permute-done.22 = bf16[256,256]{1,0:T(8,128)(2,1)S(1)} collective-permute-done((bf16[256,256]{1,0:T(8,128)(2,1)S(1)}, bf16[256,256]{1,0:T(8,128)(2,1)S(1)}, u32[]{:S(2)}, u32[]{:S(2)}) %collective-permute-start.22) | collective-permute-done | bytes 131104 | tf_op jit(solution)/shard_map/ppermute | solution.py:389
  (83 shorter events, 24.2 us)
Async XLA Ops:
  1.7 17.1 %collective-permute-start = (bf16[64,4096]{1,0:T(8,128)(2,1)S(1)}, bf16[64,4096]{1,0:T(8,128)(2,1)S(1)}, u32[]{:S(2)}, u32[]{:S(2)}) collective-permute-start(bf16[64,4096]{1,0:T(8,128)(2,1)S(1)} %slice_bitcast_fusion), channel_id=1, source_target_pairs={{0,15},{1,14},{2,13},{3,12},{4,11},{5,10},{6,9},{7,8},{8,7},{9,6},... | collective-permute-start | bytes 1572872 | tf_op jit(solution)/shard_map/ppermute | solution.py:385
  18.8 6.2 %copy-start.6 = (bf16[1,1,128,4096]{3,2,1,0:T(8,128)(2,1)S(1)}, bf16[1,1,128,4096]{3,2,1,0:T(8,128)(2,1)}, u32[]{:S(2)}) copy-start(bf16[1,1,128,4096]{3,2,1,0:T(8,128)(2,1)} %param.5) | copy-start | bytes 3145732
  18.8 39.2 %all-to-all-start = ((bf16[8,3,128,256]{3,2,1,0:T(8,128)(2,1)}), bf16[8,3,128,256]{3,2,1,0:T(8,128)(2,1)}, u32[]{:S(2)}, u32[]{:S(2)}) async-start(bf16[8,3,128,256]{3,2,1,0:T(8,128)(2,1)} %gate.4), calls=%async_computation | async-start | bytes 3145728 | tf_op jit(solution)/shard_map/all_to_all | solution.py:381
  25.5 29.1 %collective-permute-start.2 = (bf16[64,4096]{1,0:T(8,128)(2,1)S(1)}, bf16[64,4096]{1,0:T(8,128)(2,1)}, u32[]{:S(2)}, u32[]{:S(2)}) collective-permute-start(bf16[64,4096]{1,0:T(8,128)(2,1)S(1)} %upstream_rows.1.refs_0_), channel_id=1, source_target_pairs={{0,3},{1,2},{2,1},{3,0},{4,7},{5,6},{6,5},{7,4},{8,11},{9,10},{10,... | collective-permute-start | bytes 1572872 | tf_op jit(solution)/shard_map/ppermute | solution.py:377
  27.1 29.4 %collective-permute-start.1 = (bf16[64,4096]{1,0:T(8,128)(2,1)S(1)}, bf16[64,4096]{1,0:T(8,128)(2,1)}, u32[]{:S(2)}, u32[]{:S(2)}) collective-permute-start(bf16[64,4096]{1,0:T(8,128)(2,1)S(1)} %upstream_rows.1.refs_0_), channel_id=1, source_target_pairs={{0,1},{1,0},{2,3},{3,2},{4,5},{5,4},{6,7},{7,6},{8,9},{9,8},{10,11... | collective-permute-start | bytes 1572872 | tf_op jit(solution)/shard_map/ppermute | solution.py:377
  28.9 29.2 %collective-permute-start.3 = (bf16[64,4096]{1,0:T(8,128)(2,1)S(1)}, bf16[64,4096]{1,0:T(8,128)(2,1)}, u32[]{:S(2)}, u32[]{:S(2)}) collective-permute-start(bf16[64,4096]{1,0:T(8,128)(2,1)S(1)} %upstream_rows.1.refs_0_), channel_id=1, source_target_pairs={{0,4},{1,5},{2,6},{3,7},{4,0},{5,1},{6,2},{7,3},{8,12},{9,13},{10,... | collective-permute-start | bytes 1572872 | tf_op jit(solution)/shard_map/ppermute | solution.py:377
  54.7 15.4 %collective-permute-start.5 = (bf16[64,4096]{1,0:T(8,128)(2,1)}, bf16[64,4096]{1,0:T(8,128)(2,1)S(1)}, u32[]{:S(2)}, u32[]{:S(2)}) collective-permute-start(bf16[64,4096]{1,0:T(8,128)(2,1)} %collective-permute-done.2.refs_1_.refs_3_), channel_id=1, source_target_pairs={{0,1},{1,0},{2,3},{3,2},{4,5},{5,4},{6,7},{7,6},{8,9},{9,8},{10,11... | collective-permute-start | bytes 1572872 | tf_op jit(solution)/shard_map/ppermute | solution.py:377
  56.5 13.6 %collective-permute-start.6 = (bf16[64,4096]{1,0:T(8,128)(2,1)}, bf16[64,4096]{1,0:T(8,128)(2,1)}, u32[]{:S(2)}, u32[]{:S(2)}) collective-permute-start(bf16[64,4096]{1,0:T(8,128)(2,1)} %collective-permute-done.1.refs_0_.refs_1_), channel_id=1, source_target_pairs={{0,4},{1,5},{2,6},{3,7},{4,0},{5,1},{6,2},{7,3},{8,12},{9,13},{10,... | collective-permute-start | bytes 1572872 | tf_op jit(solution)/shard_map/ppermute | solution.py:377
  58.0 13.2 %collective-permute-start.4 = (bf16[64,4096]{1,0:T(8,128)(2,1)}, bf16[64,4096]{1,0:T(8,128)(2,1)}, u32[]{:S(2)}, u32[]{:S(2)}) collective-permute-start(bf16[64,4096]{1,0:T(8,128)(2,1)} %collective-permute-done.3.refs_2_.refs_4_), channel_id=1, source_target_pairs={{0,3},{1,2},{2,1},{3,0},{4,7},{5,6},{6,5},{7,4},{8,11},{9,10},{10,... | collective-permute-start | bytes 1572872 | tf_op jit(solution)/shard_map/ppermute | solution.py:377
  73.0 8.0 %collective-permute-start.7 = (bf16[512,256]{1,0:T(8,128)(2,1)S(1)}, bf16[512,256]{1,0:T(8,128)(2,1)}, u32[]{:S(2)}, u32[]{:S(2)}) collective-permute-start(bf16[512,256]{1,0:T(8,128)(2,1)S(1)} %get-tuple-element.32), channel_id=1, source_target_pairs={{0,8},{8,0},{1,9},{9,1},{2,10},{10,2},{3,11},{11,3},{4,12},{12,4},... | collective-permute-start | bytes 786440 | tf_op jit(solution)/shard_map/ppermute | solution.py:389
  76.0 13.4 %collective-permute-start.8 = (bf16[64,4096]{1,0:T(8,128)(2,1)}, bf16[64,4096]{1,0:T(8,128)(2,1)}, u32[]{:S(2)}, u32[]{:S(2)}) collective-permute-start(bf16[64,4096]{1,0:T(8,128)(2,1)} %get-tuple-element.36.refs_7_), channel_id=1, source_target_pairs={{0,1},{1,0},{2,3},{3,2},{4,5},{5,4},{6,7},{7,6},{8,9},{9,8},{10,11... | collective-permute-start | bytes 1572872 | tf_op jit(solution)/shard_map/ppermute | solution.py:377
  85.1 14.9 %collective-permute-start.10 = (bf16[64,4096]{1,0:T(8,128)(2,1)}, bf16[64,4096]{1,0:T(8,128)(2,1)S(1)}, u32[]{:S(2)}, u32[]{:S(2)}) collective-permute-start(bf16[64,4096]{1,0:T(8,128)(2,1)} %get-tuple-element.38), channel_id=1, source_target_pairs={{0,3},{1,2},{2,1},{3,0},{4,7},{5,6},{6,5},{7,4},{8,11},{9,10},{10,... | collective-permute-start | bytes 1572872 | tf_op jit(solution)/shard_map/ppermute | solution.py:377
  86.5 14.6 %collective-permute-start.11 = (bf16[64,4096]{1,0:T(8,128)(2,1)}, bf16[64,4096]{1,0:T(8,128)(2,1)S(1)}, u32[]{:S(2)}, u32[]{:S(2)}) collective-permute-start(bf16[64,4096]{1,0:T(8,128)(2,1)} %get-tuple-element.41), channel_id=1, source_target_pairs={{0,4},{1,5},{2,6},{3,7},{4,0},{5,1},{6,2},{7,3},{8,12},{9,13},{10,... | collective-permute-start | bytes 1572872 | tf_op jit(solution)/shard_map/ppermute | solution.py:377
  87.1 14.0 %collective-permute-start.12 = (bf16[64,4096]{1,0:T(8,128)(2,1)}, bf16[64,4096]{1,0:T(8,128)(2,1)S(1)}, u32[]{:S(2)}, u32[]{:S(2)}) collective-permute-start(bf16[64,4096]{1,0:T(8,128)(2,1)} %get-tuple-element.42), channel_id=1, source_target_pairs={{0,1},{1,0},{2,3},{3,2},{4,5},{5,4},{6,7},{7,6},{8,9},{9,8},{10,11... | collective-permute-start | bytes 1572872 | tf_op jit(solution)/shard_map/ppermute | solution.py:377
  94.1 5.9 %copy-start.19 = (bf16[64,4096]{1,0:T(8,128)(2,1)S(1)}, bf16[64,4096]{1,0:T(8,128)(2,1)}, u32[]{:S(2)}) copy-start(bf16[64,4096]{1,0:T(8,128)(2,1)} %get-tuple-element.37) | copy-start | bytes 1572868
  97.2 3.9 %copy-start.20 = (bf16[64,4096]{1,0:T(8,128)(2,1)S(1)}, bf16[64,4096]{1,0:T(8,128)(2,1)}, u32[]{:S(2)}) copy-start(bf16[64,4096]{1,0:T(8,128)(2,1)} %get-tuple-element.40) | copy-start | bytes 1572868
  97.2 10.8 %collective-permute-start.9 = (bf16[512,256]{1,0:T(8,128)(2,1)S(1)}, bf16[512,256]{1,0:T(8,128)(2,1)S(1)}, u32[]{:S(2)}, u32[]{:S(2)}) collective-permute-start(bf16[512,256]{1,0:T(8,128)(2,1)S(1)} %grad_attended.1.refs_8_.g_own), channel_id=1, source_target_pairs={{0,8},{8,0},{1,9},{9,1},{2,10},{10,2},{3,11},{11,3},{4,12},{12,4},... | collective-permute-start | bytes 786440 | tf_op jit(solution)/shard_map/ppermute | solution.py:389
  100.1 14.9 %collective-permute-start.13 = (bf16[64,4096]{1,0:T(8,128)(2,1)S(1)}, bf16[64,4096]{1,0:T(8,128)(2,1)S(1)}, u32[]{:S(2)}, u32[]{:S(2)}) collective-permute-start(bf16[64,4096]{1,0:T(8,128)(2,1)S(1)} %add_convert_fusion.2.refs_9_), channel_id=1, source_target_pairs={{0,4},{1,5},{2,6},{3,7},{4,0},{5,1},{6,2},{7,3},{8,12},{9,13},{10,... | collective-permute-start | bytes 1572872 | tf_op jit(solution)/shard_map/ppermute | solution.py:377
  101.3 13.9 %collective-permute-start.14 = (bf16[64,4096]{1,0:T(8,128)(2,1)S(1)}, bf16[64,4096]{1,0:T(8,128)(2,1)S(1)}, u32[]{:S(2)}, u32[]{:S(2)}) collective-permute-start(bf16[64,4096]{1,0:T(8,128)(2,1)S(1)} %add_convert_fusion.1.refs_1_), channel_id=1, source_target_pairs={{0,3},{1,2},{2,1},{3,0},{4,7},{5,6},{6,5},{7,4},{8,11},{9,10},{10,... | collective-permute-start | bytes 1572872 | tf_op jit(solution)/shard_map/ppermute | solution.py:377
  102.1 5.9 %copy-start = (bf16[3,1024,256]{2,1,0:T(8,128)(2,1)S(1)}, bf16[3,1024,256]{2,1,0:T(8,128)(2,1)}, u32[]{:S(2)}) copy-start(bf16[3,1024,256]{2,1,0:T(8,128)(2,1)} %get-tuple-element.34.cat) | copy-start | bytes 4718596
  102.1 5.9 %copy-start.11 = (bf16[1024,1024]{1,0:T(8,128)(2,1)S(1)}, bf16[1024,1024]{1,0:T(8,128)(2,1)}, u32[]{:S(2)}) copy-start(bf16[1024,1024]{1,0:T(8,128)(2,1)} %get-tuple-element.35.probs_t) | copy-start | bytes 6291460
  106.5 18.6 %collective-permute-start.17 = (bf16[4,256,512]{2,1,0:T(8,128)(2,1)S(1)}, bf16[4,256,512]{2,1,0:T(8,128)(2,1)S(1)}, u32[]{:S(2)}, u32[]{:S(2)}) collective-permute-start(bf16[4,256,512]{2,1,0:T(8,128)(2,1)S(1)} %get-tuple-element.47), channel_id=1, source_target_pairs={{0,16},{16,0},{32,48},{48,32},{64,80},{80,64},{96,112},{112,96},{1... | collective-permute-start | bytes 3145736 | tf_op jit(solution)/shard_map/ppermute | solution.py:377
  108.0 7.0 %copy-start.18 = (bf16[64,4096]{1,0:T(8,128)(2,1)S(1)}, bf16[64,4096]{1,0:T(8,128)(2,1)}, u32[]{:S(2)}) copy-start(bf16[64,4096]{1,0:T(8,128)(2,1)} %get-tuple-element.44) | copy-start | bytes 1572868
  115.9 12.9 %collective-permute-start.15 = (bf16[64,4096]{1,0:T(8,128)(2,1)S(1)}, bf16[64,4096]{1,0:T(8,128)(2,1)S(1)}, u32[]{:S(2)}, u32[]{:S(2)}) collective-permute-start(bf16[64,4096]{1,0:T(8,128)(2,1)S(1)} %get-tuple-element.45), channel_id=1, source_target_pairs={{0,1},{1,0},{2,3},{3,2},{4,5},{5,4},{6,7},{7,6},{8,9},{9,8},{10,11... | collective-permute-start | bytes 1572872 | tf_op jit(solution)/shard_map/ppermute | solution.py:377
  117.7 11.8 %collective-permute-start.16 = (bf16[64,4096]{1,0:T(8,128)(2,1)S(1)}, bf16[64,4096]{1,0:T(8,128)(2,1)S(1)}, u32[]{:S(2)}, u32[]{:S(2)}) collective-permute-start(bf16[64,4096]{1,0:T(8,128)(2,1)S(1)} %get-tuple-element.46), channel_id=1, source_target_pairs={{0,4},{1,5},{2,6},{3,7},{4,0},{5,1},{6,2},{7,3},{8,12},{9,13},{10,... | collective-permute-start | bytes 1572872 | tf_op jit(solution)/shard_map/ppermute | solution.py:377
  125.0 4.4 %copy-start.9 = (bf16[64,4096]{1,0:T(8,128)(2,1)S(1)}, bf16[64,4096]{1,0:T(8,128)(2,1)}, u32[]{:S(2)}) copy-start(bf16[64,4096]{1,0:T(8,128)(2,1)} %get-tuple-element.33.refs_9_.p0) | copy-start | bytes 1572868
  129.9 26.6 %collective-permute-start.18 = (bf16[64,4096]{1,0:T(8,128)(2,1)S(1)}, bf16[64,4096]{1,0:T(8,128)(2,1)S(1)}, u32[]{:S(2)}, u32[]{:S(2)}) collective-permute-start(bf16[64,4096]{1,0:T(8,128)(2,1)S(1)} %mix_sum.1.own), channel_id=1, source_target_pairs={{0,15},{1,14},{2,13},{3,12},{4,11},{5,10},{6,9},{7,8},{8,7},{9,6},... | collective-permute-start | bytes 1572872 | tf_op jit(solution)/shard_map/ppermute | solution.py:385
  134.1 32.4 %all-to-all-start.1 = ((bf16[8,3,128,256]{3,2,1,0:T(8,128)(2,1)}), bf16[8,3,128,256]{3,2,1,0:T(8,128)(2,1)S(1)}, u32[]{:S(2)}, u32[]{:S(2)}) async-start(bf16[8,3,128,256]{3,2,1,0:T(8,128)(2,1)} %attention_bwd.3.refs_0_), calls=%async_computation.1 | async-start | bytes 3145728 | tf_op jit(solution)/shard_map/all_to_all | solution.py:381
  138.5 9.5 %collective-permute-start.19 = (bf16[256,512]{1,0:T(8,128)(2,1)}, bf16[256,512]{1,0:T(8,128)(2,1)S(1)}, u32[]{:S(2)}, u32[]{:S(2)}) collective-permute-start(bf16[256,512]{1,0:T(8,128)(2,1)} %get-tuple-element.51), channel_id=1, source_target_pairs={{0,32},{16,48},{32,0},{48,16},{64,96},{80,112},{96,64},{112,80},{1... | collective-permute-start | bytes 786440 | tf_op jit(solution)/shard_map/ppermute | solution.py:377
  139.9 14.0 %collective-permute-start.20 = (bf16[256,512]{1,0:T(8,128)(2,1)}, bf16[256,512]{1,0:T(8,128)(2,1)S(1)}, u32[]{:S(2)}, u32[]{:S(2)}) collective-permute-start(bf16[256,512]{1,0:T(8,128)(2,1)} %get-tuple-element.52), channel_id=1, source_target_pairs={{0,64},{16,80},{32,96},{48,112},{64,0},{80,16},{96,32},{112,48},{1... | collective-permute-start | bytes 786440 | tf_op jit(solution)/shard_map/ppermute | solution.py:377
  142.7 13.8 %collective-permute-start.21 = (bf16[256,512]{1,0:T(8,128)(2,1)}, bf16[256,512]{1,0:T(8,128)(2,1)S(1)}, u32[]{:S(2)}, u32[]{:S(2)}) collective-permute-start(bf16[256,512]{1,0:T(8,128)(2,1)} %copy-done.17), channel_id=1, source_target_pairs={{0,96},{16,112},{32,64},{48,80},{64,32},{80,48},{96,0},{112,16},{1... | collective-permute-start | bytes 786440 | tf_op jit(solution)/shard_map/ppermute | solution.py:377
  157.6 8.1 %collective-permute-start.22 = (bf16[256,256]{1,0:T(8,128)(2,1)S(1)}, bf16[256,256]{1,0:T(8,128)(2,1)S(1)}, u32[]{:S(2)}, u32[]{:S(2)}) collective-permute-start(bf16[256,256]{1,0:T(8,128)(2,1)S(1)} %select_convert_fusion), channel_id=1, source_target_pairs={{0,8},{8,0},{1,9},{9,1},{2,10},{10,2},{3,11},{11,3},{4,12},{12,4},... | collective-permute-start | bytes 393224 | tf_op jit(solution)/shard_map/ppermute | solution.py:389
  (14 other events, 24.1 us)
